TPU v7x, 128 devices: a whole 4x4x4 slice. The times are simulated.
128 devices in a mesh: aud: 8 (over z, core), vid: 16 (over y, x).
Axes of the slice: x: 4, y: 4, z: 4, core: 2. Of those that a mesh axis runs over, the one named last changes fastest.
Arguments:
- audio: float32 [16384, 1024], P('aud', 'vid'), may hold values from -8 to 8
- video: float32 [16384, 1024], P('vid', 'aud'), may hold values from -8 to 8
- scale: float32 [], replicated, may hold values from 6 to 12
- bias: float32 [], replicated, may hold values from -7 to -5
Outputs:
- row_loss: float32 [16384], P('aud')
- grad_audio: float32 [16384, 1024], P('aud', 'vid')
- grad_video: float32 [16384, 1024], P('vid', 'aud')
All inputs are finite; a program needn't handle non-finite values.
Results may differ from a plain program's by a relative error of at most 0.0003.
Values sent between devices are 32-bit elements; how exact they have to be, the bound alone decides.
No kernel may reach another device: no remote copies, remote signals or barrier semaphores. Data moves between devices by JAX's collectives and lax.ppermute only.
A program may use at most 128 MiB of HBM per device.

v0:
```python
import jax
import jax.numpy as jnp
from jax import lax
from jax.experimental import pallas as pl
from jax.experimental.pallas import tpu as pltpu
from jax.sharding import Mesh, PartitionSpec as P

F32 = jnp.float32
BF16 = jnp.bfloat16
F8 = jnp.float8_e4m3fn
UP_VALUE = 2.0**8
UP_REST = 2.0**17
DOWN = 2.0**-25
EPS = 1e-06
CHUNKS = (1024, 1024)
BLOCK = 512
SUBS = 2
VMEM = 56 * 2**20
PLANE = ("core", "y", "x")
MIB = 2**20
ROWS = [[4 * i + j for j in range(4)] for i in range(4)]
COLUMNS = [[16 + 4 * j + i for j in range(4)] for i in range(4)]
INNER = ROWS + COLUMNS


def dot(a, b, dims):
    return lax.dot_general(a, b, (dims, ((), ())), preferred_element_type=F32)


def split(x, axis, value_first):
    high = x.astype(BF16)
    rest = ((x - high.astype(F32)) * UP_REST).astype(F8)
    value = (x * UP_VALUE).astype(F8)
    pair = (value, rest) if value_first else (rest, value)
    return high, jnp.concatenate(pair, axis=axis)


def product(a, b, dims):
    return dot(a[0], b[0], dims) + DOWN * dot(a[1], b[1], dims)


def prepare_kernel(place, whole, inv_ref, unit_t_out, v_high_out, v_small_out, t_high_out, t_small_out, *scratch):
    flipped, unit_t_ref, v_high, v_small, t_high, t_small, sems = scratch
    core, y, x = place[0], place[1], place[2]
    n = whole.shape[0]
    outs = (unit_t_out, t_high_out, t_small_out, v_high_out, v_small_out)
    copies = [
        pltpu.make_async_copy(ref, out, sems.at[k])
        for k, (ref, out) in enumerate(zip((unit_t_ref, t_high, t_small, v_high, v_small), outs))
    ]
    v_t = whole[...].T
    inv = lax.rsqrt(jnp.sum(v_t * v_t, axis=0, keepdims=True) + EPS)
    inv_ref[...] = inv
    flipped[...] = (v_t * inv).reshape(16, 64, n)
    for outer in range(4):
        for inner in range(4):
            row = lax.rem(y + 4 - jnp.where(core == 0, outer, inner), 4)
            column = lax.rem(x + 4 - jnp.where(core == 0, inner, outer), 4)
            at = 64 * (4 * outer + inner)
            unit_t_ref[at : at + 64, :] = flipped[4 * row + column]
    copies[0].start()
    unit_t = unit_t_ref[...]
    t_high[...], t_small[...] = split(unit_t, 1, True)
    copies[1].start()
    copies[2].start()
    v_high[...], v_small[...] = split(unit_t.T, 1, True)
    copies[3].start()
    copies[4].start()
    for copy in copies:
        copy.wait()


def prepare(video, place):
    n = video.shape[0]
    whole = pl.BlockSpec(memory_space=pltpu.VMEM)
    shape = jax.ShapeDtypeStruct
    parts = [
        shape((1024, n), F32),
        shape((n, 1024), BF16),
        shape((n, 2048), F8),
        shape((1024, n), BF16),
        shape((1024, 2 * n), F8),
    ]
    return pl.pallas_call(
        prepare_kernel,
        in_specs=[pl.BlockSpec(memory_space=pltpu.SMEM), whole],
        out_specs=[whole] + [pl.BlockSpec(memory_space=pl.ANY)] * 5,
        out_shape=[shape((1, n), F32)] + parts,
        scratch_shapes=[pltpu.VMEM((16, 64, n), F32)]
        + [pltpu.VMEM(p.shape, p.dtype) for p in parts]
        + [pltpu.SemaphoreType.DMA((5,))],
        compiler_params=pltpu.CompilerParams(vmem_limit_bytes=VMEM),
        cost_estimate=pl.CostEstimate(flops=0, bytes_accessed=16 * MIB, transcendentals=0),
        name="video_parts",
    )(place, video)


def inverse(d):
    r = pl.reciprocal(d, approx=True)
    return r * (2.0 - d * r)


def soft(power):
    return jnp.where(power < 1e-3, power - 0.5 * power * power, jnp.log(1.0 + power))


def pairs_kernel(first, last, count, skipped, refs):
    place, scalars, *refs = refs
    audio, refs = refs[:count], refs[count + skipped :]
    unit_t_hbm, *sources = refs[:5]
    sources.append(unit_t_hbm)
    refs = refs[5:]
    before = None
    if not first:
        before, *refs = refs
    grads_a, inv_ref, refs = refs[:4], refs[4], refs[5:]
    if last:
        whole, *refs = refs
    state, near, v_high, v_small, t_high, t_small, sems = refs
    step = pl.program_id(0)
    scale, bias = scalars[0], scalars[1]
    n = v_high.shape[0]
    block = inv_ref.shape[1]
    sub = block // SUBS
    offset = place[3] + step * block
    loads = [
        pltpu.make_async_copy(source, to, sems.at[k])
        for k, (source, to) in enumerate(zip(sources, (v_high, v_small, t_high, t_small, near)))
    ]
    if not first:
        loads.append(pltpu.make_async_copy(before, state, sems.at[5]))

    @pl.when(step == 0)
    def _():
        for load in loads:
            load.start()
        if first:
            state[...] = jnp.zeros_like(state)

    audio_t = jnp.concatenate([r[...] for r in audio], axis=0)
    inv = lax.rsqrt(jnp.sum(audio_t * audio_t, axis=0, keepdims=True) + EPS)
    inv_ref[...] = inv
    unit_t = audio_t * inv

    @pl.when(step == 0)
    def _():
        for load in loads[:2]:
            load.wait()

    def similar(k):
        part = split(unit_t[:, k * sub : (k + 1) * sub], 0, False)
        return scale * product((v_high[...], v_small[...]), part, ((1,), (0,)))

    def judge(k, scaled):
        power = jnp.exp(scaled + bias)
        sig = power * inverse(1.0 + power)
        paired = (
            lax.broadcasted_iota(jnp.int32, (n, sub), 0)
            - lax.broadcasted_iota(jnp.int32, (n, sub), 1)
        ) == offset + k * sub
        loss = jnp.sum(soft(power), axis=0, keepdims=True)
        return paired, split(jnp.where(paired, 0.0, sig), 0, False), loss

    def pull_rows(k, away, loss):
        lanes = slice(k * sub, (k + 1) * sub)
        grad_a = product((t_high[...], t_small[...]), away, ((1,), (0,)))
        inner = jnp.sum(grad_a * unit_t[:, lanes], axis=0, keepdims=True)
        for p, ref in enumerate(grads_a):
            ref[0:256, lanes] = grad_a[256 * p : 256 * p + 256, :]
            ref[256:257, lanes] = loss
            ref[257:258, lanes] = inner
            ref[258:264, lanes] = jnp.zeros((6, sub), F32)

    scores = [similar(k) for k in range(SUBS)]
    judged = [judge(0, scores[0])]

    @pl.when(step == 0)
    def _():
        for load in loads[2:]:
            load.wait()

    for k in range(SUBS):
        if k > 0:
            judged.append(judge(k, scores[k]))
        pull_rows(k, judged[k][1], judged[k][2])
    high = jnp.concatenate([j[1][0] for j in judged], axis=1)
    small = jnp.concatenate([j[1][1][:n] for j in judged] + [j[1][1][n:] for j in judged], axis=1)
    state[...] += product(split(unit_t, 1, True), (high, small), ((1,), (1,)))

    @pl.when((offset >= 0) & (offset < n))
    def _():
        at = pl.multiple_of(offset, block)
        own = jnp.concatenate(
            [jnp.sum(jnp.where(j[0], s, 0.0), axis=0, keepdims=True) for j, s in zip(judged, scores)],
            axis=1,
        )
        value = own + bias
        diag = -1.0 / (1.0 + jnp.exp(value))
        pull = near[:, pl.ds(at, block)] * diag
        inner_own = jnp.sum(pull * unit_t, axis=0, keepdims=True)
        for k, ref in enumerate(grads_a):
            ref[0:256, :] += pull[256 * k : 256 * k + 256, :]
            ref[256:257, :] += -value
            ref[257:258, :] += inner_own
        state[:, pl.ds(at, block)] += unit_t * diag

    if last:

        @pl.when(step == pl.num_programs(0) - 1)
        def _():
            core, y, x = place[0], place[1], place[2]
            for half in range(n // block):
                lanes = pl.ds(half * block, block)
                row = jnp.sum(near[:, lanes] * state[:, lanes], axis=0, keepdims=True)
                for owner in range(8):
                    whole[owner, 128:129, lanes] = row
            for owner in range(8):
                whole[owner, 129:136, :] = jnp.zeros((7, n), F32)
                for part in range(2):
                    dy = lax.rem(y + 4 - owner // 2, 4)
                    dx = lax.rem(x + 4 - 2 * (owner % 2) - part, 4)
                    at = jnp.where(core == 0, 4 * dy + dx, 4 * dx + dy) * 64
                    rows = pl.ds(pl.multiple_of(at, 64), 64)
                    whole[owner, 64 * part : 64 * part + 64, :] = state[rows, :]


def pairs(audio, ahead, video, place, scalars, before, last):
    rows = audio[0].shape[1]
    first = before is None
    n = video[1].shape[0]
    smem = pl.BlockSpec(memory_space=pltpu.SMEM)
    still = lambda shape: pl.BlockSpec(shape, lambda i: (0, 0), pipeline_mode=pl.Buffered(1))
    moving = lambda height: pl.BlockSpec((height, BLOCK), lambda i: (0, i))
    shape = jax.ShapeDtypeStruct
    anywhere = pl.BlockSpec(memory_space=pl.ANY)
    in_specs = [smem, smem] + [moving(a.shape[0]) for a in audio] + [anywhere] * (len(ahead) + 5)
    operands = [place, scalars, *audio, *ahead, *video]
    out_specs = [moving(264)] * 4 + [moving(1)]
    out_shape = [shape((264, rows), F32)] * 4 + [shape((1, rows), F32)]
    scratch = [pltpu.VMEM((1024, n), F32)] + [pltpu.VMEM(v.shape, v.dtype) for v in video[1:]]
    scratch.append(pltpu.SemaphoreType.DMA((6,)))
    if not first:
        in_specs.append(anywhere)
        operands.append(before)
    if last:
        out_specs.append(pl.BlockSpec((8, 136, n), lambda i: (0, 0, 0), pipeline_mode=pl.Buffered(1)))
        out_shape.append(shape((8, 136, n), F32))
        scratch = [pltpu.VMEM((1024, n), F32)] + scratch
    else:
        out_specs.append(still((1024, n)))
        out_shape.append(shape((1024, n), F32))

    def body(*refs):
        pairs_kernel(first, last, len(audio), len(ahead), refs)

    return pl.pallas_call(
        body,
        grid=(rows // BLOCK,),
        in_specs=in_specs,
        out_specs=out_specs,
        out_shape=out_shape,
        scratch_shapes=scratch,
        compiler_params=pltpu.CompilerParams(vmem_limit_bytes=VMEM),
        cost_estimate=pl.CostEstimate(
            flops=6 * 2 * rows * n * 1024, bytes_accessed=24 * MIB, transcendentals=3 * rows * n
        ),
        name="pairs_last" if last else "pairs_first" if first else "pairs_next",
    )(*operands)


def perm(inner, k):
    pairs_of = []
    for core in range(2):
        for y in range(4):
            for x in range(4):
                along_x = (core == 0) == inner
                to = (core, y, (x + k) % 4) if along_x else (core, (y + k) % 4, x)
                pairs_of.append((16 * core + 4 * y + x, 16 * to[0] + 4 * to[1] + to[2]))
    return pairs_of


def move(block, inner, k):
    return lax.ppermute(block, PLANE, perm(inner, k))


def after(arrays, late):
    spec = pl.BlockSpec(memory_space=pl.ANY)
    return pl.pallas_call(
        lambda *refs: None,
        in_specs=[spec] * (len(arrays) + len(late)),
        out_specs=[spec] * len(late),
        out_shape=[jax.ShapeDtypeStruct(a.shape, a.dtype) for a in late],
        input_output_aliases={len(arrays) + i: i for i in range(len(late))},
        name="after",
    )(*arrays, *late)


def local(audio, video, scale, bias):
    z, core, y, x = (lax.axis_index(a) for a in ("z", "core", "y", "x"))
    n = video.shape[0]
    audio_t = audio.T
    rows = audio_t.shape[1]
    scalars = jnp.stack([scale, bias])
    base = (2 * z + core) * rows - (4 * y + x) * n

    whole_video = lax.all_gather(video, ("z", "core"), axis=1, tiled=True)
    row = [audio_t] + [move(audio_t, True, k) for k in (1, 2, 3)]
    gathered, early, starts, start = [], [], [], 0
    for part in CHUNKS:
        block = jnp.concatenate([r[:, start : start + part] for r in row], axis=0)
        if start > 0:
            (block,) = after([below[:8] + above[:8]], [block])
        below, above = move(block, False, 1), move(block, False, 3)
        if start + part < rows:
            far = [move(below[:128], False, 1), move(above[128:], False, 3)]
        else:
            far = [move(block, False, 2)]
        gathered.append([block, below, *far, above])
        early.append([below, above] if start + part < rows else [block])
        starts.append(start)
        start += part
    place = jnp.stack([core, y, x]).astype(jnp.int32)
    inv_v, *parts = prepare(whole_video, place)
    state = None
    invs, halves = [], []
    for c, blocks in enumerate(gathered):
        at = jnp.stack([core, y, x, base + starts[c]]).astype(jnp.int32)
        last = c == len(CHUNKS) - 1
        ahead = early[c + 1] if c + 1 < len(CHUNKS) else []
        outs = pairs(blocks, ahead, parts, at, scalars, state, last)
        grads, inv, state = outs[:4], outs[4], outs[5]
        invs.append(inv)
        if c > 0:
            seen = came[0][256:264] + came[1][256:264] + came[2][256:264]
            *others, state = after([seen], [*grads[1:], state])
            grads = [grads[0], *others]
            halves.append(kept + came[0] + came[1] + came[2])
        kept = grads[0]
        came = [move(grads[k], False, 4 - k) for k in (1, 2, 3)]
    halves.append(kept + came[0] + came[1] + came[2])

    total_v = lax.psum_scatter(state.reshape(1088, n), ("z", "core"), scatter_dimension=0, tiled=True)
    place_in = jnp.where(core == 0, x, y)
    done = []
    for c, h in enumerate(halves):
        to = [jnp.concatenate([h[64 * k : 64 * k + 64], h[256:264]], axis=0) for k in range(4)]
        if c < len(CHUNKS) - 1:
            ring = jnp.stack([to[0], to[3], to[2], to[1], to[0], to[3], to[2]])
            ring = lax.dynamic_slice_in_dim(ring, lax.rem(4 - place_in, 4), 4, 0)
            done.append(jnp.sum(lax.all_to_all(ring, PLANE, 0, 0, axis_index_groups=INNER), axis=0))
        else:
            done.append(to[0] + sum(move(to[k], True, 4 - k) for k in (1, 2, 3)))
    total_a = jnp.concatenate(done, axis=1)
    inv_a = jnp.concatenate(invs, axis=1)
    row_loss, inner_a = total_a[64], total_a[65:66]
    grad_a = scale * (total_a[0:64] * inv_a - audio_t * (inv_a * inv_a * inner_a))
    grad_v = scale * (total_v[0:128] * inv_v - video.T * (inv_v * inv_v * total_v[128:129]))
    return row_loss, grad_a.T, grad_v.T


def solution(mesh):
    fine = Mesh(mesh.devices.reshape(4, 2, 4, 4), ("z", "core", "y", "x"))
    aud, vid = ("z", "core"), ("y", "x")
    return jax.shard_map(
        local,
        mesh=fine,
        in_specs=(P(aud, vid), P(vid, aud), P(), P()),
        out_specs=(P(aud), P(aud, vid), P(vid, aud)),
        check_vma=False,
    )
```

profile of v0, /device:TPU:0, one launch (start us, length us, event | category | flops | bytes accessed | tf_op | source)
XLA Modules:
  0.0 187.3 jit_solution(518533891090614144)
XLA Ops:
  7.9 1.6 collective-permute-start
  9.6 2.7 %collective-permute-start.1 = (f32[64,2048]{1,0:T(8,128)}, f32[64,2048]{1,0:T(8,128)S(1)}, u32[]{:S(2)}, u32[]{:S(2)}) collective-permute-start(f32[64,2048]{1,0:T(8,128)} %bitcast.47), channel_id=1, source_target_pairs={{0,2},{1,3},{2,0},{3,1},{4,6},{5,7},{6,4},{7,5},{8,10},{9,11},{10,... | collective-permute-start | bytes 1572872 | tf_op jit(solution)/shard_map/ppermute | solution.py:283
  14.8 3.8 %collective-permute-done = f32[64,2048]{1,0:T(8,128)S(1)} collective-permute-done((f32[64,2048]{1,0:T(8,128)}, f32[64,2048]{1,0:T(8,128)S(1)}, u32[]{:S(2)}, u32[]{:S(2)}) %collective-permute-start) | collective-permute-done | bytes 524320 | tf_op jit(solution)/shard_map/ppermute | solution.py:283
  18.7 6.6 %collective-permute-done.1 = f32[64,2048]{1,0:T(8,128)S(1)} collective-permute-done((f32[64,2048]{1,0:T(8,128)}, f32[64,2048]{1,0:T(8,128)S(1)}, u32[]{:S(2)}, u32[]{:S(2)}) %collective-permute-start.1) | collective-permute-done | bytes 524320 | tf_op jit(solution)/shard_map/ppermute | solution.py:283
  25.5 1.6 collective-permute-start.3
  27.1 1.7 collective-permute-start.5
  30.0 11.7 %collective-permute-done.3.refs_3_ = f32[256,1024]{1,0:T(8,128)} collective-permute-done((f32[256,1024]{1,0:T(8,128)S(1)}, f32[256,1024]{1,0:T(8,128)}, u32[]{:S(2)}, u32[]{:S(2)}) %collective-permute-start.3) | collective-permute-done | bytes 1048608 | tf_op jit(solution)/shard_map/ppermute | solution.py:283
  44.3 2.9 %collective-permute-start.6 = (f32[128,1024]{1,0:T(8,128)S(1)}, f32[128,1024]{1,0:T(8,128)}, u32[]{:S(2)}, u32[]{:S(2)}) collective-permute-start(f32[128,1024]{1,0:T(8,128)S(1)} %slice.127), channel_id=1, source_target_pairs={{0,12},{1,13},{2,14},{3,15},{4,0},{5,1},{6,2},{7,3},{8,4},{9,5},{1... | collective-permute-start | bytes 1572872 | tf_op jit(solution)/shard_map/ppermute | solution.py:283
  52.2 2.1 %collective-permute-start.11 = (f32[256,1024]{1,0:T(8,128)}, f32[256,1024]{1,0:T(8,128)}, u32[]{:S(2)}, u32[]{:S(2)}) collective-permute-start(f32[256,1024]{1,0:T(8,128)} %after.2.refs_7_.refs_2_), channel_id=1, source_target_pairs={{0,8},{1,9},{2,10},{3,11},{4,12},{5,13},{6,14},{7,15},{8,0},{9,1},... | collective-permute-start | bytes 3145736 | tf_op jit(solution)/shard_map/ppermute | solution.py:283
  55.6 10.6 %video_parts.1 = (f32[1,1024]{1,0:T(1,128)}, f32[1024,1024]{1,0:T(8,128)}, bf16[1024,1024]{1,0:T(8,128)(2,1)}, f8e4m3fn[1024,2048]{1,0:T(32,128)(4,1)}, bf16[102...) custom-call(s32[3]{0:T(128)} %pad_add_fusion.2.place, f32[1024,1024]{1,0:T(8,128)} %all-gather.2.cloned.1.call-done.whole), custom_call_target="tpu_custom_call" | custom-call | bytes 16777216 | tf_op jit(solution)/shard_map/video_parts/pallas_call | solution.py:84
  66.2 26.1 %pairs_first.1 = (f32[264,1024]{1,0:T(8,128)}, f32[264,1024]{1,0:T(8,128)}, f32[264,1024]{1,0:T(8,128)}, f32[264,1024]{1,0:T(8,128)}, f32[1,1024]{1,0:T(1,128)}, /*index=5*/f32[1024,1024]{1,0:T(8,128)}) custom-call(s32[4]{0:T(128)} %pad_add_fusion.refs_0_, f32[2]{0:T(128)} %pad_maximum_fusion.10.refs_1_, f32[256,1024]{1,0:T(8,128)} %copy-done.3, ...), custom_call_target="tpu_custom_call" | custom-call | flops 12884901888 | bytes 25165824 | tf_op jit(solution)/shard_map/pairs_first/pallas_call | solution.py:256
  94.5 24.9 %pairs_last.1 = (f32[264,1024]{1,0:T(8,128)}, f32[264,1024]{1,0:T(8,128)}, f32[264,1024]{1,0:T(8,128)}, f32[264,1024]{1,0:T(8,128)}, f32[1,1024]{1,0:T(1,128)}, /*index=5*/f32[8,136,1024]{2,1,0:T(8,128)}) custom-call(s32[4]{0:T(128)} %get-tuple-element.50.refs_0_, f32[2]{0:T(128)} %pad_maximum_fusion.10.refs_1_, f32[256,1024]{1,0:T(8,128)} %after.2.refs_7_.refs_2_, ...), custom_call_target="tpu_custom_call" | custom-call | flops 12884901888 | bytes 25165824 | tf_op jit(solution)/shard_map/pairs_last/pallas_call | solution.py:256
  121.6 1.7 add_add_fusion.1
  124.5 1.5 collective-permute-start.14
  128.8 3.9 %all-to-all-start = ((f32[4,72,1024]{2,1,0:T(8,128)}), f32[4,72,1024]{2,1,0:T(8,128)S(1)}, u32[]{:S(2)}, u32[]{:S(2)}) async-start(f32[4,72,1024]{2,1,0:T(8,128)} %constant_dynamic-slice_fusion), calls=%async_computation | async-start | bytes 2359296 | tf_op jit(solution)/shard_map/all_to_all | solution.py:350
  132.8 12.0 %collective-permute-done.13 = f32[264,1024]{1,0:T(8,128)S(1)} collective-permute-done((f32[264,1024]{1,0:T(8,128)}, f32[264,1024]{1,0:T(8,128)S(1)}, u32[]{:S(2)}, u32[]{:S(2)}) %collective-permute-start.13) | collective-permute-done | bytes 1081376 | tf_op jit(solution)/shard_map/ppermute | solution.py:283
  144.8 3.1 %collective-permute-done.14 = f32[264,1024]{1,0:T(8,128)} collective-permute-done((f32[264,1024]{1,0:T(8,128)}, f32[264,1024]{1,0:T(8,128)}, u32[]{:S(2)}, u32[]{:S(2)}) %collective-permute-start.14) | collective-permute-done | bytes 1081376 | tf_op jit(solution)/shard_map/ppermute | solution.py:283
  147.9 11.5 %collective-permute-done.15 = f32[264,1024]{1,0:T(8,128)} collective-permute-done((f32[264,1024]{1,0:T(8,128)}, f32[264,1024]{1,0:T(8,128)}, u32[]{:S(2)}, u32[]{:S(2)}) %collective-permute-start.15) | collective-permute-done | bytes 1081376 | tf_op jit(solution)/shard_map/ppermute | solution.py:283
  159.4 2.0 %add_add_fusion = f32[264,1024]{1,0:T(8,128)S(1)} fusion(f32[264,1024]{1,0:T(8,128)} %collective-permute-done.15, f32[264,1024]{1,0:T(8,128)} %collective-permute-done.14, f32[264,1024]{1,0:T(8,128)S(1)} %copy-done.2, f32[264,1024]{1,0:T(8,128)S(1)} %collective-permute-done.13), kind=kLoop, calls=%fused_computation | loop fusion | flops 811008 | bytes 5406720 | tf_op jit(solution)/shard_map/add | solution.py:340
  161.6 1.7 collective-permute-start.16
  163.4 1.6 collective-permute-start.17
  165.6 2.9 %collective-permute-done.16 = f32[72,1024]{1,0:T(8,128)} collective-permute-done((f32[72,1024]{1,0:T(8,128)S(1)}, f32[72,1024]{1,0:T(8,128)}, u32[]{:S(2)}, u32[]{:S(2)}) %collective-permute-start.16) | collective-permute-done | bytes 294944 | tf_op jit(solution)/shard_map/ppermute | solution.py:283
  168.5 3.3 %collective-permute-done.17 = f32[72,1024]{1,0:T(8,128)} collective-permute-done((f32[72,1024]{1,0:T(8,128)S(1)}, f32[72,1024]{1,0:T(8,128)}, u32[]{:S(2)}, u32[]{:S(2)}) %collective-permute-start.17) | collective-permute-done | bytes 294944 | tf_op jit(solution)/shard_map/ppermute | solution.py:283
  171.8 3.1 %collective-permute-done.18 = f32[72,1024]{1,0:T(8,128)} collective-permute-done((f32[72,1024]{1,0:T(8,128)S(1)}, f32[72,1024]{1,0:T(8,128)}, u32[]{:S(2)}, u32[]{:S(2)}) %collective-permute-start.18) | collective-permute-done | bytes 294944 | tf_op jit(solution)/shard_map/ppermute | solution.py:283
  (81 shorter events, 26.9 us)
Async XLA Ops:
  7.2 48.4 %all-gather.2.cloned.1.call-start = ((), (), s32[]{:S(2)}) async-start(), calls=%async_computation.2 | async-start | bytes 4718592 | tf_op jit(solution)/shard_map/all_gather | solution.py:306
  7.9 169.6 %reduce-scatter.2.cloned.1.call-start = ((), (), s32[]{:S(2)}) async-start(), calls=%async_computation.3 | async-start | bytes 5013504 | tf_op jit(solution)/shard_map/reduce_scatter | solution.py:342
  7.9 10.7 %collective-permute-start = (f32[64,2048]{1,0:T(8,128)}, f32[64,2048]{1,0:T(8,128)S(1)}, u32[]{:S(2)}, u32[]{:S(2)}) collective-permute-start(f32[64,2048]{1,0:T(8,128)} %bitcast.46), channel_id=1, source_target_pairs={{0,1},{1,2},{2,3},{3,0},{4,5},{5,6},{6,7},{7,4},{8,9},{9,10},{10,1... | collective-permute-start | bytes 1572872 | tf_op jit(solution)/shard_map/ppermute | solution.py:283
  9.6 15.7 %collective-permute-start.1 = (f32[64,2048]{1,0:T(8,128)}, f32[64,2048]{1,0:T(8,128)S(1)}, u32[]{:S(2)}, u32[]{:S(2)}) collective-permute-start(f32[64,2048]{1,0:T(8,128)} %bitcast.47), channel_id=1, source_target_pairs={{0,2},{1,3},{2,0},{3,1},{4,6},{5,7},{6,4},{7,5},{8,10},{9,11},{10,... | collective-permute-start | bytes 1572872 | tf_op jit(solution)/shard_map/ppermute | solution.py:283
  12.3 13.0 %collective-permute-start.2 = (f32[64,2048]{1,0:T(8,128)}, f32[64,2048]{1,0:T(8,128)S(1)}, u32[]{:S(2)}, u32[]{:S(2)}) collective-permute-start(f32[64,2048]{1,0:T(8,128)} %bitcast.48), channel_id=1, source_target_pairs={{0,3},{1,0},{2,1},{3,2},{4,7},{5,4},{6,5},{7,6},{8,11},{9,8},{10,9... | collective-permute-start | bytes 1572872 | tf_op jit(solution)/shard_map/ppermute | solution.py:283
  25.5 24.3 %copy-start.3 = (f32[256,1024]{1,0:T(8,128)}, f32[256,1024]{1,0:T(8,128)S(1)}, u32[]{:S(2)}) copy-start(f32[256,1024]{1,0:T(8,128)S(1)} %pad_maximum_fusion.refs_2_) | copy-start | bytes 3145732
  25.5 16.2 %collective-permute-start.3 = (f32[256,1024]{1,0:T(8,128)S(1)}, f32[256,1024]{1,0:T(8,128)}, u32[]{:S(2)}, u32[]{:S(2)}) collective-permute-start(f32[256,1024]{1,0:T(8,128)S(1)} %pad_maximum_fusion.refs_2_), channel_id=1, source_target_pairs={{0,4},{1,5},{2,6},{3,7},{4,8},{5,9},{6,10},{7,11},{8,12},{9,13},{1... | collective-permute-start | bytes 3145736 | tf_op jit(solution)/shard_map/ppermute | solution.py:283
  27.1 16.1 %collective-permute-start.5 = (f32[256,1024]{1,0:T(8,128)S(1)}, f32[256,1024]{1,0:T(8,128)}, u32[]{:S(2)}, u32[]{:S(2)}) collective-permute-start(f32[256,1024]{1,0:T(8,128)S(1)} %pad_maximum_fusion.refs_2_), channel_id=1, source_target_pairs={{0,12},{1,13},{2,14},{3,15},{4,0},{5,1},{6,2},{7,3},{8,4},{9,5},{1... | collective-permute-start | bytes 3145736 | tf_op jit(solution)/shard_map/ppermute | solution.py:283
  42.8 23.5 %collective-permute-start.4 = (f32[128,1024]{1,0:T(8,128)S(1)}, f32[128,1024]{1,0:T(8,128)}, u32[]{:S(2)}, u32[]{:S(2)}) collective-permute-start(f32[128,1024]{1,0:T(8,128)S(1)} %slice.126), channel_id=1, source_target_pairs={{0,4},{1,5},{2,6},{3,7},{4,8},{5,9},{6,10},{7,11},{8,12},{9,13},{1... | collective-permute-start | bytes 1572872 | tf_op jit(solution)/shard_map/ppermute | solution.py:283
  44.3 21.9 %collective-permute-start.6 = (f32[128,1024]{1,0:T(8,128)S(1)}, f32[128,1024]{1,0:T(8,128)}, u32[]{:S(2)}, u32[]{:S(2)}) collective-permute-start(f32[128,1024]{1,0:T(8,128)S(1)} %slice.127), channel_id=1, source_target_pairs={{0,12},{1,13},{2,14},{3,15},{4,0},{5,1},{6,2},{7,3},{8,4},{9,5},{1... | collective-permute-start | bytes 1572872 | tf_op jit(solution)/shard_map/ppermute | solution.py:283
  52.2 40.9 %collective-permute-start.10 = (f32[256,1024]{1,0:T(8,128)}, f32[256,1024]{1,0:T(8,128)}, u32[]{:S(2)}, u32[]{:S(2)}) collective-permute-start(f32[256,1024]{1,0:T(8,128)} %after.2.refs_7_.refs_2_), channel_id=1, source_target_pairs={{0,4},{1,5},{2,6},{3,7},{4,8},{5,9},{6,10},{7,11},{8,12},{9,13},{1... | collective-permute-start | bytes 3145736 | tf_op jit(solution)/shard_map/ppermute | solution.py:283
  52.2 42.3 %collective-permute-start.11 = (f32[256,1024]{1,0:T(8,128)}, f32[256,1024]{1,0:T(8,128)}, u32[]{:S(2)}, u32[]{:S(2)}) collective-permute-start(f32[256,1024]{1,0:T(8,128)} %after.2.refs_7_.refs_2_), channel_id=1, source_target_pairs={{0,8},{1,9},{2,10},{3,11},{4,12},{5,13},{6,14},{7,15},{8,0},{9,1},... | collective-permute-start | bytes 3145736 | tf_op jit(solution)/shard_map/ppermute | solution.py:283
  54.2 40.2 %collective-permute-start.12 = (f32[256,1024]{1,0:T(8,128)}, f32[256,1024]{1,0:T(8,128)}, u32[]{:S(2)}, u32[]{:S(2)}) collective-permute-start(f32[256,1024]{1,0:T(8,128)} %after.2.refs_7_.refs_2_), channel_id=1, source_target_pairs={{0,12},{1,13},{2,14},{3,15},{4,0},{5,1},{6,2},{7,3},{8,4},{9,5},{1... | collective-permute-start | bytes 3145736 | tf_op jit(solution)/shard_map/ppermute | solution.py:283
  92.3 27.1 %collective-permute-start.7 = (f32[264,1024]{1,0:T(8,128)}, f32[264,1024]{1,0:T(8,128)S(1)}, u32[]{:S(2)}, u32[]{:S(2)}) collective-permute-start(f32[264,1024]{1,0:T(8,128)} %get-tuple-element.31), channel_id=1, source_target_pairs={{0,12},{1,13},{2,14},{3,15},{4,0},{5,1},{6,2},{7,3},{8,4},{9,5},{1... | collective-permute-start | bytes 3244040 | tf_op jit(solution)/shard_map/ppermute | solution.py:283
  92.4 27.0 %collective-permute-start.8 = (f32[264,1024]{1,0:T(8,128)}, f32[264,1024]{1,0:T(8,128)S(1)}, u32[]{:S(2)}, u32[]{:S(2)}) collective-permute-start(f32[264,1024]{1,0:T(8,128)} %get-tuple-element.32), channel_id=1, source_target_pairs={{0,8},{1,9},{2,10},{3,11},{4,12},{5,13},{6,14},{7,15},{8,0},{9,1},... | collective-permute-start | bytes 3244040 | tf_op jit(solution)/shard_map/ppermute | solution.py:283
  93.1 27.8 %collective-permute-start.9 = (f32[264,1024]{1,0:T(8,128)}, f32[264,1024]{1,0:T(8,128)S(1)}, u32[]{:S(2)}, u32[]{:S(2)}) collective-permute-start(f32[264,1024]{1,0:T(8,128)} %get-tuple-element.33), channel_id=1, source_target_pairs={{0,4},{1,5},{2,6},{3,7},{4,8},{5,9},{6,10},{7,11},{8,12},{9,13},{1... | collective-permute-start | bytes 3244040 | tf_op jit(solution)/shard_map/ppermute | solution.py:283
  123.3 21.5 %collective-permute-start.13 = (f32[264,1024]{1,0:T(8,128)}, f32[264,1024]{1,0:T(8,128)S(1)}, u32[]{:S(2)}, u32[]{:S(2)}) collective-permute-start(f32[264,1024]{1,0:T(8,128)} %get-tuple-element.40), channel_id=1, source_target_pairs={{0,12},{1,13},{2,14},{3,15},{4,0},{5,1},{6,2},{7,3},{8,4},{9,5},{1... | collective-permute-start | bytes 3244040 | tf_op jit(solution)/shard_map/ppermute | solution.py:283
  124.5 23.4 %collective-permute-start.14 = (f32[264,1024]{1,0:T(8,128)}, f32[264,1024]{1,0:T(8,128)}, u32[]{:S(2)}, u32[]{:S(2)}) collective-permute-start(f32[264,1024]{1,0:T(8,128)} %get-tuple-element.41), channel_id=1, source_target_pairs={{0,8},{1,9},{2,10},{3,11},{4,12},{5,13},{6,14},{7,15},{8,0},{9,1},... | collective-permute-start | bytes 3244040 | tf_op jit(solution)/shard_map/ppermute | solution.py:283
  126.0 33.3 %collective-permute-start.15 = (f32[264,1024]{1,0:T(8,128)}, f32[264,1024]{1,0:T(8,128)}, u32[]{:S(2)}, u32[]{:S(2)}) collective-permute-start(f32[264,1024]{1,0:T(8,128)} %get-tuple-element.42), channel_id=1, source_target_pairs={{0,4},{1,5},{2,6},{3,7},{4,8},{5,9},{6,10},{7,11},{8,12},{9,13},{1... | collective-permute-start | bytes 3244040 | tf_op jit(solution)/shard_map/ppermute | solution.py:283
  128.8 30.6 %copy-start.2 = (f32[264,1024]{1,0:T(8,128)S(1)}, f32[264,1024]{1,0:T(8,128)}, u32[]{:S(2)}) copy-start(f32[264,1024]{1,0:T(8,128)} %get-tuple-element.35) | copy-start | bytes 3244036
  128.8 36.7 %all-to-all-start = ((f32[4,72,1024]{2,1,0:T(8,128)}), f32[4,72,1024]{2,1,0:T(8,128)S(1)}, u32[]{:S(2)}, u32[]{:S(2)}) async-start(f32[4,72,1024]{2,1,0:T(8,128)} %constant_dynamic-slice_fusion), calls=%async_computation | async-start | bytes 2359296 | tf_op jit(solution)/shard_map/all_to_all | solution.py:350
  161.6 6.9 %collective-permute-start.16 = (f32[72,1024]{1,0:T(8,128)S(1)}, f32[72,1024]{1,0:T(8,128)}, u32[]{:S(2)}, u32[]{:S(2)}) collective-permute-start(f32[72,1024]{1,0:T(8,128)S(1)} %get-tuple-element.69), channel_id=1, source_target_pairs={{0,3},{1,0},{2,1},{3,2},{4,7},{5,4},{6,5},{7,6},{8,11},{9,8},{10,9... | collective-permute-start | bytes 884744 | tf_op jit(solution)/shard_map/ppermute | solution.py:283
  163.4 8.4 %collective-permute-start.17 = (f32[72,1024]{1,0:T(8,128)S(1)}, f32[72,1024]{1,0:T(8,128)}, u32[]{:S(2)}, u32[]{:S(2)}) collective-permute-start(f32[72,1024]{1,0:T(8,128)S(1)} %get-tuple-element.68), channel_id=1, source_target_pairs={{0,2},{1,3},{2,0},{3,1},{4,6},{5,7},{6,4},{7,5},{8,10},{9,11},{10,... | collective-permute-start | bytes 884744 | tf_op jit(solution)/shard_map/ppermute | solution.py:283
  164.9 9.9 %collective-permute-start.18 = (f32[72,1024]{1,0:T(8,128)S(1)}, f32[72,1024]{1,0:T(8,128)}, u32[]{:S(2)}, u32[]{:S(2)}) collective-permute-start(f32[72,1024]{1,0:T(8,128)S(1)} %concatenate.57), channel_id=1, source_target_pairs={{0,1},{1,2},{2,3},{3,0},{4,5},{5,6},{6,7},{7,4},{8,9},{9,10},{10,1... | collective-permute-start | bytes 884744 | tf_op jit(solution)/shard_map/ppermute | solution.py:283
  (5 other events, 24.2 us)
Sparse Core Ops, SparseCore 0:
  9.7 38.7 all-gather.1
  121.7 39.8 reduce-scatter.1
where the time goes:
time: 188 us; the launch traced here: 187 us
  Pallas kernels  61.6 us (33%)
  waiting for transfers between devices  60.2 us (32%)
  starting transfers between devices  29.8 us (16%)
  between operations  15.7 us (8%)
  other arithmetic  14.1 us (8%)
  local copies, waits for them, and re-layouts  5.95 us (3%)
    ppermute x19, waiting for transfers between devices, move(): return lax.ppermute(block, PLANE, perm(inner, k))  59.5 us
    pallas_call x2, Pallas kernels, pairs(): pl.pallas_call(body, grid=(rows // BLOCK,), in_specs=in_specs, out_specs=...  51 us
    ppermute x19, starting transfers between devices, move(): return lax.ppermute(block, PLANE, perm(inner, k))  25.8 us
    pallas_call x1, Pallas kernels, prepare(): pl.pallas_call(prepare_kernel, in_specs=[pl.BlockSpec(memory_space=pltpu....  10.6 us
    all_to_all x1, starting transfers between devices, local(): lax.all_to_all(ring, PLANE, 0, 0, axis_index_groups=INNER)  3.93 us
  transfers between devices with their start and end apart: 22, of which 10 were waited for; matrix products, arithmetic and copies ran while one was open for 9% of the time, Pallas kernels for 33%

commit v1 on v0

--- a/solution.py
+++ b/solution.py
@@ -39,8 +39,8 @@
     return dot(a[0], b[0], dims) + DOWN * dot(a[1], b[1], dims)
 
 
-def prepare_kernel(place, whole, inv_ref, unit_t_out, v_high_out, v_small_out, t_high_out, t_small_out, *scratch):
-    flipped, unit_t_ref, v_high, v_small, t_high, t_small, sems = scratch
+def prepare_kernel(place, own_ref, other_ref, inv_ref, unit_t_out, v_high_out, v_small_out, t_high_out, t_small_out, *scratch):
+    whole, flipped, unit_t_ref, v_high, v_small, t_high, t_small, sems = scratch
     core, y, x = place[0], place[1], place[2]
     n = whole.shape[0]
     outs = (unit_t_out, t_high_out, t_small_out, v_high_out, v_small_out)
@@ -48,6 +48,10 @@
         pltpu.make_async_copy(ref, out, sems.at[k])
         for k, (ref, out) in enumerate(zip((unit_t_ref, t_high, t_small, v_high, v_small), outs))
     ]
+    for k, ref in enumerate((own_ref, other_ref)):
+        side = jnp.where(k == 0, core, 1 - core)
+        for row in range(4):
+            whole[:, pl.ds(pl.multiple_of(256 * row + 128 * side, 128), 128)] = ref[row]
     v_t = whole[...].T
     inv = lax.rsqrt(jnp.sum(v_t * v_t, axis=0, keepdims=True) + EPS)
     inv_ref[...] = inv
@@ -70,8 +74,8 @@
         copy.wait()
 
 
-def prepare(video, place):
-    n = video.shape[0]
+def prepare(own, other, place):
+    n = own.shape[1]
     whole = pl.BlockSpec(memory_space=pltpu.VMEM)
     shape = jax.ShapeDtypeStruct
     parts = [
@@ -83,16 +87,16 @@
     ]
     return pl.pallas_call(
         prepare_kernel,
-        in_specs=[pl.BlockSpec(memory_space=pltpu.SMEM), whole],
+        in_specs=[pl.BlockSpec(memory_space=pltpu.SMEM), whole, whole],
         out_specs=[whole] + [pl.BlockSpec(memory_space=pl.ANY)] * 5,
         out_shape=[shape((1, n), F32)] + parts,
-        scratch_shapes=[pltpu.VMEM((16, 64, n), F32)]
+        scratch_shapes=[pltpu.VMEM((n, 1024), F32), pltpu.VMEM((16, 64, n), F32)]
         + [pltpu.VMEM(p.shape, p.dtype) for p in parts]
         + [pltpu.SemaphoreType.DMA((5,))],
         compiler_params=pltpu.CompilerParams(vmem_limit_bytes=VMEM),
         cost_estimate=pl.CostEstimate(flops=0, bytes_accessed=16 * MIB, transcendentals=0),
         name="video_parts",
-    )(place, video)
+    )(place, own, other)
 
 
 def inverse(d):
@@ -303,7 +307,8 @@
     scalars = jnp.stack([scale, bias])
     base = (2 * z + core) * rows - (4 * y + x) * n
 
-    whole_video = lax.all_gather(video, ("z", "core"), axis=1, tiled=True)
+    own = lax.all_gather(video, "z", axis=0)
+    other = lax.ppermute(own, "core", [(0, 1), (1, 0)])
     row = [audio_t] + [move(audio_t, True, k) for k in (1, 2, 3)]
     gathered, early, starts, start = [], [], [], 0
     for part in CHUNKS:
@@ -320,7 +325,7 @@
         starts.append(start)
         start += part
     place = jnp.stack([core, y, x]).astype(jnp.int32)
-    inv_v, *parts = prepare(whole_video, place)
+    inv_v, *parts = prepare(own, other, place)
     state = None
     invs, halves = [], []
     for c, blocks in enumerate(gathered):
@@ -336,8 +341,12 @@
             grads = [grads[0], *others]
             halves.append(kept + came[0] + came[1] + came[2])
         kept = grads[0]
-        came = [move(grads[k], False, 4 - k) for k in (1, 2, 3)]
-    halves.append(kept + came[0] + came[1] + came[2])
+        if not last:
+            came = [move(grads[k], False, 4 - k) for k in (1, 2, 3)]
+    top, bottom = move(grads[2][:128], False, 3), move(grads[2][128:], False, 1)
+    below = jnp.concatenate([grads[1][:128] + top, grads[1][128:]], axis=0)
+    above = jnp.concatenate([grads[3][:128], grads[3][128:] + bottom], axis=0)
+    halves.append(kept + move(below, False, 3) + move(above, False, 1))
 
     total_v = lax.psum_scatter(state.reshape(1088, n), ("z", "core"), scatter_dimension=0, tiled=True)
     place_in = jnp.where(core == 0, x, y)

time: 188 us -> 216 us (1.15)
  local copies, waits for them, and re-layouts: 5.95 us -> 15.8 us
  starting transfers between devices: 29.8 us -> 38.5 us
  waiting for transfers between devices: 60.2 us -> 68.3 us
    all_gather x1, waiting for transfers between devices: 0.01 us -> 23.8 us  [local(): own = lax.all_gather(video, 'z', axis=0)]
    ppermute x19 -> x20, waiting for transfers between devices: 59.5 us -> 43.8 us  [move(): return lax.ppermute(block, PLANE, perm(inner, k))]
    ppermute x19 -> x20, starting transfers between devices: 25.8 us -> 34.6 us  [move(): return lax.ppermute(block, PLANE, perm(inner, k))]
    unnamed x19 -> x41, local copies, waits for them, and re-layouts: 1.27 us -> 6.49 us
    add x2 -> x1, other arithmetic: 3.7 us -> 0.43 us  [local(): halves.append(kept + came[0] + came[1] + came[2])]
    slice x4, local copies, waits for them, and re-layouts: 1.17 us -> 4.06 us  [local(): block = jnp.concatenate([r[:, start:start + part] for r in row], axis=0)]
    add x0 -> x3, other arithmetic: none -> 2.38 us  [the longest x1 2.22 us: local(): halves.append(kept + move(below, False, 3) + move(above, False, 1))]
  transfers between devices with their start and end apart: 22 -> 24, of which waited for: 10 -> 9; matrix products, arithmetic and copies ran while one was open for 9% -> 10% of each run, Pallas kernels for 33% -> 29%
where the time goes in v1:
time: 216 us; the launch traced here: 215 us
  waiting for transfers between devices  68.3 us (32%)
  Pallas kernels  62.3 us (29%)
  starting transfers between devices  38.5 us (18%)
  local copies, waits for them, and re-layouts  15.8 us (7%)
  between operations  15.8 us (7%)
  other arithmetic  14.6 us (7%)
    pallas_call x2, Pallas kernels, pairs(): pl.pallas_call(body, grid=(rows // BLOCK,), in_specs=in_specs, out_specs=...  51 us
    ppermute x20, waiting for transfers between devices, move(): return lax.ppermute(block, PLANE, perm(inner, k))  43.8 us
    ppermute x20, starting transfers between devices, move(): return lax.ppermute(block, PLANE, perm(inner, k))  34.6 us
    all_gather x1, waiting for transfers between devices, local(): own = lax.all_gather(video, 'z', axis=0)  23.8 us
    pallas_call x1, Pallas kernels, prepare(): pl.pallas_call(prepare_kernel, in_specs=[pl.BlockSpec(memory_space=pltpu....  11.3 us
    unnamed x41, local copies, waits for them, and re-layouts  6.49 us
  transfers between devices with their start and end apart: 24, of which 9 were waited for; matrix products, arithmetic and copies ran while one was open for 10% of the time, Pallas kernels for 29%

profile of v1, /device:TPU:0, one launch (start us, length us, event | category | flops | bytes accessed | tf_op | source)
XLA Modules:
  0.0 215.2 jit_solution(13011721494888900061)
XLA Ops:
  9.6 2.7 %collective-permute-start.1 = (f32[64,2048]{1,0:T(8,128)}, f32[64,2048]{1,0:T(8,128)S(1)}, u32[]{:S(2)}, u32[]{:S(2)}) collective-permute-start(f32[64,2048]{1,0:T(8,128)} %bitcast.50), channel_id=1, source_target_pairs={{0,2},{1,3},{2,0},{3,1},{4,6},{5,7},{6,4},{7,5},{8,10},{9,11},{10,... | collective-permute-start | bytes 1572872 | tf_op jit(solution)/shard_map/ppermute | solution.py:287
  13.8 1.8 fusion.22
  15.5 3.1 %collective-permute-done = f32[64,2048]{1,0:T(8,128)S(1)} collective-permute-done((f32[64,2048]{1,0:T(8,128)}, f32[64,2048]{1,0:T(8,128)S(1)}, u32[]{:S(2)}, u32[]{:S(2)}) %collective-permute-start) | collective-permute-done | bytes 524320 | tf_op jit(solution)/shard_map/ppermute | solution.py:287
  19.4 23.8 %all-gather.3.cloned.1.call-done = f32[4096,128]{1,0:T(8,128)} async-done(((f32[1024,128]{1,0:T(8,128)}), f32[4096,128]{1,0:T(8,128)}) %all-gather.3.cloned.1.call-update) | async-done | bytes 2097168 | tf_op jit(solution)/shard_map/all_gather | solution.py:310
  49.4 11.6 %collective-permute-done.3.refs_3_ = f32[256,1024]{1,0:T(8,128)} collective-permute-done((f32[256,1024]{1,0:T(8,128)S(1)}, f32[256,1024]{1,0:T(8,128)}, u32[]{:S(2)}, u32[]{:S(2)}) %collective-permute-start.3) | collective-permute-done | bytes 1048608 | tf_op jit(solution)/shard_map/ppermute | solution.py:287
  61.0 1.9 slice.150
  63.1 1.9 slice.151
  65.0 3.0 %collective-permute-start.6 = (f32[128,1024]{1,0:T(8,128)}, f32[128,1024]{1,0:T(8,128)}, u32[]{:S(2)}, u32[]{:S(2)}) collective-permute-start(f32[128,1024]{1,0:T(8,128)} %slice.151), channel_id=1, source_target_pairs={{0,12},{1,13},{2,14},{3,15},{4,0},{5,1},{6,2},{7,3},{8,4},{9,5},{1... | collective-permute-start | bytes 1572872 | tf_op jit(solution)/shard_map/ppermute | solution.py:287
  70.5 2.2 %pad_maximum_fusion.3.refs_1_ = f32[256,1024]{1,0:T(8,128)} fusion(f32[64,1024]{1,0:T(8,128)} %get-tuple-element.66, f32[64,1024]{1,0:T(8,128)} %get-tuple-element.64, f32[64,1024]{1,0:T(8,128)} %get-tuple-element.62, f32[64,1024]{1,0:T(8,128)S(1)} %get-tuple-element.60), kind=kLoop, calls=%fused_computation.5 | loop fusion | flops 786432 | bytes 2097152 | tf_op jit(solution)/shard_map/concatenate | solution.py:315
  74.1 1.8 collective-permute-start.12
  77.4 11.3 %video_parts.1 = (f32[1,1024]{1,0:T(1,128)}, f32[1024,1024]{1,0:T(8,128)}, bf16[1024,1024]{1,0:T(8,128)(2,1)}, f8e4m3fn[1024,2048]{1,0:T(32,128)(4,1)}, bf16[102...) custom-call(s32[3]{0:T(128)} %pad_add_fusion.2.place, f32[4,1024,128]{2,1,0:T(8,128)} %bitcast.48, ...), custom_call_target="tpu_custom_call" | custom-call | bytes 16777216 | tf_op jit(solution)/shard_map/video_parts/pallas_call | solution.py:88
  88.7 26.0 %pairs_first.1 = (f32[264,1024]{1,0:T(8,128)}, f32[264,1024]{1,0:T(8,128)}, f32[264,1024]{1,0:T(8,128)}, f32[264,1024]{1,0:T(8,128)}, f32[1,1024]{1,0:T(1,128)}, /*index=5*/f32[1024,1024]{1,0:T(8,128)}) custom-call(s32[4]{0:T(128)} %pad_add_fusion.refs_0_, f32[2]{0:T(128)} %pad_maximum_fusion.12.refs_1_, f32[256,1024]{1,0:T(8,128)} %copy-done.9, ...), custom_call_target="tpu_custom_call" | custom-call | flops 12884901888 | bytes 25165824 | tf_op jit(solution)/shard_map/pairs_first/pallas_call | solution.py:260
  114.9 3.2 %collective-permute-start.8 = (f32[264,1024]{1,0:T(8,128)}, f32[264,1024]{1,0:T(8,128)S(1)}, u32[]{:S(2)}, u32[]{:S(2)}) collective-permute-start(f32[264,1024]{1,0:T(8,128)} %get-tuple-element.31), channel_id=1, source_target_pairs={{0,12},{1,13},{2,14},{3,15},{4,0},{5,1},{6,2},{7,3},{8,4},{9,5},{1... | collective-permute-start | bytes 3244040 | tf_op jit(solution)/shard_map/ppermute | solution.py:287
  119.7 24.9 %pairs_last.1 = (f32[264,1024]{1,0:T(8,128)}, f32[264,1024]{1,0:T(8,128)}, f32[264,1024]{1,0:T(8,128)}, f32[264,1024]{1,0:T(8,128)}, f32[1,1024]{1,0:T(1,128)}, /*index=5*/f32[8,136,1024]{2,1,0:T(8,128)}) custom-call(s32[4]{0:T(128)} %get-tuple-element.50.refs_0_, f32[2]{0:T(128)} %pad_maximum_fusion.12.refs_1_, f32[256,1024]{1,0:T(8,128)} %after.2.refs_7_.refs_2_, ...), custom_call_target="tpu_custom_call" | custom-call | flops 12884901888 | bytes 25165824 | tf_op jit(solution)/shard_map/pairs_last/pallas_call | solution.py:260
  151.8 5.1 %collective-permute-done.14 = f32[128,1024]{1,0:T(8,128)S(1)} collective-permute-done((f32[128,1024]{1,0:T(8,128)S(1)}, f32[128,1024]{1,0:T(8,128)S(1)}, u32[]{:S(2)}, u32[]{:S(2)}) %collective-permute-start.14) | collective-permute-done | bytes 524320 | tf_op jit(solution)/shard_map/ppermute | solution.py:287
  157.1 2.8 %collective-permute-start.15 = (f32[264,1024]{1,0:T(8,128)S(1)}, f32[264,1024]{1,0:T(8,128)}, u32[]{:S(2)}, u32[]{:S(2)}) collective-permute-start(f32[264,1024]{1,0:T(8,128)S(1)} %pad_maximum_fusion), channel_id=1, source_target_pairs={{0,12},{1,13},{2,14},{3,15},{4,0},{5,1},{6,2},{7,3},{8,4},{9,5},{1... | collective-permute-start | bytes 3244040 | tf_op jit(solution)/shard_map/ppermute | solution.py:287
  161.9 3.9 %all-to-all-start = ((f32[4,72,1024]{2,1,0:T(8,128)}), f32[4,72,1024]{2,1,0:T(8,128)S(1)}, u32[]{:S(2)}, u32[]{:S(2)}) async-start(f32[4,72,1024]{2,1,0:T(8,128)} %constant_dynamic-slice_fusion), calls=%async_computation | async-start | bytes 2359296 | tf_op jit(solution)/shard_map/all_to_all | solution.py:359
  165.8 13.2 %collective-permute-done.15 = f32[264,1024]{1,0:T(8,128)} collective-permute-done((f32[264,1024]{1,0:T(8,128)S(1)}, f32[264,1024]{1,0:T(8,128)}, u32[]{:S(2)}, u32[]{:S(2)}) %collective-permute-start.15) | collective-permute-done | bytes 1081376 | tf_op jit(solution)/shard_map/ppermute | solution.py:287
  178.9 4.4 %collective-permute-done.17 = f32[264,1024]{1,0:T(8,128)} collective-permute-done((f32[264,1024]{1,0:T(8,128)S(1)}, f32[264,1024]{1,0:T(8,128)}, u32[]{:S(2)}, u32[]{:S(2)}) %collective-permute-start.17) | collective-permute-done | bytes 1081376 | tf_op jit(solution)/shard_map/ppermute | solution.py:287
  183.3 2.2 %add_add_fusion = f32[264,1024]{1,0:T(8,128)S(1)} fusion(f32[264,1024]{1,0:T(8,128)} %collective-permute-done.17, f32[264,1024]{1,0:T(8,128)} %get-tuple-element.35, f32[264,1024]{1,0:T(8,128)} %collective-permute-done.15), kind=kLoop, calls=%fused_computation.2 | loop fusion | flops 540672 | bytes 4325376 | tf_op jit(solution)/shard_map/add | solution.py:349
  185.7 2.4 %collective-permute-start.18 = (f32[72,1024]{1,0:T(8,128)S(1)}, f32[72,1024]{1,0:T(8,128)}, u32[]{:S(2)}, u32[]{:S(2)}) collective-permute-start(f32[72,1024]{1,0:T(8,128)S(1)} %get-tuple-element.69), channel_id=1, source_target_pairs={{0,3},{1,0},{2,1},{3,2},{4,7},{5,4},{6,5},{7,6},{8,11},{9,8},{10,9... | collective-permute-start | bytes 884744 | tf_op jit(solution)/shard_map/ppermute | solution.py:287
  188.2 6.6 %collective-permute-start.19 = (f32[72,1024]{1,0:T(8,128)S(1)}, f32[72,1024]{1,0:T(8,128)}, u32[]{:S(2)}, u32[]{:S(2)}) collective-permute-start(f32[72,1024]{1,0:T(8,128)S(1)} %get-tuple-element.68), channel_id=1, source_target_pairs={{0,2},{1,3},{2,0},{3,1},{4,6},{5,7},{6,4},{7,5},{8,10},{9,11},{10,... | collective-permute-start | bytes 884744 | tf_op jit(solution)/shard_map/ppermute | solution.py:287
  196.4 3.1 %collective-permute-done.19 = f32[72,1024]{1,0:T(8,128)} collective-permute-done((f32[72,1024]{1,0:T(8,128)S(1)}, f32[72,1024]{1,0:T(8,128)}, u32[]{:S(2)}, u32[]{:S(2)}) %collective-permute-start.19) | collective-permute-done | bytes 294944 | tf_op jit(solution)/shard_map/ppermute | solution.py:287
  199.5 3.2 %collective-permute-done.20 = f32[72,1024]{1,0:T(8,128)} collective-permute-done((f32[72,1024]{1,0:T(8,128)S(1)}, f32[72,1024]{1,0:T(8,128)}, u32[]{:S(2)}, u32[]{:S(2)}) %collective-permute-start.20) | collective-permute-done | bytes 294944 | tf_op jit(solution)/shard_map/ppermute | solution.py:287
  (115 shorter events, 33.4 us)
Async XLA Ops:
  7.2 36.1 %all-gather.3.cloned.1.call-start = ((), (), s32[]{:S(2)}) async-start(), calls=%async_computation.3 | async-start | bytes 2621440 | tf_op jit(solution)/shard_map/all_gather | solution.py:310
  7.9 197.6 %reduce-scatter.2.cloned.1.call-start = ((), (), s32[]{:S(2)}) async-start(), calls=%async_computation.2 | async-start | bytes 5013504 | tf_op jit(solution)/shard_map/reduce_scatter | solution.py:351
  7.9 10.7 %collective-permute-start = (f32[64,2048]{1,0:T(8,128)}, f32[64,2048]{1,0:T(8,128)S(1)}, u32[]{:S(2)}, u32[]{:S(2)}) collective-permute-start(f32[64,2048]{1,0:T(8,128)} %bitcast.49), channel_id=1, source_target_pairs={{0,1},{1,2},{2,3},{3,0},{4,5},{5,6},{6,7},{7,4},{8,9},{9,10},{10,1... | collective-permute-start | bytes 1572872 | tf_op jit(solution)/shard_map/ppermute | solution.py:287
  9.6 33.6 %collective-permute-start.1 = (f32[64,2048]{1,0:T(8,128)}, f32[64,2048]{1,0:T(8,128)S(1)}, u32[]{:S(2)}, u32[]{:S(2)}) collective-permute-start(f32[64,2048]{1,0:T(8,128)} %bitcast.50), channel_id=1, source_target_pairs={{0,2},{1,3},{2,0},{3,1},{4,6},{5,7},{6,4},{7,5},{8,10},{9,11},{10,... | collective-permute-start | bytes 1572872 | tf_op jit(solution)/shard_map/ppermute | solution.py:287
  12.3 31.7 %collective-permute-start.2 = (f32[64,2048]{1,0:T(8,128)}, f32[64,2048]{1,0:T(8,128)S(1)}, u32[]{:S(2)}, u32[]{:S(2)}) collective-permute-start(f32[64,2048]{1,0:T(8,128)} %bitcast.51), channel_id=1, source_target_pairs={{0,3},{1,0},{2,1},{3,2},{4,7},{5,4},{6,5},{7,6},{8,11},{9,8},{10,9... | collective-permute-start | bytes 1572872 | tf_op jit(solution)/shard_map/ppermute | solution.py:287
  43.2 32.6 %collective-permute-start.7 = (f32[4,1024,128]{2,1,0:T(8,128)}, f32[4,1024,128]{2,1,0:T(8,128)S(1)}, u32[]{:S(2)}, u32[]{:S(2)}) collective-permute-start(f32[4,1024,128]{2,1,0:T(8,128)} %bitcast.47), channel_id=1, source_target_pairs={{0,16},{16,0},{1,17},{17,1},{2,18},{18,2},{3,19},{19,3},{4,20},{20... | collective-permute-start | bytes 6291464 | tf_op jit(solution)/shard_map/ppermute | solution.py:311
  44.8 16.2 %collective-permute-start.3 = (f32[256,1024]{1,0:T(8,128)S(1)}, f32[256,1024]{1,0:T(8,128)}, u32[]{:S(2)}, u32[]{:S(2)}) collective-permute-start(f32[256,1024]{1,0:T(8,128)S(1)} %pad_maximum_fusion.2.refs_2_), channel_id=1, source_target_pairs={{0,4},{1,5},{2,6},{3,7},{4,8},{5,9},{6,10},{7,11},{8,12},{9,13},{1... | collective-permute-start | bytes 3145736 | tf_op jit(solution)/shard_map/ppermute | solution.py:287
  46.3 16.8 %collective-permute-start.5 = (f32[256,1024]{1,0:T(8,128)S(1)}, f32[256,1024]{1,0:T(8,128)}, u32[]{:S(2)}, u32[]{:S(2)}) collective-permute-start(f32[256,1024]{1,0:T(8,128)S(1)} %pad_maximum_fusion.2.refs_2_), channel_id=1, source_target_pairs={{0,12},{1,13},{2,14},{3,15},{4,0},{5,1},{6,2},{7,3},{8,4},{9,5},{1... | collective-permute-start | bytes 3145736 | tf_op jit(solution)/shard_map/ppermute | solution.py:287
  62.9 25.9 %collective-permute-start.4 = (f32[128,1024]{1,0:T(8,128)}, f32[128,1024]{1,0:T(8,128)}, u32[]{:S(2)}, u32[]{:S(2)}) collective-permute-start(f32[128,1024]{1,0:T(8,128)} %slice.150), channel_id=1, source_target_pairs={{0,4},{1,5},{2,6},{3,7},{4,8},{5,9},{6,10},{7,11},{8,12},{9,13},{1... | collective-permute-start | bytes 1572872 | tf_op jit(solution)/shard_map/ppermute | solution.py:287
  65.0 23.7 %collective-permute-start.6 = (f32[128,1024]{1,0:T(8,128)}, f32[128,1024]{1,0:T(8,128)}, u32[]{:S(2)}, u32[]{:S(2)}) collective-permute-start(f32[128,1024]{1,0:T(8,128)} %slice.151), channel_id=1, source_target_pairs={{0,12},{1,13},{2,14},{3,15},{4,0},{5,1},{6,2},{7,3},{8,4},{9,5},{1... | collective-permute-start | bytes 1572872 | tf_op jit(solution)/shard_map/ppermute | solution.py:287
  74.1 44.0 %collective-permute-start.11 = (f32[256,1024]{1,0:T(8,128)}, f32[256,1024]{1,0:T(8,128)S(1)}, u32[]{:S(2)}, u32[]{:S(2)}) collective-permute-start(f32[256,1024]{1,0:T(8,128)} %after.2.refs_7_.refs_2_), channel_id=1, source_target_pairs={{0,4},{1,5},{2,6},{3,7},{4,8},{5,9},{6,10},{7,11},{8,12},{9,13},{1... | collective-permute-start | bytes 3145736 | tf_op jit(solution)/shard_map/ppermute | solution.py:287
  74.1 44.0 %collective-permute-start.12 = (f32[256,1024]{1,0:T(8,128)}, f32[256,1024]{1,0:T(8,128)S(1)}, u32[]{:S(2)}, u32[]{:S(2)}) collective-permute-start(f32[256,1024]{1,0:T(8,128)} %after.2.refs_7_.refs_2_), channel_id=1, source_target_pairs={{0,8},{1,9},{2,10},{3,11},{4,12},{5,13},{6,14},{7,15},{8,0},{9,1},... | collective-permute-start | bytes 3145736 | tf_op jit(solution)/shard_map/ppermute | solution.py:287
  75.9 42.2 %collective-permute-start.13 = (f32[256,1024]{1,0:T(8,128)}, f32[256,1024]{1,0:T(8,128)S(1)}, u32[]{:S(2)}, u32[]{:S(2)}) collective-permute-start(f32[256,1024]{1,0:T(8,128)} %after.2.refs_7_.refs_2_), channel_id=1, source_target_pairs={{0,12},{1,13},{2,14},{3,15},{4,0},{5,1},{6,2},{7,3},{8,4},{9,5},{1... | collective-permute-start | bytes 3145736 | tf_op jit(solution)/shard_map/ppermute | solution.py:287
  114.8 29.9 %collective-permute-start.10 = (f32[264,1024]{1,0:T(8,128)}, f32[264,1024]{1,0:T(8,128)S(1)}, u32[]{:S(2)}, u32[]{:S(2)}) collective-permute-start(f32[264,1024]{1,0:T(8,128)} %get-tuple-element.33), channel_id=1, source_target_pairs={{0,4},{1,5},{2,6},{3,7},{4,8},{5,9},{6,10},{7,11},{8,12},{9,13},{1... | collective-permute-start | bytes 3244040 | tf_op jit(solution)/shard_map/ppermute | solution.py:287
  114.9 29.8 %collective-permute-start.8 = (f32[264,1024]{1,0:T(8,128)}, f32[264,1024]{1,0:T(8,128)S(1)}, u32[]{:S(2)}, u32[]{:S(2)}) collective-permute-start(f32[264,1024]{1,0:T(8,128)} %get-tuple-element.31), channel_id=1, source_target_pairs={{0,12},{1,13},{2,14},{3,15},{4,0},{5,1},{6,2},{7,3},{8,4},{9,5},{1... | collective-permute-start | bytes 3244040 | tf_op jit(solution)/shard_map/ppermute | solution.py:287
  118.1 26.6 %collective-permute-start.9 = (f32[264,1024]{1,0:T(8,128)}, f32[264,1024]{1,0:T(8,128)S(1)}, u32[]{:S(2)}, u32[]{:S(2)}) collective-permute-start(f32[264,1024]{1,0:T(8,128)} %get-tuple-element.32), channel_id=1, source_target_pairs={{0,8},{1,9},{2,10},{3,11},{4,12},{5,13},{6,14},{7,15},{8,0},{9,1},... | collective-permute-start | bytes 3244040 | tf_op jit(solution)/shard_map/ppermute | solution.py:287
  147.6 9.2 %collective-permute-start.14 = (f32[128,1024]{1,0:T(8,128)S(1)}, f32[128,1024]{1,0:T(8,128)S(1)}, u32[]{:S(2)}, u32[]{:S(2)}) collective-permute-start(f32[128,1024]{1,0:T(8,128)S(1)} %slice.132), channel_id=1, source_target_pairs={{0,12},{1,13},{2,14},{3,15},{4,0},{5,1},{6,2},{7,3},{8,4},{9,5},{1... | collective-permute-start | bytes 1572872 | tf_op jit(solution)/shard_map/ppermute | solution.py:287
  149.3 10.7 %collective-permute-start.16 = (f32[136,1024]{1,0:T(8,128)S(1)}, f32[136,1024]{1,0:T(8,128)S(1)}, u32[]{:S(2)}, u32[]{:S(2)}) collective-permute-start(f32[136,1024]{1,0:T(8,128)S(1)} %slice.136), channel_id=1, source_target_pairs={{0,4},{1,5},{2,6},{3,7},{4,8},{5,9},{6,10},{7,11},{8,12},{9,13},{1... | collective-permute-start | bytes 1671176 | tf_op jit(solution)/shard_map/ppermute | solution.py:287
  157.1 21.9 %collective-permute-start.15 = (f32[264,1024]{1,0:T(8,128)S(1)}, f32[264,1024]{1,0:T(8,128)}, u32[]{:S(2)}, u32[]{:S(2)}) collective-permute-start(f32[264,1024]{1,0:T(8,128)S(1)} %pad_maximum_fusion), channel_id=1, source_target_pairs={{0,12},{1,13},{2,14},{3,15},{4,0},{5,1},{6,2},{7,3},{8,4},{9,5},{1... | collective-permute-start | bytes 3244040 | tf_op jit(solution)/shard_map/ppermute | solution.py:287
  160.2 23.1 %collective-permute-start.17 = (f32[264,1024]{1,0:T(8,128)S(1)}, f32[264,1024]{1,0:T(8,128)}, u32[]{:S(2)}, u32[]{:S(2)}) collective-permute-start(f32[264,1024]{1,0:T(8,128)S(1)} %pad_maximum_fusion.1), channel_id=1, source_target_pairs={{0,4},{1,5},{2,6},{3,7},{4,8},{5,9},{6,10},{7,11},{8,12},{9,13},{1... | collective-permute-start | bytes 3244040 | tf_op jit(solution)/shard_map/ppermute | solution.py:287
  161.9 34.4 %all-to-all-start = ((f32[4,72,1024]{2,1,0:T(8,128)}), f32[4,72,1024]{2,1,0:T(8,128)S(1)}, u32[]{:S(2)}, u32[]{:S(2)}) async-start(f32[4,72,1024]{2,1,0:T(8,128)} %constant_dynamic-slice_fusion), calls=%async_computation | async-start | bytes 2359296 | tf_op jit(solution)/shard_map/all_to_all | solution.py:359
  185.7 10.7 %collective-permute-start.18 = (f32[72,1024]{1,0:T(8,128)S(1)}, f32[72,1024]{1,0:T(8,128)}, u32[]{:S(2)}, u32[]{:S(2)}) collective-permute-start(f32[72,1024]{1,0:T(8,128)S(1)} %get-tuple-element.69), channel_id=1, source_target_pairs={{0,3},{1,0},{2,1},{3,2},{4,7},{5,4},{6,5},{7,6},{8,11},{9,8},{10,9... | collective-permute-start | bytes 884744 | tf_op jit(solution)/shard_map/ppermute | solution.py:287
  188.2 11.4 %collective-permute-start.19 = (f32[72,1024]{1,0:T(8,128)S(1)}, f32[72,1024]{1,0:T(8,128)}, u32[]{:S(2)}, u32[]{:S(2)}) collective-permute-start(f32[72,1024]{1,0:T(8,128)S(1)} %get-tuple-element.68), channel_id=1, source_target_pairs={{0,2},{1,3},{2,0},{3,1},{4,6},{5,7},{6,4},{7,5},{8,10},{9,11},{10,... | collective-permute-start | bytes 884744 | tf_op jit(solution)/shard_map/ppermute | solution.py:287
  194.7 8.0 %collective-permute-start.20 = (f32[72,1024]{1,0:T(8,128)S(1)}, f32[72,1024]{1,0:T(8,128)}, u32[]{:S(2)}, u32[]{:S(2)}) collective-permute-start(f32[72,1024]{1,0:T(8,128)S(1)} %concatenate.65), channel_id=1, source_target_pairs={{0,1},{1,2},{2,3},{3,0},{4,5},{5,6},{6,7},{7,4},{8,9},{9,10},{10,1... | collective-permute-start | bytes 884744 | tf_op jit(solution)/shard_map/ppermute | solution.py:287
  (18 other events, 84.8 us)
Sparse Core Ops, SparseCore 0:
  9.7 33.5 all-gather.2
  146.5 37.8 reduce-scatter.1

commit v2 on v0

--- a/solution.py
+++ b/solution.py
@@ -12,15 +12,14 @@
 UP_REST = 2.0**17
 DOWN = 2.0**-25
 EPS = 1e-06
-CHUNKS = (1024, 1024)
 BLOCK = 512
 SUBS = 2
 VMEM = 56 * 2**20
 PLANE = ("core", "y", "x")
 MIB = 2**20
-ROWS = [[4 * i + j for j in range(4)] for i in range(4)]
-COLUMNS = [[16 + 4 * j + i for j in range(4)] for i in range(4)]
-INNER = ROWS + COLUMNS
+COLUMNS = [[4 * j + i for j in range(4)] for i in range(4)]
+ROWS = [[16 + 4 * i + j for j in range(4)] for i in range(4)]
+OUTER = COLUMNS + ROWS
 
 
 def dot(a, b, dims):
@@ -104,16 +103,21 @@
     return jnp.where(power < 1e-3, power - 0.5 * power * power, jnp.log(1.0 + power))
 
 
-def pairs_kernel(first, last, count, skipped, refs):
+def pairs_kernel(first, last, refs):
     place, scalars, *refs = refs
-    audio, refs = refs[:count], refs[count + skipped :]
+    audio, refs = refs[:4], refs[4:]
     unit_t_hbm, *sources = refs[:5]
     sources.append(unit_t_hbm)
     refs = refs[5:]
     before = None
     if not first:
         before, *refs = refs
-    grads_a, inv_ref, refs = refs[:4], refs[4], refs[5:]
+    if last:
+        grads_a, refs = refs[:4], refs[4:]
+    else:
+        grads_a = [refs[0].at[lax.rem(place[4] + 4 - k, 4)] for k in range(4)]
+        refs = refs[1:]
+    inv_ref, *refs = refs
     if last:
         whole, *refs = refs
     state, near, v_high, v_small, t_high, t_small, sems = refs
@@ -224,48 +228,63 @@
                     whole[owner, 64 * part : 64 * part + 64, :] = state[rows, :]
 
 
-def pairs(audio, ahead, video, place, scalars, before, last):
+def pairs(audio, video, place, scalars, before, last):
     rows = audio[0].shape[1]
     first = before is None
     n = video[1].shape[0]
     smem = pl.BlockSpec(memory_space=pltpu.SMEM)
-    still = lambda shape: pl.BlockSpec(shape, lambda i: (0, 0), pipeline_mode=pl.Buffered(1))
-    moving = lambda height: pl.BlockSpec((height, BLOCK), lambda i: (0, i))
+    anywhere = pl.BlockSpec(memory_space=pl.ANY)
     shape = jax.ShapeDtypeStruct
-    anywhere = pl.BlockSpec(memory_space=pl.ANY)
-    in_specs = [smem, smem] + [moving(a.shape[0]) for a in audio] + [anywhere] * (len(ahead) + 5)
-    operands = [place, scalars, *audio, *ahead, *video]
-    out_specs = [moving(264)] * 4 + [moving(1)]
-    out_shape = [shape((264, rows), F32)] * 4 + [shape((1, rows), F32)]
-    scratch = [pltpu.VMEM((1024, n), F32)] + [pltpu.VMEM(v.shape, v.dtype) for v in video[1:]]
-    scratch.append(pltpu.SemaphoreType.DMA((6,)))
+
+    def still(shape):
+        return pl.BlockSpec(shape, lambda i, at: (0,) * len(shape), pipeline_mode=pl.Buffered(1))
+
+    def moving(height):
+        return pl.BlockSpec((height, BLOCK), lambda i, at: (0, i))
+
+    def turned(k):
+        return pl.BlockSpec((256, BLOCK), lambda i, at: (lax.rem(at[4] + 4 - k, 4), i))
+
+    if len(audio) == 1:
+        blocks = [turned(k) for k in range(4)]
+    else:
+        blocks = [moving(256)] * 4
+    in_specs = [smem] + blocks + [anywhere] * 5
+    operands = [scalars, *(audio * (4 // len(audio))), *video]
+    parts = [pltpu.VMEM(v.shape, v.dtype) for v in (video[0], *video[1:])]
+    parts.append(pltpu.SemaphoreType.DMA((6,)))
     if not first:
         in_specs.append(anywhere)
         operands.append(before)
     if last:
-        out_specs.append(pl.BlockSpec((8, 136, n), lambda i: (0, 0, 0), pipeline_mode=pl.Buffered(1)))
-        out_shape.append(shape((8, 136, n), F32))
-        scratch = [pltpu.VMEM((1024, n), F32)] + scratch
+        out_specs = [moving(264)] * 4 + [moving(1), still((8, 136, n))]
+        out_shape = [shape((264, rows), F32)] * 4 + [shape((1, rows), F32), shape((8, 136, n), F32)]
+        scratch = [pltpu.VMEM((1024, n), F32)] + parts
     else:
-        out_specs.append(still((1024, n)))
-        out_shape.append(shape((1024, n), F32))
+        whole = pl.BlockSpec((4, 264, BLOCK), lambda i, at: (0, 0, i))
+        out_specs = [whole, moving(1), still((1024, n))]
+        out_shape = [shape((4, 264, rows), F32), shape((1, rows), F32), shape((1024, n), F32)]
+        scratch = parts
 
     def body(*refs):
-        pairs_kernel(first, last, len(audio), len(ahead), refs)
+        pairs_kernel(first, last, refs)
 
     return pl.pallas_call(
         body,
-        grid=(rows // BLOCK,),
-        in_specs=in_specs,
-        out_specs=out_specs,
+        grid_spec=pltpu.PrefetchScalarGridSpec(
+            num_scalar_prefetch=1,
+            grid=(rows // BLOCK,),
+            in_specs=in_specs,
+            out_specs=out_specs,
+            scratch_shapes=scratch,
+        ),
         out_shape=out_shape,
-        scratch_shapes=scratch,
         compiler_params=pltpu.CompilerParams(vmem_limit_bytes=VMEM),
         cost_estimate=pl.CostEstimate(
             flops=6 * 2 * rows * n * 1024, bytes_accessed=24 * MIB, transcendentals=3 * rows * n
         ),
-        name="pairs_last" if last else "pairs_first" if first else "pairs_next",
-    )(*operands)
+        name="pairs_last" if last else "pairs_first",
+    )(place, *operands)
 
 
 def perm(inner, k):
@@ -305,56 +324,34 @@
 
     whole_video = lax.all_gather(video, ("z", "core"), axis=1, tiled=True)
     row = [audio_t] + [move(audio_t, True, k) for k in (1, 2, 3)]
-    gathered, early, starts, start = [], [], [], 0
-    for part in CHUNKS:
-        block = jnp.concatenate([r[:, start : start + part] for r in row], axis=0)
-        if start > 0:
-            (block,) = after([below[:8] + above[:8]], [block])
-        below, above = move(block, False, 1), move(block, False, 3)
-        if start + part < rows:
-            far = [move(below[:128], False, 1), move(above[128:], False, 3)]
-        else:
-            far = [move(block, False, 2)]
-        gathered.append([block, below, *far, above])
-        early.append([below, above] if start + part < rows else [block])
-        starts.append(start)
-        start += part
-    place = jnp.stack([core, y, x]).astype(jnp.int32)
-    inv_v, *parts = prepare(whole_video, place)
-    state = None
-    invs, halves = [], []
-    for c, blocks in enumerate(gathered):
-        at = jnp.stack([core, y, x, base + starts[c]]).astype(jnp.int32)
-        last = c == len(CHUNKS) - 1
-        ahead = early[c + 1] if c + 1 < len(CHUNKS) else []
-        outs = pairs(blocks, ahead, parts, at, scalars, state, last)
-        grads, inv, state = outs[:4], outs[4], outs[5]
-        invs.append(inv)
-        if c > 0:
-            seen = came[0][256:264] + came[1][256:264] + came[2][256:264]
-            *others, state = after([seen], [*grads[1:], state])
-            grads = [grads[0], *others]
-            halves.append(kept + came[0] + came[1] + came[2])
-        kept = grads[0]
-        came = [move(grads[k], False, 4 - k) for k in (1, 2, 3)]
-    halves.append(kept + came[0] + came[1] + came[2])
+    part = rows // 2
+    near, late = (jnp.concatenate([r[:, c * part : (c + 1) * part] for r in row], axis=0) for c in (0, 1))
+    near = [near] + [move(near, False, k) for k in (1, 2, 3)]
+    late = [lax.all_gather(late, PLANE, axis=0, tiled=True, axis_index_groups=OUTER)]
+    inv_v, *parts = prepare(whole_video, jnp.stack([core, y, x]).astype(jnp.int32))
+    outer = jnp.where(core == 0, y, x)
+    places = [jnp.stack([core, y, x, base + c * part, outer]).astype(jnp.int32) for c in (0, 1)]
+    whole, inv_near, state = pairs(near, parts, places[0], scalars, None, False)
+    *grads, inv_late, state = pairs(late, parts, places[1], scalars, state, True)
+    whole = whole.reshape(1056, part)
+    halves = [
+        lax.psum_scatter(whole, PLANE, scatter_dimension=0, tiled=True, axis_index_groups=OUTER),
+        grads[0] + sum(move(grads[k], False, 4 - k) for k in (1, 2, 3)),
+    ]
 
     total_v = lax.psum_scatter(state.reshape(1088, n), ("z", "core"), scatter_dimension=0, tiled=True)
-    place_in = jnp.where(core == 0, x, y)
-    done = []
-    for c, h in enumerate(halves):
-        to = [jnp.concatenate([h[64 * k : 64 * k + 64], h[256:264]], axis=0) for k in range(4)]
-        if c < len(CHUNKS) - 1:
-            ring = jnp.stack([to[0], to[3], to[2], to[1], to[0], to[3], to[2]])
-            ring = lax.dynamic_slice_in_dim(ring, lax.rem(4 - place_in, 4), 4, 0)
-            done.append(jnp.sum(lax.all_to_all(ring, PLANE, 0, 0, axis_index_groups=INNER), axis=0))
-        else:
-            done.append(to[0] + sum(move(to[k], True, 4 - k) for k in (1, 2, 3)))
-    total_a = jnp.concatenate(done, axis=1)
-    inv_a = jnp.concatenate(invs, axis=1)
+    grad_v = scale * (total_v[0:128] * inv_v - video.T * (inv_v * inv_v * total_v[128:129]))
+    to = [
+        jnp.concatenate(
+            [jnp.concatenate([h[64 * k : 64 * k + 64], h[256:264]], axis=0) for h in halves], axis=1
+        )
+        for k in range(4)
+    ]
+    (kept,) = after([grad_v[:8]], [to[0]])
+    total_a = kept + sum(move(to[k], True, 4 - k) for k in (1, 2, 3))
+    inv_a = jnp.concatenate([inv_near, inv_late], axis=1)
     row_loss, inner_a = total_a[64], total_a[65:66]
     grad_a = scale * (total_a[0:64] * inv_a - audio_t * (inv_a * inv_a * inner_a))
-    grad_v = scale * (total_v[0:128] * inv_v - video.T * (inv_v * inv_v * total_v[128:129]))
     return row_loss, grad_a.T, grad_v.T
 
 

time: 188 us -> 179 us (0.952)
  starting transfers between devices: 29.8 us -> 19.7 us
  other arithmetic: 14.1 us -> 11 us
  Pallas kernels: 61.6 us -> 63.7 us
    ppermute x19 -> x12, waiting for transfers between devices: 59.5 us -> 38.9 us  [move(): return lax.ppermute(block, PLANE, perm(inner, k))]
    all_gather x1, waiting for transfers between devices: 0.01 us -> 12.7 us  [local(): whole_video = lax.all_gather(video, ('z', 'core'), axis=1, tiled=True)]
    reduce_scatter x1, waiting for transfers between devices: 0.01 us -> 7.74 us  [local(): lax.psum_scatter(state.reshape(1088, n), ('z', 'core'), scatter_dimension...]
    ppermute x19 -> x12, starting transfers between devices: 25.8 us -> 19.5 us  [move(): return lax.ppermute(block, PLANE, perm(inner, k))]
    all_to_all x1 -> x0, starting transfers between devices: 3.93 us -> none  [local(): lax.all_to_all(ring, PLANE, 0, 0, axis_index_groups=INNER)]
    add x5 -> x2, other arithmetic: 6.92 us -> 3.86 us  [the longest x1 2.32 us: local(): grads[0] + sum((move(grads[k], False, 4 - k) for k in (1, 2, 3)))]
    unnamed x19 -> x25, local copies, waits for them, and re-layouts: 1.27 us -> 3.42 us
    pallas_call x2, Pallas kernels: 51 us -> 53 us  [pairs(): pl.pallas_call(body, grid_spec=pltpu.PrefetchScalarGridSpec(num_scalar_pr...]
  transfers between devices with their start and end apart: 22 -> 16, of which waited for: 10 -> 8; matrix products, arithmetic and copies ran while one was open for 9% -> 8% of each run, Pallas kernels for 33% -> 36%
where the time goes in v2:
time: 179 us; the launch traced here: 177 us
  Pallas kernels  63.7 us (36%)
  waiting for transfers between devices  60 us (34%)
  starting transfers between devices  19.7 us (11%)
  between operations  15.4 us (9%)
  other arithmetic  11 us (6%)
  local copies, waits for them, and re-layouts  7.73 us (4%)
    pallas_call x2, Pallas kernels, pairs(): pl.pallas_call(body, grid_spec=pltpu.PrefetchScalarGridSpec(num_scalar_pr...  53 us
    ppermute x12, waiting for transfers between devices, move(): return lax.ppermute(block, PLANE, perm(inner, k))  38.9 us
    ppermute x12, starting transfers between devices, move(): return lax.ppermute(block, PLANE, perm(inner, k))  19.5 us
    all_gather x1, waiting for transfers between devices, local(): whole_video = lax.all_gather(video, ('z', 'core'), axis=1, tiled=True)  12.7 us
    pallas_call x1, Pallas kernels, prepare(): pl.pallas_call(prepare_kernel, in_specs=[pl.BlockSpec(memory_space=pltpu....  10.6 us
    reduce_scatter x1, waiting for transfers between devices, local(): lax.psum_scatter(state.reshape(1088, n), ('z', 'core'), scatter_dimension...  7.74 us
  transfers between devices with their start and end apart: 16, of which 8 were waited for; matrix products, arithmetic and copies ran while one was open for 8% of the time, Pallas kernels for 36%

profile of v2, /device:TPU:0, one launch (start us, length us, event | category | flops | bytes accessed | tf_op | source)
XLA Modules:
  0.0 177.4 jit_solution(17310620324381909104)
XLA Ops:
  7.9 1.6 collective-permute-start
  9.6 2.7 %collective-permute-start.1 = (f32[64,2048]{1,0:T(8,128)}, f32[64,2048]{1,0:T(8,128)S(1)}, u32[]{:S(2)}, u32[]{:S(2)}) collective-permute-start(f32[64,2048]{1,0:T(8,128)} %bitcast.28), channel_id=1, source_target_pairs={{0,2},{1,3},{2,0},{3,1},{4,6},{5,7},{6,4},{7,5},{8,10},{9,11},{10,... | collective-permute-start | bytes 1572872 | tf_op jit(solution)/shard_map/ppermute | solution.py:302
  12.3 1.4 collective-permute-start.2
  14.8 3.8 %collective-permute-done = f32[64,2048]{1,0:T(8,128)S(1)} collective-permute-done((f32[64,2048]{1,0:T(8,128)}, f32[64,2048]{1,0:T(8,128)S(1)}, u32[]{:S(2)}, u32[]{:S(2)}) %collective-permute-start) | collective-permute-done | bytes 524320 | tf_op jit(solution)/shard_map/ppermute | solution.py:302
  18.7 6.6 %collective-permute-done.1 = f32[64,2048]{1,0:T(8,128)S(1)} collective-permute-done((f32[64,2048]{1,0:T(8,128)}, f32[64,2048]{1,0:T(8,128)S(1)}, u32[]{:S(2)}, u32[]{:S(2)}) %collective-permute-start.1) | collective-permute-done | bytes 524320 | tf_op jit(solution)/shard_map/ppermute | solution.py:302
  26.7 1.6 collective-permute-start.3
  28.4 2.9 %collective-permute-start.4 = (f32[256,1024]{1,0:T(8,128)S(1)}, f32[256,1024]{1,0:T(8,128)S(1)}, u32[]{:S(2)}, u32[]{:S(2)}) collective-permute-start(f32[256,1024]{1,0:T(8,128)S(1)} %pad_maximum_fusion.7.refs_2_), channel_id=1, source_target_pairs={{0,8},{1,9},{2,10},{3,11},{4,12},{5,13},{6,14},{7,15},{8,0},{9,1},... | collective-permute-start | bytes 3145736 | tf_op jit(solution)/shard_map/ppermute | solution.py:302
  31.3 1.3 collective-permute-start.5
  35.8 12.7 %all-gather.5.cloned.1.call-done.whole = f32[1024,1024]{1,0:T(8,128)} async-done(((f32[1024,128]{1,0:T(8,128)}), f32[1024,1024]{1,0:T(8,128)}) %all-gather.5.cloned.1.call-update) | async-done | bytes 4194320 | tf_op jit(solution)/shard_map/all_gather | solution.py:325
  48.5 10.6 %video_parts.1 = (f32[1,1024]{1,0:T(1,128)}, f32[1024,1024]{1,0:T(8,128)}, bf16[1024,1024]{1,0:T(8,128)(2,1)}, f8e4m3fn[1024,2048]{1,0:T(32,128)(4,1)}, bf16[102...) custom-call(s32[3]{0:T(128)} %pad_add_fusion.place, f32[1024,1024]{1,0:T(8,128)} %all-gather.5.cloned.1.call-done.whole), custom_call_target="tpu_custom_call" | custom-call | bytes 16777216 | tf_op jit(solution)/shard_map/video_parts/pallas_call | solution.py:83
  60.5 27.4 %pairs_first.1 = (f32[4,264,1024]{2,1,0:T(8,128)}, f32[1,1024]{1,0:T(1,128)}, f32[1024,1024]{1,0:T(8,128)}) custom-call(s32[5]{0:T(128)} %stack.54.refs_0_, f32[2]{0:T(128)} %pad_maximum_fusion.9.refs_1_, f32[256,1024]{1,0:T(8,128)} %copy-done.5, f32[256,1024]{1,0:T(8,128)} %copy-done.9, f32[256,1024]{1,0:T(8,128)} %copy-done.10, ...), custom_call_target="tpu_custom_call" | custom-call | flops 12884901888 | bytes 25165824 | tf_op jit(solution)/shard_map/pairs_first/pallas_call | solution.py:272
  88.5 25.7 %pairs_last.1 = (f32[264,1024]{1,0:T(8,128)}, f32[264,1024]{1,0:T(8,128)}, f32[264,1024]{1,0:T(8,128)}, f32[264,1024]{1,0:T(8,128)}, f32[1,1024]{1,0:T(1,128)}, /*index=5*/f32[8,136,1024]{2,1,0:T(8,128)}) custom-call(s32[5]{0:T(128)} %stack.48.refs_0_, f32[2]{0:T(128)} %pad_maximum_fusion.9.refs_1_, ...), custom_call_target="tpu_custom_call" | custom-call | flops 12884901888 | bytes 25165824 | tf_op jit(solution)/shard_map/pairs_last/pallas_call | solution.py:272
  116.6 13.2 %collective-permute-done.6 = f32[264,1024]{1,0:T(8,128)} collective-permute-done((f32[264,1024]{1,0:T(8,128)}, f32[264,1024]{1,0:T(8,128)}, u32[]{:S(2)}, u32[]{:S(2)}) %collective-permute-start.6) | collective-permute-done | bytes 1081376 | tf_op jit(solution)/shard_map/ppermute | solution.py:302
  129.8 2.0 %collective-permute-done.7 = f32[264,1024]{1,0:T(8,128)} collective-permute-done((f32[264,1024]{1,0:T(8,128)}, f32[264,1024]{1,0:T(8,128)}, u32[]{:S(2)}, u32[]{:S(2)}) %collective-permute-start.7) | collective-permute-done | bytes 1081376 | tf_op jit(solution)/shard_map/ppermute | solution.py:302
  131.7 11.5 %collective-permute-done.8 = f32[264,1024]{1,0:T(8,128)} collective-permute-done((f32[264,1024]{1,0:T(8,128)}, f32[264,1024]{1,0:T(8,128)}, u32[]{:S(2)}, u32[]{:S(2)}) %collective-permute-start.8) | collective-permute-done | bytes 1081376 | tf_op jit(solution)/shard_map/ppermute | solution.py:302
  143.2 2.3 %add_add_fusion = f32[264,1024]{1,0:T(8,128)S(1)} fusion(f32[264,1024]{1,0:T(8,128)S(1)} %copy-done.4, f32[264,1024]{1,0:T(8,128)} %collective-permute-done.8, f32[264,1024]{1,0:T(8,128)} %collective-permute-done.6, f32[264,1024]{1,0:T(8,128)} %collective-permute-done.7), kind=kLoop, calls=%fused_computation | loop fusion | flops 811008 | bytes 5406720 | tf_op jit(solution)/shard_map/add | solution.py:339
  147.7 1.5 collective-permute-start.11
  149.3 1.3 fusion.2
  150.6 2.7 %collective-permute-start.10 = (f32[72,2048]{1,0:T(8,128)}, f32[72,2048]{1,0:T(8,128)S(1)}, u32[]{:S(2)}, u32[]{:S(2)}) collective-permute-start(f32[72,2048]{1,0:T(8,128)} %get-tuple-element.52), channel_id=1, source_target_pairs={{0,2},{1,3},{2,0},{3,1},{4,6},{5,7},{6,4},{7,5},{8,10},{9,11},{10,... | collective-permute-start | bytes 1769480 | tf_op jit(solution)/shard_map/ppermute | solution.py:302
  153.3 1.5 collective-permute-start.9
  154.8 7.7 %reduce-scatter.3.cloned.1.call-done = f32[136,1024]{1,0:T(8,128)} async-done(((f32[1088,1024]{1,0:T(8,128)}), f32[136,1024]{1,0:T(8,128)}) %reduce-scatter.3.cloned.1.call-update) | async-done | bytes 557072 | tf_op jit(solution)/shard_map/reduce_scatter | solution.py:342
  163.3 1.1 fusion.7
  166.1 1.8 collective-permute-done.9
  167.8 1.5 add_add_fusion.1
  (69 shorter events, 15.5 us)
Async XLA Ops:
  7.2 41.3 %all-gather.5.cloned.1.call-start = ((), (), s32[]{:S(2)}) async-start(), calls=%async_computation.3 | async-start | bytes 4718592 | tf_op jit(solution)/shard_map/all_gather | solution.py:325
  7.9 80.6 %all-gather.3.cloned.1.call-start = ((), (), s32[]{:S(2)}) async-start(), calls=%async_computation.2 | async-start | bytes 5242880 | tf_op jit(solution)/shard_map/all_gather | solution.py:330
  7.9 10.7 %collective-permute-start = (f32[64,2048]{1,0:T(8,128)}, f32[64,2048]{1,0:T(8,128)S(1)}, u32[]{:S(2)}, u32[]{:S(2)}) collective-permute-start(f32[64,2048]{1,0:T(8,128)} %bitcast.27), channel_id=1, source_target_pairs={{0,1},{1,2},{2,3},{3,0},{4,5},{5,6},{6,7},{7,4},{8,9},{9,10},{10,1... | collective-permute-start | bytes 1572872 | tf_op jit(solution)/shard_map/ppermute | solution.py:302
  9.6 15.7 %collective-permute-start.1 = (f32[64,2048]{1,0:T(8,128)}, f32[64,2048]{1,0:T(8,128)S(1)}, u32[]{:S(2)}, u32[]{:S(2)}) collective-permute-start(f32[64,2048]{1,0:T(8,128)} %bitcast.28), channel_id=1, source_target_pairs={{0,2},{1,3},{2,0},{3,1},{4,6},{5,7},{6,4},{7,5},{8,10},{9,11},{10,... | collective-permute-start | bytes 1572872 | tf_op jit(solution)/shard_map/ppermute | solution.py:302
  12.3 13.0 %collective-permute-start.2 = (f32[64,2048]{1,0:T(8,128)}, f32[64,2048]{1,0:T(8,128)S(1)}, u32[]{:S(2)}, u32[]{:S(2)}) collective-permute-start(f32[64,2048]{1,0:T(8,128)} %bitcast.29), channel_id=1, source_target_pairs={{0,3},{1,0},{2,1},{3,2},{4,7},{5,4},{6,5},{7,6},{8,11},{9,8},{10,9... | collective-permute-start | bytes 1572872 | tf_op jit(solution)/shard_map/ppermute | solution.py:302
  26.5 120.0 %reduce-scatter.5.cloned.1.call-start = ((), (), s32[]{:S(2)}) async-start(), calls=%async_computation.5 | async-start | bytes 5406720 | tf_op jit(solution)/shard_map/reduce_scatter | solution.py:338
  26.7 32.4 %copy-start.5 = (f32[256,1024]{1,0:T(8,128)}, f32[256,1024]{1,0:T(8,128)S(1)}, u32[]{:S(2)}) copy-start(f32[256,1024]{1,0:T(8,128)S(1)} %pad_maximum_fusion.7.refs_2_) | copy-start | bytes 3145732
  26.7 32.4 %collective-permute-start.3 = (f32[256,1024]{1,0:T(8,128)S(1)}, f32[256,1024]{1,0:T(8,128)S(1)}, u32[]{:S(2)}, u32[]{:S(2)}) collective-permute-start(f32[256,1024]{1,0:T(8,128)S(1)} %pad_maximum_fusion.7.refs_2_), channel_id=1, source_target_pairs={{0,4},{1,5},{2,6},{3,7},{4,8},{5,9},{6,10},{7,11},{8,12},{9,13},{1... | collective-permute-start | bytes 3145736 | tf_op jit(solution)/shard_map/ppermute | solution.py:302
  28.4 30.8 %collective-permute-start.4 = (f32[256,1024]{1,0:T(8,128)S(1)}, f32[256,1024]{1,0:T(8,128)S(1)}, u32[]{:S(2)}, u32[]{:S(2)}) collective-permute-start(f32[256,1024]{1,0:T(8,128)S(1)} %pad_maximum_fusion.7.refs_2_), channel_id=1, source_target_pairs={{0,8},{1,9},{2,10},{3,11},{4,12},{5,13},{6,14},{7,15},{8,0},{9,1},... | collective-permute-start | bytes 3145736 | tf_op jit(solution)/shard_map/ppermute | solution.py:302
  31.3 27.9 %collective-permute-start.5 = (f32[256,1024]{1,0:T(8,128)S(1)}, f32[256,1024]{1,0:T(8,128)}, u32[]{:S(2)}, u32[]{:S(2)}) collective-permute-start(f32[256,1024]{1,0:T(8,128)S(1)} %pad_maximum_fusion.7.refs_2_), channel_id=1, source_target_pairs={{0,12},{1,13},{2,14},{3,15},{4,0},{5,1},{6,2},{7,3},{8,4},{9,5},{1... | collective-permute-start | bytes 3145736 | tf_op jit(solution)/shard_map/ppermute | solution.py:302
  87.9 74.6 %reduce-scatter.3.cloned.1.call-start = ((), (), s32[]{:S(2)}) async-start(), calls=%async_computation.4 | async-start | bytes 5013504 | tf_op jit(solution)/shard_map/reduce_scatter | solution.py:342
  114.2 2.2 %copy-start.1 = (f32[1024,128]{1,0:T(8,128)S(1)}, f32[1024,128]{1,0:T(8,128)}, u32[]{:S(2)}) copy-start(f32[1024,128]{1,0:T(8,128)} %param.5) | copy-start | bytes 1572868
  114.2 2.4 %copy-start.8 = (f32[1,1024]{1,0:T(1,128)S(1)}, f32[1,1024]{1,0:T(1,128)}, u32[]{:S(2)}) copy-start(f32[1,1024]{1,0:T(1,128)} %get-tuple-element.31) | copy-start | bytes 12292
  114.2 29.0 %copy-start.4 = (f32[264,1024]{1,0:T(8,128)S(1)}, f32[264,1024]{1,0:T(8,128)}, u32[]{:S(2)}) copy-start(f32[264,1024]{1,0:T(8,128)} %get-tuple-element.27) | copy-start | bytes 3244036
  114.3 15.5 %collective-permute-start.6 = (f32[264,1024]{1,0:T(8,128)}, f32[264,1024]{1,0:T(8,128)}, u32[]{:S(2)}, u32[]{:S(2)}) collective-permute-start(f32[264,1024]{1,0:T(8,128)} %get-tuple-element.28), channel_id=1, source_target_pairs={{0,12},{1,13},{2,14},{3,15},{4,0},{5,1},{6,2},{7,3},{8,4},{9,5},{1... | collective-permute-start | bytes 3244040 | tf_op jit(solution)/shard_map/ppermute | solution.py:302
  114.7 17.1 %collective-permute-start.7 = (f32[264,1024]{1,0:T(8,128)}, f32[264,1024]{1,0:T(8,128)}, u32[]{:S(2)}, u32[]{:S(2)}) collective-permute-start(f32[264,1024]{1,0:T(8,128)} %get-tuple-element.29), channel_id=1, source_target_pairs={{0,8},{1,9},{2,10},{3,11},{4,12},{5,13},{6,14},{7,15},{8,0},{9,1},... | collective-permute-start | bytes 3244040 | tf_op jit(solution)/shard_map/ppermute | solution.py:302
  115.5 27.7 %collective-permute-start.8 = (f32[264,1024]{1,0:T(8,128)}, f32[264,1024]{1,0:T(8,128)}, u32[]{:S(2)}, u32[]{:S(2)}) collective-permute-start(f32[264,1024]{1,0:T(8,128)} %get-tuple-element.30), channel_id=1, source_target_pairs={{0,4},{1,5},{2,6},{3,7},{4,8},{5,9},{6,10},{7,11},{8,12},{9,13},{1... | collective-permute-start | bytes 3244040 | tf_op jit(solution)/shard_map/ppermute | solution.py:302
  146.5 2.7 %copy-start.3 = (f32[264,1024]{1,0:T(8,128)S(1)}, f32[264,1024]{1,0:T(8,128)}, u32[]{:S(2)}) copy-start(f32[264,1024]{1,0:T(8,128)} %reduce-scatter.5.cloned.1.call-done) | copy-start | bytes 3244036
  147.7 18.4 %collective-permute-start.11 = (f32[72,2048]{1,0:T(8,128)S(1)}, f32[72,2048]{1,0:T(8,128)}, u32[]{:S(2)}, u32[]{:S(2)}) collective-permute-start(f32[72,2048]{1,0:T(8,128)S(1)} %pad_maximum_fusion.8), channel_id=1, source_target_pairs={{0,1},{1,2},{2,3},{3,0},{4,5},{5,6},{6,7},{7,4},{8,9},{9,10},{10,1... | collective-permute-start | bytes 1769480 | tf_op jit(solution)/shard_map/ppermute | solution.py:302
  149.3 5.5 %copy-start.7 = (f32[1,1024]{1,0:T(1,128)S(1)}, f32[1,1024]{1,0:T(1,128)}, u32[]{:S(2)}) copy-start(f32[1,1024]{1,0:T(1,128)} %get-tuple-element.32) | copy-start | bytes 12292
  149.3 13.2 %copy-start.6 = (f32[1,1024]{1,0:T(1,128)S(1)}, f32[1,1024]{1,0:T(1,128)}, u32[]{:S(2)}) copy-start(f32[1,1024]{1,0:T(1,128)} %get-tuple-element.25) | copy-start | bytes 12292
  150.6 15.4 %collective-permute-start.10 = (f32[72,2048]{1,0:T(8,128)}, f32[72,2048]{1,0:T(8,128)S(1)}, u32[]{:S(2)}, u32[]{:S(2)}) collective-permute-start(f32[72,2048]{1,0:T(8,128)} %get-tuple-element.52), channel_id=1, source_target_pairs={{0,2},{1,3},{2,0},{3,1},{4,6},{5,7},{6,4},{7,5},{8,10},{9,11},{10,... | collective-permute-start | bytes 1769480 | tf_op jit(solution)/shard_map/ppermute | solution.py:302
  153.3 14.6 %collective-permute-start.9 = (f32[72,2048]{1,0:T(8,128)}, f32[72,2048]{1,0:T(8,128)}, u32[]{:S(2)}, u32[]{:S(2)}) collective-permute-start(f32[72,2048]{1,0:T(8,128)} %get-tuple-element.53), channel_id=1, source_target_pairs={{0,3},{1,0},{2,1},{3,2},{4,7},{5,4},{6,5},{7,6},{8,11},{9,8},{10,9... | collective-permute-start | bytes 1769480 | tf_op jit(solution)/shard_map/ppermute | solution.py:302
  166.0 4.0 %copy-start.2 = (f32[2048,64]{0,1:T(8,128)S(1)}, f32[2048,64]{0,1:T(8,128)}, u32[]{:S(2)}) copy-start(f32[2048,64]{0,1:T(8,128)} %param.4) | copy-start | bytes 1572868
  (5 other events, 6.6 us)
Sparse Core Ops, SparseCore 0:
  9.7 38.7 all-gather.4
  50.1 32.6 all-gather.2
  88.0 31.7 reduce-scatter.4
  122.1 40.3 reduce-scatter.2

commit v3 on v2

--- a/solution.py
+++ b/solution.py
@@ -103,67 +103,61 @@
     return jnp.where(power < 1e-3, power - 0.5 * power * power, jnp.log(1.0 + power))
 
 
-def pairs_kernel(first, last, refs):
+def pairs_kernel(first, refs):
     place, scalars, *refs = refs
     audio, refs = refs[:4], refs[4:]
-    unit_t_hbm, *sources = refs[:5]
-    sources.append(unit_t_hbm)
-    refs = refs[5:]
-    before = None
-    if not first:
-        before, *refs = refs
-    if last:
-        grads_a, refs = refs[:4], refs[4:]
-    else:
+    sources, refs = refs[:5], refs[5 if first else 9 :]
+    if first:
         grads_a = [refs[0].at[lax.rem(place[4] + 4 - k, 4)] for k in range(4)]
         refs = refs[1:]
-    inv_ref, *refs = refs
-    if last:
-        whole, *refs = refs
-    state, near, v_high, v_small, t_high, t_small, sems = refs
+    else:
+        grads_a, refs = refs[:4], refs[4:]
+    side_ref, unit_high, unit_small, away_high, away_small, *refs = refs
+    near, v_high, v_small, t_high, t_small, sems = refs
     step = pl.program_id(0)
     scale, bias = scalars[0], scalars[1]
     n = v_high.shape[0]
-    block = inv_ref.shape[1]
+    block = side_ref.shape[1]
     sub = block // SUBS
     offset = place[3] + step * block
     loads = [
         pltpu.make_async_copy(source, to, sems.at[k])
-        for k, (source, to) in enumerate(zip(sources, (v_high, v_small, t_high, t_small, near)))
-    ]
-    if not first:
-        loads.append(pltpu.make_async_copy(before, state, sems.at[5]))
+        for k, (source, to) in enumerate(zip(sources, (near, v_high, v_small, t_high, t_small)))
+    ]
 
     @pl.when(step == 0)
     def _():
-        for load in loads:
+        for load in (*loads[1:], loads[0]):
             load.start()
-        if first:
-            state[...] = jnp.zeros_like(state)
 
     audio_t = jnp.concatenate([r[...] for r in audio], axis=0)
     inv = lax.rsqrt(jnp.sum(audio_t * audio_t, axis=0, keepdims=True) + EPS)
-    inv_ref[...] = inv
+    side_ref[0:1, :] = inv
+    side_ref[1:8, :] = jnp.zeros((7, block), F32)
     unit_t = audio_t * inv
 
     @pl.when(step == 0)
     def _():
-        for load in loads[:2]:
+        for load in loads[1:3]:
             load.wait()
 
     def similar(k):
-        part = split(unit_t[:, k * sub : (k + 1) * sub], 0, False)
+        lanes = slice(k * sub, (k + 1) * sub)
+        part = split(unit_t[:, lanes], 0, False)
+        unit_high[:, lanes], unit_small[:, lanes] = part
         return scale * product((v_high[...], v_small[...]), part, ((1,), (0,)))
 
     def judge(k, scaled):
+        lanes = slice(k * sub, (k + 1) * sub)
         power = jnp.exp(scaled + bias)
         sig = power * inverse(1.0 + power)
         paired = (
             lax.broadcasted_iota(jnp.int32, (n, sub), 0)
             - lax.broadcasted_iota(jnp.int32, (n, sub), 1)
         ) == offset + k * sub
-        loss = jnp.sum(soft(power), axis=0, keepdims=True)
-        return paired, split(jnp.where(paired, 0.0, sig), 0, False), loss
+        away = split(jnp.where(paired, 0.0, sig), 0, False)
+        away_high[:, lanes], away_small[:, lanes] = away
+        return paired, away, jnp.sum(soft(power), axis=0, keepdims=True)
 
     def pull_rows(k, away, loss):
         lanes = slice(k * sub, (k + 1) * sub)
@@ -180,16 +174,13 @@
 
     @pl.when(step == 0)
     def _():
-        for load in loads[2:]:
+        for load in (*loads[3:], loads[0]):
             load.wait()
 
     for k in range(SUBS):
         if k > 0:
             judged.append(judge(k, scores[k]))
         pull_rows(k, judged[k][1], judged[k][2])
-    high = jnp.concatenate([j[1][0] for j in judged], axis=1)
-    small = jnp.concatenate([j[1][1][:n] for j in judged] + [j[1][1][n:] for j in judged], axis=1)
-    state[...] += product(split(unit_t, 1, True), (high, small), ((1,), (1,)))
 
     @pl.when((offset >= 0) & (offset < n))
     def _():
@@ -200,47 +191,29 @@
         )
         value = own + bias
         diag = -1.0 / (1.0 + jnp.exp(value))
+        side_ref[1:2, :] = diag
         pull = near[:, pl.ds(at, block)] * diag
         inner_own = jnp.sum(pull * unit_t, axis=0, keepdims=True)
         for k, ref in enumerate(grads_a):
             ref[0:256, :] += pull[256 * k : 256 * k + 256, :]
             ref[256:257, :] += -value
             ref[257:258, :] += inner_own
-        state[:, pl.ds(at, block)] += unit_t * diag
-
-    if last:
-
-        @pl.when(step == pl.num_programs(0) - 1)
-        def _():
-            core, y, x = place[0], place[1], place[2]
-            for half in range(n // block):
-                lanes = pl.ds(half * block, block)
-                row = jnp.sum(near[:, lanes] * state[:, lanes], axis=0, keepdims=True)
-                for owner in range(8):
-                    whole[owner, 128:129, lanes] = row
-            for owner in range(8):
-                whole[owner, 129:136, :] = jnp.zeros((7, n), F32)
-                for part in range(2):
-                    dy = lax.rem(y + 4 - owner // 2, 4)
-                    dx = lax.rem(x + 4 - 2 * (owner % 2) - part, 4)
-                    at = jnp.where(core == 0, 4 * dy + dx, 4 * dx + dy) * 64
-                    rows = pl.ds(pl.multiple_of(at, 64), 64)
-                    whole[owner, 64 * part : 64 * part + 64, :] = state[rows, :]
-
-
-def pairs(audio, video, place, scalars, before, last):
+
+
+def pairs(audio, video, place, scalars, before):
     rows = audio[0].shape[1]
     first = before is None
     n = video[1].shape[0]
     smem = pl.BlockSpec(memory_space=pltpu.SMEM)
     anywhere = pl.BlockSpec(memory_space=pl.ANY)
     shape = jax.ShapeDtypeStruct
-
-    def still(shape):
-        return pl.BlockSpec(shape, lambda i, at: (0,) * len(shape), pipeline_mode=pl.Buffered(1))
+    skip = 0 if first else rows // BLOCK
 
     def moving(height):
         return pl.BlockSpec((height, BLOCK), lambda i, at: (0, i))
+
+    def shared(height):
+        return pl.BlockSpec((height, BLOCK), lambda i, at: (0, i + skip))
 
     def turned(k):
         return pl.BlockSpec((256, BLOCK), lambda i, at: (lax.rem(at[4] + 4 - k, 4), i))
@@ -251,23 +224,27 @@
         blocks = [moving(256)] * 4
     in_specs = [smem] + blocks + [anywhere] * 5
     operands = [scalars, *(audio * (4 // len(audio))), *video]
-    parts = [pltpu.VMEM(v.shape, v.dtype) for v in (video[0], *video[1:])]
-    parts.append(pltpu.SemaphoreType.DMA((6,)))
-    if not first:
-        in_specs.append(anywhere)
-        operands.append(before)
-    if last:
-        out_specs = [moving(264)] * 4 + [moving(1), still((8, 136, n))]
-        out_shape = [shape((264, rows), F32)] * 4 + [shape((1, rows), F32), shape((8, 136, n), F32)]
-        scratch = [pltpu.VMEM((1024, n), F32)] + parts
+    if first:
+        out_specs = [pl.BlockSpec((4, 264, BLOCK), lambda i, at: (0, 0, i))]
+        out_shape = [shape((4, 264, rows), F32)]
+        aliases = {}
     else:
-        whole = pl.BlockSpec((4, 264, BLOCK), lambda i, at: (0, 0, i))
-        out_specs = [whole, moving(1), still((1024, n))]
-        out_shape = [shape((4, 264, rows), F32), shape((1, rows), F32), shape((1024, n), F32)]
-        scratch = parts
+        aliases = {1 + len(operands) + k: 5 + k for k in range(4)}
+        in_specs += [anywhere] * 4
+        operands += before
+        out_specs = [moving(264)] * 4
+        out_shape = [shape((264, rows), F32)] * 4
+    out_specs += [moving(8), shared(1024), shared(2048), shared(n), shared(2 * n)]
+    out_shape += [
+        shape((8, rows), F32),
+        shape((1024, 2 * rows), BF16),
+        shape((2048, 2 * rows), F8),
+        shape((n, 2 * rows), BF16),
+        shape((2 * n, 2 * rows), F8),
+    ]
 
     def body(*refs):
-        pairs_kernel(first, last, refs)
+        pairs_kernel(first, refs)
 
     return pl.pallas_call(
         body,
@@ -276,15 +253,107 @@
             grid=(rows // BLOCK,),
             in_specs=in_specs,
             out_specs=out_specs,
-            scratch_shapes=scratch,
+            scratch_shapes=[pltpu.VMEM(v.shape, v.dtype) for v in video] + [pltpu.SemaphoreType.DMA((5,))],
         ),
         out_shape=out_shape,
+        input_output_aliases=aliases,
         compiler_params=pltpu.CompilerParams(vmem_limit_bytes=VMEM),
         cost_estimate=pl.CostEstimate(
-            flops=6 * 2 * rows * n * 1024, bytes_accessed=24 * MIB, transcendentals=3 * rows * n
+            flops=4 * 2 * rows * n * 1024, bytes_accessed=32 * MIB, transcendentals=3 * rows * n
         ),
-        name="pairs_last" if last else "pairs_first",
+        name="pairs_first" if first else "pairs_last",
     )(place, *operands)
+
+
+def video_kernel(place, unit_high, unit_small, away_high, away_small, near_side, late_side, *refs):
+    early, (late, unit_t_hbm, whole), refs = refs[:4], refs[4:7], refs[7:]
+    state, unit_t, rows_ref, sems = refs
+    step = pl.program_id(0)
+    n = away_high.shape[0]
+    block = near_side.shape[1]
+    half = pl.num_programs(0) // 2
+    offset = place[3] + step * block
+    crossing = (offset >= 0) & (offset < n)
+    load = pltpu.make_async_copy(unit_t_hbm, unit_t, sems.at[4])
+    from_early, from_late = [], []
+    for k in range(4):
+        to = rows_ref.at[pl.ds(256 * k, 256), :]
+        lanes = pl.ds(pl.multiple_of(lax.rem(step, half) * block, block), block)
+        turn = pl.multiple_of(lax.rem(place[4] + 4 - k, 4) * 256, 256)
+        from_early.append(pltpu.make_async_copy(early[k].at[:, lanes], to, sems.at[k]))
+        from_late.append(pltpu.make_async_copy(late.at[pl.ds(turn, 256), lanes], to, sems.at[k]))
+
+    @pl.when(step == 0)
+    def _():
+        load.start()
+        state[...] = jnp.zeros_like(state)
+
+    @pl.when(crossing & (step < half))
+    def _():
+        for copy in from_early:
+            copy.start()
+
+    @pl.when(crossing & (step >= half))
+    def _():
+        for copy in from_late:
+            copy.start()
+
+    dims = ((1,), (1,))
+    small = dot(unit_small[1024:], away_small[:n], dims) + dot(unit_small[:1024], away_small[n:], dims)
+    state[...] += dot(unit_high[...], away_high[...], dims) + DOWN * small
+
+    @pl.when(crossing)
+    def _():
+        for copy in from_early:
+            copy.wait()
+        side = jnp.where(step < half, near_side[0:2, :], late_side[0:2, :])
+        at = pl.multiple_of(offset, block)
+        state[:, pl.ds(at, block)] += rows_ref[...] * (side[0:1, :] * side[1:2, :])
+
+    @pl.when(step == pl.num_programs(0) - 1)
+    def _():
+        load.wait()
+        core, y, x = place[0], place[1], place[2]
+        row = jnp.sum(unit_t[...] * state[...], axis=0, keepdims=True)
+        for owner in range(8):
+            whole[owner, 128:129, :] = row
+            whole[owner, 129:136, :] = jnp.zeros((7, n), F32)
+            for part in range(2):
+                dy = lax.rem(y + 4 - owner // 2, 4)
+                dx = lax.rem(x + 4 - 2 * (owner % 2) - part, 4)
+                at = jnp.where(core == 0, 4 * dy + dx, 4 * dx + dy) * 64
+                piece = pl.ds(pl.multiple_of(at, 64), 64)
+                whole[owner, 64 * part : 64 * part + 64, :] = state[piece, :]
+
+
+def video_sums(shared, sides, early, late, unit_t, place):
+    n = shared[2].shape[0]
+    count = shared[0].shape[1] // BLOCK
+    anywhere = pl.BlockSpec(memory_space=pl.ANY)
+    moving = lambda height: pl.BlockSpec((height, BLOCK), lambda i, at: (0, i))
+    first = pl.BlockSpec((8, BLOCK), lambda i, at: (0, jnp.minimum(i, count // 2 - 1)))
+    second = pl.BlockSpec((8, BLOCK), lambda i, at: (0, jnp.maximum(i - count // 2, 0)))
+    return pl.pallas_call(
+        video_kernel,
+        grid_spec=pltpu.PrefetchScalarGridSpec(
+            num_scalar_prefetch=1,
+            grid=(count,),
+            in_specs=[moving(s.shape[0]) for s in shared] + [first, second] + [anywhere] * 6,
+            out_specs=pl.BlockSpec((8, 136, n), lambda i, at: (0, 0, 0), pipeline_mode=pl.Buffered(1)),
+            scratch_shapes=[
+                pltpu.VMEM((1024, n), F32),
+                pltpu.VMEM((1024, n), F32),
+                pltpu.VMEM((1024, BLOCK), F32),
+                pltpu.SemaphoreType.DMA((5,)),
+            ],
+        ),
+        out_shape=jax.ShapeDtypeStruct((8, 136, n), F32),
+        compiler_params=pltpu.CompilerParams(vmem_limit_bytes=VMEM),
+        cost_estimate=pl.CostEstimate(
+            flops=2 * 2 * BLOCK * count * n * 1024, bytes_accessed=32 * MIB, transcendentals=0
+        ),
+        name="video_sums",
+    )(place, *shared, *sides, *early, late, unit_t)
 
 
 def perm(inner, k):
@@ -331,13 +400,16 @@
     inv_v, *parts = prepare(whole_video, jnp.stack([core, y, x]).astype(jnp.int32))
     outer = jnp.where(core == 0, y, x)
     places = [jnp.stack([core, y, x, base + c * part, outer]).astype(jnp.int32) for c in (0, 1)]
-    whole, inv_near, state = pairs(near, parts, places[0], scalars, None, False)
-    *grads, inv_late, state = pairs(late, parts, places[1], scalars, state, True)
+    whole, side_near, *shared = pairs(near, parts, places[0], scalars, None)
+    *grads, side_late = (outs := pairs(late, parts, places[1], scalars, shared))[:5]
+    state = video_sums(outs[5:], [side_near, side_late], near, late[0], parts[0], places[0])
     whole = whole.reshape(1056, part)
+    came = [move(grads[k], False, 4 - k) for k in (1, 2, 3)]
     halves = [
         lax.psum_scatter(whole, PLANE, scatter_dimension=0, tiled=True, axis_index_groups=OUTER),
-        grads[0] + sum(move(grads[k], False, 4 - k) for k in (1, 2, 3)),
-    ]
+        grads[0] + came[0] + came[1] + came[2],
+    ]
+    (state,) = after([came[0][256:264] + came[2][256:264]], [state])
 
     total_v = lax.psum_scatter(state.reshape(1088, n), ("z", "core"), scatter_dimension=0, tiled=True)
     grad_v = scale * (total_v[0:128] * inv_v - video.T * (inv_v * inv_v * total_v[128:129]))
@@ -349,7 +421,7 @@
     ]
     (kept,) = after([grad_v[:8]], [to[0]])
     total_a = kept + sum(move(to[k], True, 4 - k) for k in (1, 2, 3))
-    inv_a = jnp.concatenate([inv_near, inv_late], axis=1)
+    inv_a = jnp.concatenate([side_near[0:1], side_late[0:1]], axis=1)
     row_loss, inner_a = total_a[64], total_a[65:66]
     grad_a = scale * (total_a[0:64] * inv_a - audio_t * (inv_a * inv_a * inner_a))
     return row_loss, grad_a.T, grad_v.T

time: 179 us -> 181 us (1.011)
  waiting for transfers between devices: 60 us -> 49.5 us
  Pallas kernels: 63.7 us -> 72.7 us
  local copies, waits for them, and re-layouts: 7.73 us -> 10.3 us
    pallas_call x0 -> x1, Pallas kernels: none -> 18.4 us  [video_sums(): pl.pallas_call(video_kernel, grid_spec=pltpu.PrefetchScalarGridSpec(num_s...]
    ppermute x12, waiting for transfers between devices: 38.9 us -> 26.8 us  [move(): return lax.ppermute(block, PLANE, perm(inner, k))]
    pallas_call x2, Pallas kernels: 53 us -> 43.5 us  [pairs(): pl.pallas_call(body, grid_spec=pltpu.PrefetchScalarGridSpec(num_scalar_pr...]
    unnamed x25 -> x20, local copies, waits for them, and re-layouts: 3.42 us -> 4.6 us
  transfers between devices with their start and end apart: 16 -> 16, of which waited for: 8 -> 6; matrix products, arithmetic and copies ran while one was open for 8% -> 8% of each run, Pallas kernels for 36% -> 40%
where the time goes in v3:
time: 181 us; the launch traced here: 180 us
  Pallas kernels  72.7 us (40%)
  waiting for transfers between devices  49.5 us (27%)
  starting transfers between devices  21.3 us (12%)
  between operations  15.3 us (8%)
  other arithmetic  10.8 us (6%)
  local copies, waits for them, and re-layouts  10.3 us (6%)
    pallas_call x2, Pallas kernels, pairs(): pl.pallas_call(body, grid_spec=pltpu.PrefetchScalarGridSpec(num_scalar_pr...  43.5 us
    ppermute x12, waiting for transfers between devices, move(): return lax.ppermute(block, PLANE, perm(inner, k))  26.8 us
    ppermute x12, starting transfers between devices, move(): return lax.ppermute(block, PLANE, perm(inner, k))  20.9 us
    pallas_call x1, Pallas kernels, video_sums(): pl.pallas_call(video_kernel, grid_spec=pltpu.PrefetchScalarGridSpec(num_s...  18.4 us
    all_gather x1, waiting for transfers between devices, local(): whole_video = lax.all_gather(video, ('z', 'core'), axis=1, tiled=True)  12.8 us
    pallas_call x1, Pallas kernels, prepare(): pl.pallas_call(prepare_kernel, in_specs=[pl.BlockSpec(memory_space=pltpu....  10.8 us
    reduce_scatter x1, waiting for transfers between devices, local(): lax.psum_scatter(state.reshape(1088, n), ('z', 'core'), scatter_dimension...  9.23 us
    unnamed x20, local copies, waits for them, and re-layouts  4.6 us
  transfers between devices with their start and end apart: 16, of which 6 were waited for; matrix products, arithmetic and copies ran while one was open for 8% of the time, Pallas kernels for 40%

profile of v3, /device:TPU:0, one launch (start us, length us, event | category | flops | bytes accessed | tf_op | source)
XLA Modules:
  0.0 180.1 jit_solution(11190180806073296162)
XLA Ops:
  7.9 1.6 collective-permute-start
  9.6 2.7 %collective-permute-start.1 = (f32[64,2048]{1,0:T(8,128)}, f32[64,2048]{1,0:T(8,128)S(1)}, u32[]{:S(2)}, u32[]{:S(2)}) collective-permute-start(f32[64,2048]{1,0:T(8,128)} %bitcast.28), channel_id=1, source_target_pairs={{0,2},{1,3},{2,0},{3,1},{4,6},{5,7},{6,4},{7,5},{8,10},{9,11},{10,... | collective-permute-start | bytes 1572872 | tf_op jit(solution)/shard_map/ppermute | solution.py:371
  12.3 1.4 collective-permute-start.2
  14.8 3.8 %collective-permute-done = f32[64,2048]{1,0:T(8,128)S(1)} collective-permute-done((f32[64,2048]{1,0:T(8,128)}, f32[64,2048]{1,0:T(8,128)S(1)}, u32[]{:S(2)}, u32[]{:S(2)}) %collective-permute-start) | collective-permute-done | bytes 524320 | tf_op jit(solution)/shard_map/ppermute | solution.py:371
  18.7 6.6 %collective-permute-done.1 = f32[64,2048]{1,0:T(8,128)S(1)} collective-permute-done((f32[64,2048]{1,0:T(8,128)}, f32[64,2048]{1,0:T(8,128)S(1)}, u32[]{:S(2)}, u32[]{:S(2)}) %collective-permute-start.1) | collective-permute-done | bytes 524320 | tf_op jit(solution)/shard_map/ppermute | solution.py:371
  26.7 1.6 collective-permute-start.3
  28.3 2.9 %collective-permute-start.4 = (f32[256,1024]{1,0:T(8,128)S(1)}, f32[256,1024]{1,0:T(8,128)S(1)}, u32[]{:S(2)}, u32[]{:S(2)}) collective-permute-start(f32[256,1024]{1,0:T(8,128)S(1)} %pad_maximum_fusion.7.refs_2_.refs_0_), channel_id=1, source_target_pairs={{0,8},{1,9},{2,10},{3,11},{4,12},{5,13},{6,14},{7,15},{8,0},{9,1},... | collective-permute-start | bytes 3145736 | tf_op jit(solution)/shard_map/ppermute | solution.py:371
  31.2 1.3 collective-permute-start.5
  35.7 12.8 %all-gather.5.cloned.1.call-done.whole = f32[1024,1024]{1,0:T(8,128)} async-done(((f32[1024,128]{1,0:T(8,128)}), f32[1024,1024]{1,0:T(8,128)}) %all-gather.5.cloned.1.call-update) | async-done | bytes 4194320 | tf_op jit(solution)/shard_map/all_gather | solution.py:394
  48.5 10.8 %video_parts.1 = (f32[1,1024]{1,0:T(1,128)}, f32[1024,1024]{1,0:T(8,128)}, bf16[1024,1024]{1,0:T(8,128)(2,1)}, f8e4m3fn[1024,2048]{1,0:T(32,128)(4,1)}, bf16[102...) custom-call(s32[3]{0:T(128)} %pad_add_fusion.place, f32[1024,1024]{1,0:T(8,128)} %all-gather.5.cloned.1.call-done.whole), custom_call_target="tpu_custom_call" | custom-call | bytes 16777216 | tf_op jit(solution)/shard_map/video_parts/pallas_call | solution.py:83
  60.6 22.8 %pairs_first.1 = (f32[4,264,1024]{2,1,0:T(8,128)}, f32[8,1024]{1,0:T(8,128)}, bf16[1024,2048]{1,0:T(8,128)(2,1)}, f8e4m3fn[2048,2048]{1,0:T(32,128)(4,1)}, bf16[...) custom-call(s32[5]{0:T(128)} %stack.54.refs_0_.place, f32[2]{0:T(128)} %pad_maximum_fusion.10.refs_1_, ...), custom_call_target="tpu_custom_call" | custom-call | flops 8589934592 | bytes 33554432 | tf_op jit(solution)/shard_map/pairs_first/pallas_call | solution.py:249
  84.3 20.7 %pairs_last.1 = (f32[264,1024]{1,0:T(8,128)}, f32[264,1024]{1,0:T(8,128)}, f32[264,1024]{1,0:T(8,128)}, f32[264,1024]{1,0:T(8,128)}, f32[8,1024]{1,0:T(8,128)}, ...) custom-call(s32[5]{0:T(128)} %stack.48.refs_0_, ...), custom_call_target="tpu_custom_call", output_to_operand_aliasing={{5}: (11, {}), {6}: (12, {}), {7}: (13, {}), {8}: (14, {})} | custom-call | flops 8589934592 | bytes 33554432 | tf_op jit(solution)/shard_map/pairs_last/pallas_call | solution.py:249
  105.0 1.2 collective-permute-start.6
  107.1 18.4 %video_sums.1.refs_1_ = f32[8,136,1024]{2,1,0:T(8,128)} custom-call(s32[5]{0:T(128)} %stack.54.refs_0_.place, bf16[1024,2048]{1,0:T(8,128)(2,1)} %get-tuple-element.35.unit_high, f8e4m3fn[2048,2048]{1,0:T(32,128)(4,1)} %get-tuple-element.36.unit_small, bf16[1024,2048]{1,0:T(8,128)(2,1)} %get-tuple-element.37.away_high, ...), custom_call_target="tpu_custom_call" | custom-call | flops 8589934592 | bytes 33554432 | tf_op jit(solution)/shard_map/video_sums/pallas_call | solution.py:336
  127.3 1.2 copy-done.8
  128.5 1.5 collective-permute-start.8
  130.0 15.2 %collective-permute-done.8 = f32[264,1024]{1,0:T(8,128)S(1)} collective-permute-done((f32[264,1024]{1,0:T(8,128)S(1)}, f32[264,1024]{1,0:T(8,128)S(1)}, u32[]{:S(2)}, u32[]{:S(2)}) %collective-permute-start.8) | collective-permute-done | bytes 1081376 | tf_op jit(solution)/shard_map/ppermute | solution.py:371
  145.2 1.7 add_add_fusion
  149.0 1.5 collective-permute-start.11
  150.7 1.3 fusion.2
  152.0 2.7 %collective-permute-start.10 = (f32[72,2048]{1,0:T(8,128)}, f32[72,2048]{1,0:T(8,128)S(1)}, u32[]{:S(2)}, u32[]{:S(2)}) collective-permute-start(f32[72,2048]{1,0:T(8,128)} %get-tuple-element.64), channel_id=1, source_target_pairs={{0,2},{1,3},{2,0},{3,1},{4,6},{5,7},{6,4},{7,5},{8,10},{9,11},{10,... | collective-permute-start | bytes 1769480 | tf_op jit(solution)/shard_map/ppermute | solution.py:371
  154.7 1.5 collective-permute-start.9
  157.9 9.2 %reduce-scatter.3.cloned.1.call-done = f32[136,1024]{1,0:T(8,128)} async-done(((f32[1088,1024]{1,0:T(8,128)}), f32[136,1024]{1,0:T(8,128)}) %reduce-scatter.3.cloned.1.call-update) | async-done | bytes 557072 | tf_op jit(solution)/shard_map/reduce_scatter | solution.py:414
  170.6 1.4 add_add_fusion.1
  (68 shorter events, 18.7 us)
Async XLA Ops:
  7.2 41.3 %all-gather.5.cloned.1.call-start = ((), (), s32[]{:S(2)}) async-start(), calls=%async_computation.3 | async-start | bytes 4718592 | tf_op jit(solution)/shard_map/all_gather | solution.py:394
  7.9 76.4 %all-gather.3.cloned.1.call-start = ((), (), s32[]{:S(2)}) async-start(), calls=%async_computation.2 | async-start | bytes 5242880 | tf_op jit(solution)/shard_map/all_gather | solution.py:399
  7.9 10.7 %collective-permute-start = (f32[64,2048]{1,0:T(8,128)}, f32[64,2048]{1,0:T(8,128)S(1)}, u32[]{:S(2)}, u32[]{:S(2)}) collective-permute-start(f32[64,2048]{1,0:T(8,128)} %bitcast.27), channel_id=1, source_target_pairs={{0,1},{1,2},{2,3},{3,0},{4,5},{5,6},{6,7},{7,4},{8,9},{9,10},{10,1... | collective-permute-start | bytes 1572872 | tf_op jit(solution)/shard_map/ppermute | solution.py:371
  9.6 15.7 %collective-permute-start.1 = (f32[64,2048]{1,0:T(8,128)}, f32[64,2048]{1,0:T(8,128)S(1)}, u32[]{:S(2)}, u32[]{:S(2)}) collective-permute-start(f32[64,2048]{1,0:T(8,128)} %bitcast.28), channel_id=1, source_target_pairs={{0,2},{1,3},{2,0},{3,1},{4,6},{5,7},{6,4},{7,5},{8,10},{9,11},{10,... | collective-permute-start | bytes 1572872 | tf_op jit(solution)/shard_map/ppermute | solution.py:371
  12.3 13.0 %collective-permute-start.2 = (f32[64,2048]{1,0:T(8,128)}, f32[64,2048]{1,0:T(8,128)S(1)}, u32[]{:S(2)}, u32[]{:S(2)}) collective-permute-start(f32[64,2048]{1,0:T(8,128)} %bitcast.29), channel_id=1, source_target_pairs={{0,3},{1,0},{2,1},{3,2},{4,7},{5,4},{6,5},{7,6},{8,11},{9,8},{10,9... | collective-permute-start | bytes 1572872 | tf_op jit(solution)/shard_map/ppermute | solution.py:371
  26.5 121.4 %reduce-scatter.5.cloned.1.call-start = ((), (), s32[]{:S(2)}) async-start(), calls=%async_computation.5 | async-start | bytes 5406720 | tf_op jit(solution)/shard_map/reduce_scatter | solution.py:409
  26.7 32.6 %copy-start.1 = (f32[256,1024]{1,0:T(8,128)}, f32[256,1024]{1,0:T(8,128)S(1)}, u32[]{:S(2)}) copy-start(f32[256,1024]{1,0:T(8,128)S(1)} %pad_maximum_fusion.7.refs_2_.refs_0_) | copy-start | bytes 3145732
  26.7 32.6 %collective-permute-start.3 = (f32[256,1024]{1,0:T(8,128)S(1)}, f32[256,1024]{1,0:T(8,128)S(1)}, u32[]{:S(2)}, u32[]{:S(2)}) collective-permute-start(f32[256,1024]{1,0:T(8,128)S(1)} %pad_maximum_fusion.7.refs_2_.refs_0_), channel_id=1, source_target_pairs={{0,4},{1,5},{2,6},{3,7},{4,8},{5,9},{6,10},{7,11},{8,12},{9,13},{1... | collective-permute-start | bytes 3145736 | tf_op jit(solution)/shard_map/ppermute | solution.py:371
  28.3 31.0 %collective-permute-start.4 = (f32[256,1024]{1,0:T(8,128)S(1)}, f32[256,1024]{1,0:T(8,128)S(1)}, u32[]{:S(2)}, u32[]{:S(2)}) collective-permute-start(f32[256,1024]{1,0:T(8,128)S(1)} %pad_maximum_fusion.7.refs_2_.refs_0_), channel_id=1, source_target_pairs={{0,8},{1,9},{2,10},{3,11},{4,12},{5,13},{6,14},{7,15},{8,0},{9,1},... | collective-permute-start | bytes 3145736 | tf_op jit(solution)/shard_map/ppermute | solution.py:371
  31.2 28.1 %collective-permute-start.5 = (f32[256,1024]{1,0:T(8,128)S(1)}, f32[256,1024]{1,0:T(8,128)}, u32[]{:S(2)}, u32[]{:S(2)}) collective-permute-start(f32[256,1024]{1,0:T(8,128)S(1)} %pad_maximum_fusion.7.refs_2_.refs_0_), channel_id=1, source_target_pairs={{0,12},{1,13},{2,14},{3,15},{4,0},{5,1},{6,2},{7,3},{8,4},{9,5},{1... | collective-permute-start | bytes 3145736 | tf_op jit(solution)/shard_map/ppermute | solution.py:371
  59.3 1.3 copy-start.6
  83.4 83.7 %reduce-scatter.3.cloned.1.call-start = ((), (), s32[]{:S(2)}) async-start(), calls=%async_computation.4 | async-start | bytes 5013504 | tf_op jit(solution)/shard_map/reduce_scatter | solution.py:414
  105.0 20.5 %collective-permute-start.6 = (f32[264,1024]{1,0:T(8,128)}, f32[264,1024]{1,0:T(8,128)S(1)}, u32[]{:S(2)}, u32[]{:S(2)}) collective-permute-start(f32[264,1024]{1,0:T(8,128)} %get-tuple-element.33), channel_id=1, source_target_pairs={{0,12},{1,13},{2,14},{3,15},{4,0},{5,1},{6,2},{7,3},{8,4},{9,5},{1... | collective-permute-start | bytes 3244040 | tf_op jit(solution)/shard_map/ppermute | solution.py:371
  106.2 20.5 %collective-permute-start.7 = (f32[264,1024]{1,0:T(8,128)}, f32[264,1024]{1,0:T(8,128)S(1)}, u32[]{:S(2)}, u32[]{:S(2)}) collective-permute-start(f32[264,1024]{1,0:T(8,128)} %get-tuple-element.34), channel_id=1, source_target_pairs={{0,4},{1,5},{2,6},{3,7},{4,8},{5,9},{6,10},{7,11},{8,12},{9,13},{1... | collective-permute-start | bytes 3244040 | tf_op jit(solution)/shard_map/ppermute | solution.py:371
  128.5 16.7 %collective-permute-start.8 = (f32[264,1024]{1,0:T(8,128)S(1)}, f32[264,1024]{1,0:T(8,128)S(1)}, u32[]{:S(2)}, u32[]{:S(2)}) collective-permute-start(f32[264,1024]{1,0:T(8,128)S(1)} %copy-done.8), channel_id=1, source_target_pairs={{0,8},{1,9},{2,10},{3,11},{4,12},{5,13},{6,14},{7,15},{8,0},{9,1},... | collective-permute-start | bytes 3244040 | tf_op jit(solution)/shard_map/ppermute | solution.py:371
  147.9 2.7 %copy-start.4 = (f32[264,1024]{1,0:T(8,128)S(1)}, f32[264,1024]{1,0:T(8,128)}, u32[]{:S(2)}) copy-start(f32[264,1024]{1,0:T(8,128)} %reduce-scatter.5.cloned.1.call-done) | copy-start | bytes 3244036
  149.0 1.6 slice-start
  149.0 1.6 slice-start.1
  149.0 21.6 %collective-permute-start.11 = (f32[72,2048]{1,0:T(8,128)S(1)}, f32[72,2048]{1,0:T(8,128)S(1)}, u32[]{:S(2)}, u32[]{:S(2)}) collective-permute-start(f32[72,2048]{1,0:T(8,128)S(1)} %pad_maximum_fusion.8), channel_id=1, source_target_pairs={{0,1},{1,2},{2,3},{3,0},{4,5},{5,6},{6,7},{7,4},{8,9},{9,10},{10,1... | collective-permute-start | bytes 1769480 | tf_op jit(solution)/shard_map/ppermute | solution.py:371
  150.7 5.5 %copy-start.2 = (f32[1024,128]{1,0:T(8,128)S(1)}, f32[1024,128]{1,0:T(8,128)}, u32[]{:S(2)}) copy-start(f32[1024,128]{1,0:T(8,128)} %param.5) | copy-start | bytes 1572868
  150.7 16.4 %copy-start.7 = (f32[1,1024]{1,0:T(1,128)S(1)}, f32[1,1024]{1,0:T(1,128)}, u32[]{:S(2)}) copy-start(f32[1,1024]{1,0:T(1,128)} %get-tuple-element.41) | copy-start | bytes 12292
  152.0 18.6 %collective-permute-start.10 = (f32[72,2048]{1,0:T(8,128)}, f32[72,2048]{1,0:T(8,128)S(1)}, u32[]{:S(2)}, u32[]{:S(2)}) collective-permute-start(f32[72,2048]{1,0:T(8,128)} %get-tuple-element.64), channel_id=1, source_target_pairs={{0,2},{1,3},{2,0},{3,1},{4,6},{5,7},{6,4},{7,5},{8,10},{9,11},{10,... | collective-permute-start | bytes 1769480 | tf_op jit(solution)/shard_map/ppermute | solution.py:371
  154.7 15.9 %collective-permute-start.9 = (f32[72,2048]{1,0:T(8,128)}, f32[72,2048]{1,0:T(8,128)}, u32[]{:S(2)}, u32[]{:S(2)}) collective-permute-start(f32[72,2048]{1,0:T(8,128)} %get-tuple-element.65), channel_id=1, source_target_pairs={{0,3},{1,0},{2,1},{3,2},{4,7},{5,4},{6,5},{7,6},{8,11},{9,8},{10,9... | collective-permute-start | bytes 1769480 | tf_op jit(solution)/shard_map/ppermute | solution.py:371
  170.6 2.1 %copy-start.3 = (f32[2048,64]{0,1:T(8,128)S(1)}, f32[2048,64]{0,1:T(8,128)}, u32[]{:S(2)}) copy-start(f32[2048,64]{0,1:T(8,128)} %param.4) | copy-start | bytes 1572868
  (3 other events, 3.2 us)
Sparse Core Ops, SparseCore 0:
  9.7 38.7 all-gather.4
  50.1 32.6 all-gather.2
  85.2 35.1 reduce-scatter.4
  127.5 39.6 reduce-scatter.2

commit v4 on v3

--- a/solution.py
+++ b/solution.py
@@ -405,22 +405,19 @@
     state = video_sums(outs[5:], [side_near, side_late], near, late[0], parts[0], places[0])
     whole = whole.reshape(1056, part)
     came = [move(grads[k], False, 4 - k) for k in (1, 2, 3)]
-    halves = [
-        lax.psum_scatter(whole, PLANE, scatter_dimension=0, tiled=True, axis_index_groups=OUTER),
-        grads[0] + came[0] + came[1] + came[2],
-    ]
+
+    def inward(h):
+        to = [jnp.concatenate([h[64 * k : 64 * k + 64], h[256:264]], axis=0) for k in range(4)]
+        return [to[0]] + [move(to[k], True, 4 - k) for k in (1, 2, 3)]
+
+    early = inward(lax.psum_scatter(whole, PLANE, scatter_dimension=0, tiled=True, axis_index_groups=OUTER))
+    (kept,) = after([early[1][64:72] + early[2][64:72] + early[3][64:72]], [grads[0]])
+    late = inward(kept + came[0] + came[1] + came[2])
     (state,) = after([came[0][256:264] + came[2][256:264]], [state])
 
     total_v = lax.psum_scatter(state.reshape(1088, n), ("z", "core"), scatter_dimension=0, tiled=True)
     grad_v = scale * (total_v[0:128] * inv_v - video.T * (inv_v * inv_v * total_v[128:129]))
-    to = [
-        jnp.concatenate(
-            [jnp.concatenate([h[64 * k : 64 * k + 64], h[256:264]], axis=0) for h in halves], axis=1
-        )
-        for k in range(4)
-    ]
-    (kept,) = after([grad_v[:8]], [to[0]])
-    total_a = kept + sum(move(to[k], True, 4 - k) for k in (1, 2, 3))
+    total_a = jnp.concatenate([sum(early[1:], early[0]), sum(late[1:], late[0])], axis=1)
     inv_a = jnp.concatenate([side_near[0:1], side_late[0:1]], axis=1)
     row_loss, inner_a = total_a[64], total_a[65:66]
     grad_a = scale * (total_a[0:64] * inv_a - audio_t * (inv_a * inv_a * inner_a))

time: 181 us -> 179 us (0.989)
  waiting for transfers between devices: 49.5 us -> 45.2 us
  starting transfers between devices: 21.3 us -> 23.7 us
    reduce_scatter x1, waiting for transfers between devices: 9.23 us -> 0.01 us  [local(): lax.psum_scatter(state.reshape(1088, n), ('z', 'core'), scatter_dimension...]
    ppermute x12 -> x15, waiting for transfers between devices: 26.8 us -> 32.6 us  [move(): return lax.ppermute(block, PLANE, perm(inner, k))]
    ppermute x12 -> x15, starting transfers between devices: 20.9 us -> 23.3 us  [move(): return lax.ppermute(block, PLANE, perm(inner, k))]
    unnamed x20 -> x26, local copies, waits for them, and re-layouts: 4.6 us -> 2.28 us
  transfers between devices with their start and end apart: 16 -> 19, of which waited for: 6 -> 12; matrix products, arithmetic and copies ran while one was open for 8% -> 9% of each run, Pallas kernels for 40% -> 41%
where the time goes in v4:
time: 179 us; the launch traced here: 178 us
  Pallas kernels  72.7 us (41%)
  waiting for transfers between devices  45.2 us (25%)
  starting transfers between devices  23.7 us (13%)
  between operations  15.3 us (9%)
  other arithmetic  10.8 us (6%)
  local copies, waits for them, and re-layouts  9.84 us (5%)
    pallas_call x2, Pallas kernels, pairs(): pl.pallas_call(body, grid_spec=pltpu.PrefetchScalarGridSpec(num_scalar_pr...  43.7 us
    ppermute x15, waiting for transfers between devices, move(): return lax.ppermute(block, PLANE, perm(inner, k))  32.6 us
    ppermute x15, starting transfers between devices, move(): return lax.ppermute(block, PLANE, perm(inner, k))  23.3 us
    pallas_call x1, Pallas kernels, video_sums(): pl.pallas_call(video_kernel, grid_spec=pltpu.PrefetchScalarGridSpec(num_s...  18.4 us
    all_gather x1, waiting for transfers between devices, local(): whole_video = lax.all_gather(video, ('z', 'core'), axis=1, tiled=True)  11.9 us
    pallas_call x1, Pallas kernels, prepare(): pl.pallas_call(prepare_kernel, in_specs=[pl.BlockSpec(memory_space=pltpu....  10.6 us
  transfers between devices with their start and end apart: 19, of which 12 were waited for; matrix products, arithmetic and copies ran while one was open for 9% of the time, Pallas kernels for 41%

profile of v4, /device:TPU:0, one launch (start us, length us, event | category | flops | bytes accessed | tf_op | source)
XLA Modules:
  0.0 177.6 jit_solution(6740941527853222638)
XLA Ops:
  7.9 2.9 %collective-permute-start.2 = (f32[64,2048]{1,0:T(8,128)}, f32[64,2048]{1,0:T(8,128)S(1)}, u32[]{:S(2)}, u32[]{:S(2)}) collective-permute-start(f32[64,2048]{1,0:T(8,128)} %bitcast.27), channel_id=1, source_target_pairs={{0,3},{1,0},{2,1},{3,2},{4,7},{5,4},{6,5},{7,6},{8,11},{9,8},{10,9... | collective-permute-start | bytes 1572872 | tf_op jit(solution)/shard_map/ppermute | solution.py:371
  13.6 9.9 %collective-permute-done.2 = f32[64,2048]{1,0:T(8,128)S(1)} collective-permute-done((f32[64,2048]{1,0:T(8,128)}, f32[64,2048]{1,0:T(8,128)S(1)}, u32[]{:S(2)}, u32[]{:S(2)}) %collective-permute-start.2) | collective-permute-done | bytes 524320 | tf_op jit(solution)/shard_map/ppermute | solution.py:371
  23.6 3.8 %collective-permute-done = f32[64,2048]{1,0:T(8,128)S(1)} collective-permute-done((f32[64,2048]{1,0:T(8,128)}, f32[64,2048]{1,0:T(8,128)S(1)}, u32[]{:S(2)}, u32[]{:S(2)}) %collective-permute-start) | collective-permute-done | bytes 524320 | tf_op jit(solution)/shard_map/ppermute | solution.py:371
  28.7 3.1 %collective-permute-start.5 = (f32[256,1024]{1,0:T(8,128)S(1)}, f32[256,1024]{1,0:T(8,128)S(1)}, u32[]{:S(2)}, u32[]{:S(2)}) collective-permute-start(f32[256,1024]{1,0:T(8,128)S(1)} %pad_maximum_fusion.refs_2_.refs_0_), channel_id=1, source_target_pairs={{0,12},{1,13},{2,14},{3,15},{4,0},{5,1},{6,2},{7,3},{8,4},{9,5},{1... | collective-permute-start | bytes 3145736 | tf_op jit(solution)/shard_map/ppermute | solution.py:371
  36.5 11.9 %all-gather.3.cloned.1.call-done.whole = f32[1024,1024]{1,0:T(8,128)} async-done(((f32[1024,128]{1,0:T(8,128)}), f32[1024,1024]{1,0:T(8,128)}) %all-gather.3.cloned.1.call-update) | async-done | bytes 4194320 | tf_op jit(solution)/shard_map/all_gather | solution.py:394
  48.5 10.6 %video_parts.1 = (f32[1,1024]{1,0:T(1,128)}, f32[1024,1024]{1,0:T(8,128)}, bf16[1024,1024]{1,0:T(8,128)(2,1)}, f8e4m3fn[1024,2048]{1,0:T(32,128)(4,1)}, bf16[102...) custom-call(s32[3]{0:T(128)} %pad_add_fusion.place, f32[1024,1024]{1,0:T(8,128)} %all-gather.3.cloned.1.call-done.whole), custom_call_target="tpu_custom_call" | custom-call | bytes 16777216 | tf_op jit(solution)/shard_map/video_parts/pallas_call | solution.py:83
  60.4 22.9 %pairs_first.1 = (f32[4,264,1024]{2,1,0:T(8,128)}, f32[8,1024]{1,0:T(8,128)}, bf16[1024,2048]{1,0:T(8,128)(2,1)}, f8e4m3fn[2048,2048]{1,0:T(32,128)(4,1)}, bf16[...) custom-call(s32[5]{0:T(128)} %stack.48.refs_0_.place, f32[2]{0:T(128)} %pad_maximum_fusion.11.refs_1_, ...), custom_call_target="tpu_custom_call" | custom-call | flops 8589934592 | bytes 33554432 | tf_op jit(solution)/shard_map/pairs_first/pallas_call | solution.py:249
  84.2 20.8 %pairs_last.1 = (f32[264,1024]{1,0:T(8,128)}, f32[264,1024]{1,0:T(8,128)}, f32[264,1024]{1,0:T(8,128)}, f32[264,1024]{1,0:T(8,128)}, f32[8,1024]{1,0:T(8,128)}, ...) custom-call(s32[5]{0:T(128)} %stack.54.refs_0_, ...), custom_call_target="tpu_custom_call", output_to_operand_aliasing={{5}: (11, {}), {6}: (12, {}), {7}: (13, {}), {8}: (14, {})} | custom-call | flops 8589934592 | bytes 33554432 | tf_op jit(solution)/shard_map/pairs_last/pallas_call | solution.py:249
  105.0 1.2 collective-permute-start.9
  107.1 18.4 %video_sums.1.refs_1_ = f32[8,136,1024]{2,1,0:T(8,128)} custom-call(s32[5]{0:T(128)} %stack.48.refs_0_.place, bf16[1024,2048]{1,0:T(8,128)(2,1)} %get-tuple-element.40.unit_high, f8e4m3fn[2048,2048]{1,0:T(32,128)(4,1)} %get-tuple-element.41.unit_small, bf16[1024,2048]{1,0:T(8,128)(2,1)} %get-tuple-element.42.away_high, ...), custom_call_target="tpu_custom_call" | custom-call | flops 8589934592 | bytes 33554432 | tf_op jit(solution)/shard_map/video_sums/pallas_call | solution.py:336
  125.5 1.2 collective-permute-done.11
  127.4 1.6 collective-permute-start.10
  129.9 1.5 collective-permute-start.8
  133.4 2.1 %collective-permute-start.6 = (f32[72,1024]{1,0:T(8,128)S(1)}, f32[72,1024]{1,0:T(8,128)S(1)}, u32[]{:S(2)}, u32[]{:S(2)}) collective-permute-start(f32[72,1024]{1,0:T(8,128)S(1)} %get-tuple-element.66), channel_id=1, source_target_pairs={{0,3},{1,0},{2,1},{3,2},{4,7},{5,4},{6,5},{7,6},{8,11},{9,8},{10,9... | collective-permute-start | bytes 884744 | tf_op jit(solution)/shard_map/ppermute | solution.py:371
  135.5 1.8 collective-permute-start.7
  137.3 4.8 %collective-permute-done.8 = f32[72,1024]{1,0:T(8,128)S(1)} collective-permute-done((f32[72,1024]{1,0:T(8,128)S(1)}, f32[72,1024]{1,0:T(8,128)S(1)}, u32[]{:S(2)}, u32[]{:S(2)}) %collective-permute-start.8) | collective-permute-done | bytes 294944 | tf_op jit(solution)/shard_map/ppermute | solution.py:371
  142.0 1.6 collective-permute-done.6
  143.7 4.7 %collective-permute-done.7 = f32[72,1024]{1,0:T(8,128)S(1)} collective-permute-done((f32[72,1024]{1,0:T(8,128)S(1)}, f32[72,1024]{1,0:T(8,128)S(1)}, u32[]{:S(2)}, u32[]{:S(2)}) %collective-permute-start.7) | collective-permute-done | bytes 294944 | tf_op jit(solution)/shard_map/ppermute | solution.py:371
  149.1 1.5 collective-permute-done.10
  150.6 1.7 add_add_fusion
  153.1 1.6 collective-permute-start.14
  155.5 1.7 collective-permute-start.12
  157.2 1.8 collective-permute-start.13
  162.4 3.1 %collective-permute-done.13 = f32[72,1024]{1,0:T(8,128)} collective-permute-done((f32[72,1024]{1,0:T(8,128)S(1)}, f32[72,1024]{1,0:T(8,128)}, u32[]{:S(2)}, u32[]{:S(2)}) %collective-permute-start.13) | collective-permute-done | bytes 294944 | tf_op jit(solution)/shard_map/ppermute | solution.py:371
  (79 shorter events, 26.2 us)
Async XLA Ops:
  7.2 41.3 %all-gather.3.cloned.1.call-start = ((), (), s32[]{:S(2)}) async-start(), calls=%async_computation.2 | async-start | bytes 4718592 | tf_op jit(solution)/shard_map/all_gather | solution.py:394
  7.9 76.3 %all-gather.5.cloned.1.call-start = ((), (), s32[]{:S(2)}) async-start(), calls=%async_computation.4 | async-start | bytes 5242880 | tf_op jit(solution)/shard_map/all_gather | solution.py:399
  7.9 15.5 %collective-permute-start.2 = (f32[64,2048]{1,0:T(8,128)}, f32[64,2048]{1,0:T(8,128)S(1)}, u32[]{:S(2)}, u32[]{:S(2)}) collective-permute-start(f32[64,2048]{1,0:T(8,128)} %bitcast.27), channel_id=1, source_target_pairs={{0,3},{1,0},{2,1},{3,2},{4,7},{5,4},{6,5},{7,6},{8,11},{9,8},{10,9... | collective-permute-start | bytes 1572872 | tf_op jit(solution)/shard_map/ppermute | solution.py:371
  10.9 12.7 %collective-permute-start.1 = (f32[64,2048]{1,0:T(8,128)}, f32[64,2048]{1,0:T(8,128)S(1)}, u32[]{:S(2)}, u32[]{:S(2)}) collective-permute-start(f32[64,2048]{1,0:T(8,128)} %bitcast.28), channel_id=1, source_target_pairs={{0,2},{1,3},{2,0},{3,1},{4,6},{5,7},{6,4},{7,5},{8,10},{9,11},{10,... | collective-permute-start | bytes 1572872 | tf_op jit(solution)/shard_map/ppermute | solution.py:371
  11.7 15.7 %collective-permute-start = (f32[64,2048]{1,0:T(8,128)}, f32[64,2048]{1,0:T(8,128)S(1)}, u32[]{:S(2)}, u32[]{:S(2)}) collective-permute-start(f32[64,2048]{1,0:T(8,128)} %bitcast.29), channel_id=1, source_target_pairs={{0,1},{1,2},{2,3},{3,0},{4,5},{5,6},{6,7},{7,4},{8,9},{9,10},{10,1... | collective-permute-start | bytes 1572872 | tf_op jit(solution)/shard_map/ppermute | solution.py:371
  28.5 100.4 %reduce-scatter.3.cloned.1.call-start = ((), (), s32[]{:S(2)}) async-start(), calls=%async_computation.3 | async-start | bytes 5406720 | tf_op jit(solution)/shard_map/reduce_scatter | solution.py:413
  28.7 30.4 %copy-start = (f32[256,1024]{1,0:T(8,128)}, f32[256,1024]{1,0:T(8,128)S(1)}, u32[]{:S(2)}) copy-start(f32[256,1024]{1,0:T(8,128)S(1)} %pad_maximum_fusion.refs_2_.refs_0_) | copy-start | bytes 3145732
  28.7 30.4 %collective-permute-start.5 = (f32[256,1024]{1,0:T(8,128)S(1)}, f32[256,1024]{1,0:T(8,128)S(1)}, u32[]{:S(2)}, u32[]{:S(2)}) collective-permute-start(f32[256,1024]{1,0:T(8,128)S(1)} %pad_maximum_fusion.refs_2_.refs_0_), channel_id=1, source_target_pairs={{0,12},{1,13},{2,14},{3,15},{4,0},{5,1},{6,2},{7,3},{8,4},{9,5},{1... | collective-permute-start | bytes 3145736 | tf_op jit(solution)/shard_map/ppermute | solution.py:371
  31.8 27.3 %collective-permute-start.4 = (f32[256,1024]{1,0:T(8,128)S(1)}, f32[256,1024]{1,0:T(8,128)S(1)}, u32[]{:S(2)}, u32[]{:S(2)}) collective-permute-start(f32[256,1024]{1,0:T(8,128)S(1)} %pad_maximum_fusion.refs_2_.refs_0_), channel_id=1, source_target_pairs={{0,8},{1,9},{2,10},{3,11},{4,12},{5,13},{6,14},{7,15},{8,0},{9,1},... | collective-permute-start | bytes 3145736 | tf_op jit(solution)/shard_map/ppermute | solution.py:371
  32.4 27.0 %collective-permute-start.3 = (f32[256,1024]{1,0:T(8,128)S(1)}, f32[256,1024]{1,0:T(8,128)}, u32[]{:S(2)}, u32[]{:S(2)}) collective-permute-start(f32[256,1024]{1,0:T(8,128)S(1)} %pad_maximum_fusion.refs_2_.refs_0_), channel_id=1, source_target_pairs={{0,4},{1,5},{2,6},{3,7},{4,8},{5,9},{6,10},{7,11},{8,12},{9,13},{1... | collective-permute-start | bytes 3145736 | tf_op jit(solution)/shard_map/ppermute | solution.py:371
  83.3 84.8 %reduce-scatter.5.cloned.1.call-start = ((), (), s32[]{:S(2)}) async-start(), calls=%async_computation.5 | async-start | bytes 5013504 | tf_op jit(solution)/shard_map/reduce_scatter | solution.py:418
  105.0 20.5 %collective-permute-start.9 = (f32[264,1024]{1,0:T(8,128)}, f32[264,1024]{1,0:T(8,128)S(1)}, u32[]{:S(2)}, u32[]{:S(2)}) collective-permute-start(f32[264,1024]{1,0:T(8,128)} %get-tuple-element.35), channel_id=1, source_target_pairs={{0,12},{1,13},{2,14},{3,15},{4,0},{5,1},{6,2},{7,3},{8,4},{9,5},{1... | collective-permute-start | bytes 3244040 | tf_op jit(solution)/shard_map/ppermute | solution.py:371
  106.1 20.6 %collective-permute-start.11 = (f32[264,1024]{1,0:T(8,128)}, f32[264,1024]{1,0:T(8,128)S(1)}, u32[]{:S(2)}, u32[]{:S(2)}) collective-permute-start(f32[264,1024]{1,0:T(8,128)} %get-tuple-element.37), channel_id=1, source_target_pairs={{0,4},{1,5},{2,6},{3,7},{4,8},{5,9},{6,10},{7,11},{8,12},{9,13},{1... | collective-permute-start | bytes 3244040 | tf_op jit(solution)/shard_map/ppermute | solution.py:371
  127.4 23.3 %collective-permute-start.10 = (f32[264,1024]{1,0:T(8,128)}, f32[264,1024]{1,0:T(8,128)S(1)}, u32[]{:S(2)}, u32[]{:S(2)}) collective-permute-start(f32[264,1024]{1,0:T(8,128)} %get-tuple-element.36), channel_id=1, source_target_pairs={{0,8},{1,9},{2,10},{3,11},{4,12},{5,13},{6,14},{7,15},{8,0},{9,1},... | collective-permute-start | bytes 3244040 | tf_op jit(solution)/shard_map/ppermute | solution.py:371
  129.9 12.1 %collective-permute-start.8 = (f32[72,1024]{1,0:T(8,128)S(1)}, f32[72,1024]{1,0:T(8,128)S(1)}, u32[]{:S(2)}, u32[]{:S(2)}) collective-permute-start(f32[72,1024]{1,0:T(8,128)S(1)} %concatenate.56), channel_id=1, source_target_pairs={{0,1},{1,2},{2,3},{3,0},{4,5},{5,6},{6,7},{7,4},{8,9},{9,10},{10,1... | collective-permute-start | bytes 884744 | tf_op jit(solution)/shard_map/ppermute | solution.py:371
  133.4 10.3 %collective-permute-start.6 = (f32[72,1024]{1,0:T(8,128)S(1)}, f32[72,1024]{1,0:T(8,128)S(1)}, u32[]{:S(2)}, u32[]{:S(2)}) collective-permute-start(f32[72,1024]{1,0:T(8,128)S(1)} %get-tuple-element.66), channel_id=1, source_target_pairs={{0,3},{1,0},{2,1},{3,2},{4,7},{5,4},{6,5},{7,6},{8,11},{9,8},{10,9... | collective-permute-start | bytes 884744 | tf_op jit(solution)/shard_map/ppermute | solution.py:371
  135.5 12.8 %collective-permute-start.7 = (f32[72,1024]{1,0:T(8,128)S(1)}, f32[72,1024]{1,0:T(8,128)S(1)}, u32[]{:S(2)}, u32[]{:S(2)}) collective-permute-start(f32[72,1024]{1,0:T(8,128)S(1)} %get-tuple-element.67), channel_id=1, source_target_pairs={{0,2},{1,3},{2,0},{3,1},{4,6},{5,7},{6,4},{7,5},{8,10},{9,11},{10,... | collective-permute-start | bytes 884744 | tf_op jit(solution)/shard_map/ppermute | solution.py:371
  142.0 6.3 %copy-start.5 = (f32[72,1024]{1,0:T(8,128)}, f32[72,1024]{1,0:T(8,128)S(1)}, u32[]{:S(2)}) copy-start(f32[72,1024]{1,0:T(8,128)S(1)} %collective-permute-done.8) | copy-start | bytes 884740
  153.1 8.2 %collective-permute-start.14 = (f32[72,1024]{1,0:T(8,128)}, f32[72,1024]{1,0:T(8,128)}, u32[]{:S(2)}, u32[]{:S(2)}) collective-permute-start(f32[72,1024]{1,0:T(8,128)} %concatenate.57), channel_id=1, source_target_pairs={{0,1},{1,2},{2,3},{3,0},{4,5},{5,6},{6,7},{7,4},{8,9},{9,10},{10,1... | collective-permute-start | bytes 884744 | tf_op jit(solution)/shard_map/ppermute | solution.py:371
  154.7 6.0 %copy-start.6 = (f32[72,1024]{1,0:T(8,128)S(1)}, f32[72,1024]{1,0:T(8,128)}, u32[]{:S(2)}) copy-start(f32[72,1024]{1,0:T(8,128)} %copy-done.5) | copy-start | bytes 884740
  154.7 6.0 %copy-start.8 = (f32[72,1024]{1,0:T(8,128)S(1)}, f32[72,1024]{1,0:T(8,128)}, u32[]{:S(2)}) copy-start(f32[72,1024]{1,0:T(8,128)} %copy-done.7) | copy-start | bytes 884740
  155.5 6.9 %collective-permute-start.12 = (f32[72,1024]{1,0:T(8,128)}, f32[72,1024]{1,0:T(8,128)S(1)}, u32[]{:S(2)}, u32[]{:S(2)}) collective-permute-start(f32[72,1024]{1,0:T(8,128)} %get-tuple-element.64), channel_id=1, source_target_pairs={{0,3},{1,0},{2,1},{3,2},{4,7},{5,4},{6,5},{7,6},{8,11},{9,8},{10,9... | collective-permute-start | bytes 884744 | tf_op jit(solution)/shard_map/ppermute | solution.py:371
  157.2 8.4 %collective-permute-start.13 = (f32[72,1024]{1,0:T(8,128)S(1)}, f32[72,1024]{1,0:T(8,128)}, u32[]{:S(2)}, u32[]{:S(2)}) collective-permute-start(f32[72,1024]{1,0:T(8,128)S(1)} %get-tuple-element.65), channel_id=1, source_target_pairs={{0,2},{1,3},{2,0},{3,1},{4,6},{5,7},{6,4},{7,5},{8,10},{9,11},{10,... | collective-permute-start | bytes 884744 | tf_op jit(solution)/shard_map/ppermute | solution.py:371
  160.7 6.5 %copy-start.2 = (f32[2048,64]{0,1:T(8,128)S(1)}, f32[2048,64]{0,1:T(8,128)}, u32[]{:S(2)}) copy-start(f32[2048,64]{0,1:T(8,128)} %param.4) | copy-start | bytes 1572868
  (7 other events, 21.7 us)
Sparse Core Ops, SparseCore 0:
  9.7 38.7 all-gather.2
  50.1 32.6 all-gather.4
  85.2 35.1 reduce-scatter.2
  127.5 39.7 reduce-scatter.4

commit v5 on v2

--- a/solution.py
+++ b/solution.py
@@ -38,33 +38,44 @@
     return dot(a[0], b[0], dims) + DOWN * dot(a[1], b[1], dims)
 
 
-def prepare_kernel(place, whole, inv_ref, unit_t_out, v_high_out, v_small_out, t_high_out, t_small_out, *scratch):
-    flipped, unit_t_ref, v_high, v_small, t_high, t_small, sems = scratch
+def prepare_kernel(place, video, inv_ref, unit_t_out, v_high_out, v_small_out, t_high_out, t_small_out, *scratch):
+    whole, unit_t_ref, v_high, v_small, t_high, t_small, in_sems, sems, quarter_sems = scratch
     core, y, x = place[0], place[1], place[2]
     n = whole.shape[0]
-    outs = (unit_t_out, t_high_out, t_small_out, v_high_out, v_small_out)
+    quarter = n // 4
+    columns = [pl.ds(256 * row, 256) for row in range(4)]
+    loads = [
+        pltpu.make_async_copy(video.at[:, c], whole.at[:, c], in_sems.at[row]) for row, c in enumerate(columns)
+    ]
+    outs = (unit_t_out, t_high_out, t_small_out)
     copies = [
         pltpu.make_async_copy(ref, out, sems.at[k])
-        for k, (ref, out) in enumerate(zip((unit_t_ref, t_high, t_small, v_high, v_small), outs))
-    ]
-    v_t = whole[...].T
-    inv = lax.rsqrt(jnp.sum(v_t * v_t, axis=0, keepdims=True) + EPS)
+        for k, (ref, out) in enumerate(zip((unit_t_ref, t_high, t_small), outs))
+    ]
+    for load in loads:
+        load.start()
+    v_t = []
+    for row, c in enumerate(columns):
+        loads[row].wait()
+        v_t.append(whole[:, c].T)
+    inv = lax.rsqrt(sum(jnp.sum(v * v, axis=0, keepdims=True) for v in v_t) + EPS)
     inv_ref[...] = inv
-    flipped[...] = (v_t * inv).reshape(16, 64, n)
-    for outer in range(4):
-        for inner in range(4):
-            row = lax.rem(y + 4 - jnp.where(core == 0, outer, inner), 4)
-            column = lax.rem(x + 4 - jnp.where(core == 0, inner, outer), 4)
-            at = 64 * (4 * outer + inner)
-            unit_t_ref[at : at + 64, :] = flipped[4 * row + column]
+    for row in range(4):
+        for column in range(4):
+            dy, dx = lax.rem(y + 4 - row, 4), lax.rem(x + 4 - column, 4)
+            at = jnp.where(core == 0, 4 * dy + dx, 4 * dx + dy) * 64
+            piece = v_t[row][64 * column : 64 * column + 64, :]
+            unit_t_ref[pl.ds(pl.multiple_of(at, 64), 64), :] = piece * inv
     copies[0].start()
-    unit_t = unit_t_ref[...]
-    t_high[...], t_small[...] = split(unit_t, 1, True)
+    t_high[...], t_small[...] = split(unit_t_ref[...], 1, True)
     copies[1].start()
     copies[2].start()
-    v_high[...], v_small[...] = split(unit_t.T, 1, True)
-    copies[3].start()
-    copies[4].start()
+    for k in range(4):
+        rows = pl.ds(quarter * k, quarter)
+        v_high[rows, :], v_small[rows, :] = split(unit_t_ref[:, rows].T, 1, True)
+        for j, (ref, out) in enumerate(((v_high, v_high_out), (v_small, v_small_out))):
+            copies.append(pltpu.make_async_copy(ref.at[rows, :], out.at[rows, :], quarter_sems.at[2 * k + j]))
+            copies[-1].start()
     for copy in copies:
         copy.wait()
 
@@ -82,12 +93,12 @@
     ]
     return pl.pallas_call(
         prepare_kernel,
-        in_specs=[pl.BlockSpec(memory_space=pltpu.SMEM), whole],
+        in_specs=[pl.BlockSpec(memory_space=pltpu.SMEM), pl.BlockSpec(memory_space=pl.ANY)],
         out_specs=[whole] + [pl.BlockSpec(memory_space=pl.ANY)] * 5,
         out_shape=[shape((1, n), F32)] + parts,
-        scratch_shapes=[pltpu.VMEM((16, 64, n), F32)]
+        scratch_shapes=[pltpu.VMEM((n, 1024), F32)]
         + [pltpu.VMEM(p.shape, p.dtype) for p in parts]
-        + [pltpu.SemaphoreType.DMA((5,))],
+        + [pltpu.SemaphoreType.DMA((4,)), pltpu.SemaphoreType.DMA((3,)), pltpu.SemaphoreType.DMA((8,))],
         compiler_params=pltpu.CompilerParams(vmem_limit_bytes=VMEM),
         cost_estimate=pl.CostEstimate(flops=0, bytes_accessed=16 * MIB, transcendentals=0),
         name="video_parts",

time: 179 us -> 177 us (0.989)
  transfers between devices with their start and end apart: 16 -> 16, of which waited for: 8 -> 8; matrix products, arithmetic and copies ran while one was open for 8% -> 8% of each run, Pallas kernels for 36% -> 35%
where the time goes in v5:
time: 177 us; the launch traced here: 176 us
  Pallas kernels  62.3 us (35%)
  waiting for transfers between devices  60 us (34%)
  starting transfers between devices  19.6 us (11%)
  between operations  15.4 us (9%)
  other arithmetic  11 us (6%)
  local copies, waits for them, and re-layouts  7.73 us (4%)
    pallas_call x2, Pallas kernels, pairs(): pl.pallas_call(body, grid_spec=pltpu.PrefetchScalarGridSpec(num_scalar_pr...  53.4 us
    ppermute x12, waiting for transfers between devices, move(): return lax.ppermute(block, PLANE, perm(inner, k))  38.9 us
    ppermute x12, starting transfers between devices, move(): return lax.ppermute(block, PLANE, perm(inner, k))  19.5 us
    all_gather x1, waiting for transfers between devices, local(): whole_video = lax.all_gather(video, ('z', 'core'), axis=1, tiled=True)  12.7 us
    pallas_call x1, Pallas kernels, prepare(): pl.pallas_call(prepare_kernel, in_specs=[pl.BlockSpec(memory_space=pltpu....  8.95 us
    reduce_scatter x1, waiting for transfers between devices, local(): lax.psum_scatter(state.reshape(1088, n), ('z', 'core'), scatter_dimension...  7.74 us
  transfers between devices with their start and end apart: 16, of which 8 were waited for; matrix products, arithmetic and copies ran while one was open for 8% of the time, Pallas kernels for 35%

profile of v5, /device:TPU:0, one launch (start us, length us, event | category | flops | bytes accessed | tf_op | source)
XLA Modules:
  0.0 176.0 jit_solution(5956088241267042344)
XLA Ops:
  7.9 1.6 collective-permute-start
  9.6 2.7 %collective-permute-start.1 = (f32[64,2048]{1,0:T(8,128)}, f32[64,2048]{1,0:T(8,128)S(1)}, u32[]{:S(2)}, u32[]{:S(2)}) collective-permute-start(f32[64,2048]{1,0:T(8,128)} %bitcast.28), channel_id=1, source_target_pairs={{0,2},{1,3},{2,0},{3,1},{4,6},{5,7},{6,4},{7,5},{8,10},{9,11},{10,... | collective-permute-start | bytes 1572872 | tf_op jit(solution)/shard_map/ppermute | solution.py:313
  12.3 1.4 collective-permute-start.2
  14.8 3.8 %collective-permute-done = f32[64,2048]{1,0:T(8,128)S(1)} collective-permute-done((f32[64,2048]{1,0:T(8,128)}, f32[64,2048]{1,0:T(8,128)S(1)}, u32[]{:S(2)}, u32[]{:S(2)}) %collective-permute-start) | collective-permute-done | bytes 524320 | tf_op jit(solution)/shard_map/ppermute | solution.py:313
  18.7 6.6 %collective-permute-done.1 = f32[64,2048]{1,0:T(8,128)S(1)} collective-permute-done((f32[64,2048]{1,0:T(8,128)}, f32[64,2048]{1,0:T(8,128)S(1)}, u32[]{:S(2)}, u32[]{:S(2)}) %collective-permute-start.1) | collective-permute-done | bytes 524320 | tf_op jit(solution)/shard_map/ppermute | solution.py:313
  26.7 1.6 collective-permute-start.3
  28.4 2.9 %collective-permute-start.4 = (f32[256,1024]{1,0:T(8,128)S(1)}, f32[256,1024]{1,0:T(8,128)S(1)}, u32[]{:S(2)}, u32[]{:S(2)}) collective-permute-start(f32[256,1024]{1,0:T(8,128)S(1)} %pad_maximum_fusion.7.refs_2_), channel_id=1, source_target_pairs={{0,8},{1,9},{2,10},{3,11},{4,12},{5,13},{6,14},{7,15},{8,0},{9,1},... | collective-permute-start | bytes 3145736 | tf_op jit(solution)/shard_map/ppermute | solution.py:313
  31.3 1.3 collective-permute-start.5
  35.8 12.7 %all-gather.5.cloned.1.call-done.video = f32[1024,1024]{1,0:T(8,128)} async-done(((f32[1024,128]{1,0:T(8,128)}), f32[1024,1024]{1,0:T(8,128)}) %all-gather.5.cloned.1.call-update) | async-done | bytes 4194320 | tf_op jit(solution)/shard_map/all_gather | solution.py:336
  48.5 8.9 %video_parts.1 = (f32[1,1024]{1,0:T(1,128)}, f32[1024,1024]{1,0:T(8,128)}, bf16[1024,1024]{1,0:T(8,128)(2,1)}, f8e4m3fn[1024,2048]{1,0:T(32,128)(4,1)}, bf16[102...) custom-call(s32[3]{0:T(128)} %pad_add_fusion.place, f32[1024,1024]{1,0:T(8,128)} %all-gather.5.cloned.1.call-done.video), custom_call_target="tpu_custom_call" | custom-call | bytes 16777216 | tf_op jit(solution)/shard_map/video_parts/pallas_call | solution.py:94
  58.8 27.7 %pairs_first.1 = (f32[4,264,1024]{2,1,0:T(8,128)}, f32[1,1024]{1,0:T(1,128)}, f32[1024,1024]{1,0:T(8,128)}) custom-call(s32[5]{0:T(128)} %stack.54.refs_0_, f32[2]{0:T(128)} %pad_maximum_fusion.9.refs_1_, f32[256,1024]{1,0:T(8,128)} %copy-done.5, f32[256,1024]{1,0:T(8,128)} %copy-done.9, f32[256,1024]{1,0:T(8,128)} %copy-done.10, ...), custom_call_target="tpu_custom_call" | custom-call | flops 12884901888 | bytes 25165824 | tf_op jit(solution)/shard_map/pairs_first/pallas_call | solution.py:283
  87.2 25.7 %pairs_last.1 = (f32[264,1024]{1,0:T(8,128)}, f32[264,1024]{1,0:T(8,128)}, f32[264,1024]{1,0:T(8,128)}, f32[264,1024]{1,0:T(8,128)}, f32[1,1024]{1,0:T(1,128)}, /*index=5*/f32[8,136,1024]{2,1,0:T(8,128)}) custom-call(s32[5]{0:T(128)} %stack.48.refs_0_, f32[2]{0:T(128)} %pad_maximum_fusion.9.refs_1_, ...), custom_call_target="tpu_custom_call" | custom-call | flops 12884901888 | bytes 25165824 | tf_op jit(solution)/shard_map/pairs_last/pallas_call | solution.py:283
  115.2 13.2 %collective-permute-done.6 = f32[264,1024]{1,0:T(8,128)} collective-permute-done((f32[264,1024]{1,0:T(8,128)}, f32[264,1024]{1,0:T(8,128)}, u32[]{:S(2)}, u32[]{:S(2)}) %collective-permute-start.6) | collective-permute-done | bytes 1081376 | tf_op jit(solution)/shard_map/ppermute | solution.py:313
  128.4 1.9 %collective-permute-done.7 = f32[264,1024]{1,0:T(8,128)} collective-permute-done((f32[264,1024]{1,0:T(8,128)}, f32[264,1024]{1,0:T(8,128)}, u32[]{:S(2)}, u32[]{:S(2)}) %collective-permute-start.7) | collective-permute-done | bytes 1081376 | tf_op jit(solution)/shard_map/ppermute | solution.py:313
  130.4 11.5 %collective-permute-done.8 = f32[264,1024]{1,0:T(8,128)} collective-permute-done((f32[264,1024]{1,0:T(8,128)}, f32[264,1024]{1,0:T(8,128)}, u32[]{:S(2)}, u32[]{:S(2)}) %collective-permute-start.8) | collective-permute-done | bytes 1081376 | tf_op jit(solution)/shard_map/ppermute | solution.py:313
  141.9 2.3 %add_add_fusion = f32[264,1024]{1,0:T(8,128)S(1)} fusion(f32[264,1024]{1,0:T(8,128)S(1)} %copy-done.4, f32[264,1024]{1,0:T(8,128)} %collective-permute-done.8, f32[264,1024]{1,0:T(8,128)} %collective-permute-done.6, f32[264,1024]{1,0:T(8,128)} %collective-permute-done.7), kind=kLoop, calls=%fused_computation | loop fusion | flops 811008 | bytes 5406720 | tf_op jit(solution)/shard_map/add | solution.py:350
  146.3 1.5 collective-permute-start.11
  148.0 1.3 fusion.2
  149.2 2.7 %collective-permute-start.10 = (f32[72,2048]{1,0:T(8,128)}, f32[72,2048]{1,0:T(8,128)S(1)}, u32[]{:S(2)}, u32[]{:S(2)}) collective-permute-start(f32[72,2048]{1,0:T(8,128)} %get-tuple-element.52), channel_id=1, source_target_pairs={{0,2},{1,3},{2,0},{3,1},{4,6},{5,7},{6,4},{7,5},{8,10},{9,11},{10,... | collective-permute-start | bytes 1769480 | tf_op jit(solution)/shard_map/ppermute | solution.py:313
  151.9 1.5 collective-permute-start.9
  153.4 7.7 %reduce-scatter.3.cloned.1.call-done = f32[136,1024]{1,0:T(8,128)} async-done(((f32[1088,1024]{1,0:T(8,128)}), f32[136,1024]{1,0:T(8,128)}) %reduce-scatter.3.cloned.1.call-update) | async-done | bytes 557072 | tf_op jit(solution)/shard_map/reduce_scatter | solution.py:353
  161.9 1.1 fusion.7
  164.7 1.8 %collective-permute-done.9 = f32[72,2048]{1,0:T(8,128)} collective-permute-done((f32[72,2048]{1,0:T(8,128)}, f32[72,2048]{1,0:T(8,128)}, u32[]{:S(2)}, u32[]{:S(2)}) %collective-permute-start.9) | collective-permute-done | bytes 589856 | tf_op jit(solution)/shard_map/ppermute | solution.py:313
  166.5 1.5 add_add_fusion.1
  (69 shorter events, 15.5 us)
Async XLA Ops:
  7.2 41.3 %all-gather.5.cloned.1.call-start = ((), (), s32[]{:S(2)}) async-start(), calls=%async_computation.3 | async-start | bytes 4718592 | tf_op jit(solution)/shard_map/all_gather | solution.py:336
  7.9 79.3 %all-gather.3.cloned.1.call-start = ((), (), s32[]{:S(2)}) async-start(), calls=%async_computation.2 | async-start | bytes 5242880 | tf_op jit(solution)/shard_map/all_gather | solution.py:341
  7.9 10.7 %collective-permute-start = (f32[64,2048]{1,0:T(8,128)}, f32[64,2048]{1,0:T(8,128)S(1)}, u32[]{:S(2)}, u32[]{:S(2)}) collective-permute-start(f32[64,2048]{1,0:T(8,128)} %bitcast.27), channel_id=1, source_target_pairs={{0,1},{1,2},{2,3},{3,0},{4,5},{5,6},{6,7},{7,4},{8,9},{9,10},{10,1... | collective-permute-start | bytes 1572872 | tf_op jit(solution)/shard_map/ppermute | solution.py:313
  9.6 15.7 %collective-permute-start.1 = (f32[64,2048]{1,0:T(8,128)}, f32[64,2048]{1,0:T(8,128)S(1)}, u32[]{:S(2)}, u32[]{:S(2)}) collective-permute-start(f32[64,2048]{1,0:T(8,128)} %bitcast.28), channel_id=1, source_target_pairs={{0,2},{1,3},{2,0},{3,1},{4,6},{5,7},{6,4},{7,5},{8,10},{9,11},{10,... | collective-permute-start | bytes 1572872 | tf_op jit(solution)/shard_map/ppermute | solution.py:313
  12.3 13.0 %collective-permute-start.2 = (f32[64,2048]{1,0:T(8,128)}, f32[64,2048]{1,0:T(8,128)S(1)}, u32[]{:S(2)}, u32[]{:S(2)}) collective-permute-start(f32[64,2048]{1,0:T(8,128)} %bitcast.29), channel_id=1, source_target_pairs={{0,3},{1,0},{2,1},{3,2},{4,7},{5,4},{6,5},{7,6},{8,11},{9,8},{10,9... | collective-permute-start | bytes 1572872 | tf_op jit(solution)/shard_map/ppermute | solution.py:313
  26.5 118.6 %reduce-scatter.5.cloned.1.call-start = ((), (), s32[]{:S(2)}) async-start(), calls=%async_computation.5 | async-start | bytes 5406720 | tf_op jit(solution)/shard_map/reduce_scatter | solution.py:349
  26.7 30.7 %copy-start.5 = (f32[256,1024]{1,0:T(8,128)}, f32[256,1024]{1,0:T(8,128)S(1)}, u32[]{:S(2)}) copy-start(f32[256,1024]{1,0:T(8,128)S(1)} %pad_maximum_fusion.7.refs_2_) | copy-start | bytes 3145732
  26.7 30.7 %collective-permute-start.3 = (f32[256,1024]{1,0:T(8,128)S(1)}, f32[256,1024]{1,0:T(8,128)S(1)}, u32[]{:S(2)}, u32[]{:S(2)}) collective-permute-start(f32[256,1024]{1,0:T(8,128)S(1)} %pad_maximum_fusion.7.refs_2_), channel_id=1, source_target_pairs={{0,4},{1,5},{2,6},{3,7},{4,8},{5,9},{6,10},{7,11},{8,12},{9,13},{1... | collective-permute-start | bytes 3145736 | tf_op jit(solution)/shard_map/ppermute | solution.py:313
  28.4 29.1 %collective-permute-start.4 = (f32[256,1024]{1,0:T(8,128)S(1)}, f32[256,1024]{1,0:T(8,128)S(1)}, u32[]{:S(2)}, u32[]{:S(2)}) collective-permute-start(f32[256,1024]{1,0:T(8,128)S(1)} %pad_maximum_fusion.7.refs_2_), channel_id=1, source_target_pairs={{0,8},{1,9},{2,10},{3,11},{4,12},{5,13},{6,14},{7,15},{8,0},{9,1},... | collective-permute-start | bytes 3145736 | tf_op jit(solution)/shard_map/ppermute | solution.py:313
  31.3 26.2 %collective-permute-start.5 = (f32[256,1024]{1,0:T(8,128)S(1)}, f32[256,1024]{1,0:T(8,128)}, u32[]{:S(2)}, u32[]{:S(2)}) collective-permute-start(f32[256,1024]{1,0:T(8,128)S(1)} %pad_maximum_fusion.7.refs_2_), channel_id=1, source_target_pairs={{0,12},{1,13},{2,14},{3,15},{4,0},{5,1},{6,2},{7,3},{8,4},{9,5},{1... | collective-permute-start | bytes 3145736 | tf_op jit(solution)/shard_map/ppermute | solution.py:313
  86.5 74.6 %reduce-scatter.3.cloned.1.call-start = ((), (), s32[]{:S(2)}) async-start(), calls=%async_computation.4 | async-start | bytes 5013504 | tf_op jit(solution)/shard_map/reduce_scatter | solution.py:353
  112.8 2.2 %copy-start.1 = (f32[1024,128]{1,0:T(8,128)S(1)}, f32[1024,128]{1,0:T(8,128)}, u32[]{:S(2)}) copy-start(f32[1024,128]{1,0:T(8,128)} %param.5) | copy-start | bytes 1572868
  112.9 2.4 %copy-start.8 = (f32[1,1024]{1,0:T(1,128)S(1)}, f32[1,1024]{1,0:T(1,128)}, u32[]{:S(2)}) copy-start(f32[1,1024]{1,0:T(1,128)} %get-tuple-element.31) | copy-start | bytes 12292
  112.9 29.0 %copy-start.4 = (f32[264,1024]{1,0:T(8,128)S(1)}, f32[264,1024]{1,0:T(8,128)}, u32[]{:S(2)}) copy-start(f32[264,1024]{1,0:T(8,128)} %get-tuple-element.27) | copy-start | bytes 3244036
  112.9 15.5 %collective-permute-start.6 = (f32[264,1024]{1,0:T(8,128)}, f32[264,1024]{1,0:T(8,128)}, u32[]{:S(2)}, u32[]{:S(2)}) collective-permute-start(f32[264,1024]{1,0:T(8,128)} %get-tuple-element.28), channel_id=1, source_target_pairs={{0,12},{1,13},{2,14},{3,15},{4,0},{5,1},{6,2},{7,3},{8,4},{9,5},{1... | collective-permute-start | bytes 3244040 | tf_op jit(solution)/shard_map/ppermute | solution.py:313
  113.3 17.1 %collective-permute-start.7 = (f32[264,1024]{1,0:T(8,128)}, f32[264,1024]{1,0:T(8,128)}, u32[]{:S(2)}, u32[]{:S(2)}) collective-permute-start(f32[264,1024]{1,0:T(8,128)} %get-tuple-element.29), channel_id=1, source_target_pairs={{0,8},{1,9},{2,10},{3,11},{4,12},{5,13},{6,14},{7,15},{8,0},{9,1},... | collective-permute-start | bytes 3244040 | tf_op jit(solution)/shard_map/ppermute | solution.py:313
  114.1 27.7 %collective-permute-start.8 = (f32[264,1024]{1,0:T(8,128)}, f32[264,1024]{1,0:T(8,128)}, u32[]{:S(2)}, u32[]{:S(2)}) collective-permute-start(f32[264,1024]{1,0:T(8,128)} %get-tuple-element.30), channel_id=1, source_target_pairs={{0,4},{1,5},{2,6},{3,7},{4,8},{5,9},{6,10},{7,11},{8,12},{9,13},{1... | collective-permute-start | bytes 3244040 | tf_op jit(solution)/shard_map/ppermute | solution.py:313
  145.2 2.7 %copy-start.3 = (f32[264,1024]{1,0:T(8,128)S(1)}, f32[264,1024]{1,0:T(8,128)}, u32[]{:S(2)}) copy-start(f32[264,1024]{1,0:T(8,128)} %reduce-scatter.5.cloned.1.call-done) | copy-start | bytes 3244036
  146.3 18.3 %collective-permute-start.11 = (f32[72,2048]{1,0:T(8,128)S(1)}, f32[72,2048]{1,0:T(8,128)}, u32[]{:S(2)}, u32[]{:S(2)}) collective-permute-start(f32[72,2048]{1,0:T(8,128)S(1)} %pad_maximum_fusion.8), channel_id=1, source_target_pairs={{0,1},{1,2},{2,3},{3,0},{4,5},{5,6},{6,7},{7,4},{8,9},{9,10},{10,1... | collective-permute-start | bytes 1769480 | tf_op jit(solution)/shard_map/ppermute | solution.py:313
  147.9 5.5 %copy-start.7 = (f32[1,1024]{1,0:T(1,128)S(1)}, f32[1,1024]{1,0:T(1,128)}, u32[]{:S(2)}) copy-start(f32[1,1024]{1,0:T(1,128)} %get-tuple-element.32) | copy-start | bytes 12292
  147.9 13.2 %copy-start.6 = (f32[1,1024]{1,0:T(1,128)S(1)}, f32[1,1024]{1,0:T(1,128)}, u32[]{:S(2)}) copy-start(f32[1,1024]{1,0:T(1,128)} %get-tuple-element.25) | copy-start | bytes 12292
  149.2 15.4 %collective-permute-start.10 = (f32[72,2048]{1,0:T(8,128)}, f32[72,2048]{1,0:T(8,128)S(1)}, u32[]{:S(2)}, u32[]{:S(2)}) collective-permute-start(f32[72,2048]{1,0:T(8,128)} %get-tuple-element.52), channel_id=1, source_target_pairs={{0,2},{1,3},{2,0},{3,1},{4,6},{5,7},{6,4},{7,5},{8,10},{9,11},{10,... | collective-permute-start | bytes 1769480 | tf_op jit(solution)/shard_map/ppermute | solution.py:313
  151.9 14.5 %collective-permute-start.9 = (f32[72,2048]{1,0:T(8,128)}, f32[72,2048]{1,0:T(8,128)}, u32[]{:S(2)}, u32[]{:S(2)}) collective-permute-start(f32[72,2048]{1,0:T(8,128)} %get-tuple-element.53), channel_id=1, source_target_pairs={{0,3},{1,0},{2,1},{3,2},{4,7},{5,4},{6,5},{7,6},{8,11},{9,8},{10,9... | collective-permute-start | bytes 1769480 | tf_op jit(solution)/shard_map/ppermute | solution.py:313
  164.6 4.0 %copy-start.2 = (f32[2048,64]{0,1:T(8,128)S(1)}, f32[2048,64]{0,1:T(8,128)}, u32[]{:S(2)}) copy-start(f32[2048,64]{0,1:T(8,128)} %param.4) | copy-start | bytes 1572868
  (5 other events, 6.6 us)
Sparse Core Ops, SparseCore 0:
  9.7 38.7 all-gather.4
  50.1 32.6 all-gather.2
  86.6 31.5 reduce-scatter.4
  120.6 40.5 reduce-scatter.2

commit v6 on v5

--- a/solution.py
+++ b/solution.py
@@ -137,7 +137,7 @@
     n = v_high.shape[0]
     block = inv_ref.shape[1]
     sub = block // SUBS
-    offset = place[3] + step * block
+    offset = place[3] + (step if first else step + pl.num_programs(0)) * block
     loads = [
         pltpu.make_async_copy(source, to, sems.at[k])
         for k, (source, to) in enumerate(zip(sources, (v_high, v_small, t_high, t_small, near)))
@@ -339,30 +339,30 @@
     near, late = (jnp.concatenate([r[:, c * part : (c + 1) * part] for r in row], axis=0) for c in (0, 1))
     near = [near] + [move(near, False, k) for k in (1, 2, 3)]
     late = [lax.all_gather(late, PLANE, axis=0, tiled=True, axis_index_groups=OUTER)]
-    inv_v, *parts = prepare(whole_video, jnp.stack([core, y, x]).astype(jnp.int32))
     outer = jnp.where(core == 0, y, x)
-    places = [jnp.stack([core, y, x, base + c * part, outer]).astype(jnp.int32) for c in (0, 1)]
-    whole, inv_near, state = pairs(near, parts, places[0], scalars, None, False)
-    *grads, inv_late, state = pairs(late, parts, places[1], scalars, state, True)
+    place = jnp.stack([core, y, x, base, outer]).astype(jnp.int32)
+    inv_v, *parts = prepare(whole_video, place)
+    whole, inv_near, state = pairs(near, parts, place, scalars, None, False)
+    *grads, inv_late, state = pairs(late, parts, place, scalars, state, True)
     whole = whole.reshape(1056, part)
-    halves = [
-        lax.psum_scatter(whole, PLANE, scatter_dimension=0, tiled=True, axis_index_groups=OUTER),
-        grads[0] + sum(move(grads[k], False, 4 - k) for k in (1, 2, 3)),
+    early = lax.psum_scatter(whole, PLANE, scatter_dimension=0, tiled=True, axis_index_groups=OUTER)
+    came = [grads[0]] + [move(grads[k], False, 4 - k) for k in (1, 2, 3)]
+
+    def rows_of(low, high):
+        return jnp.concatenate([early[low:high], sum(c[low:high] for c in came)], axis=1)
+
+    to = [
+        jnp.concatenate([rows_of(64 * k, 64 * k + 64), rows_of(256, 264)], axis=0) for k in range(4)
     ]
 
     total_v = lax.psum_scatter(state.reshape(1088, n), ("z", "core"), scatter_dimension=0, tiled=True)
     grad_v = scale * (total_v[0:128] * inv_v - video.T * (inv_v * inv_v * total_v[128:129]))
-    to = [
-        jnp.concatenate(
-            [jnp.concatenate([h[64 * k : 64 * k + 64], h[256:264]], axis=0) for h in halves], axis=1
-        )
-        for k in range(4)
-    ]
     (kept,) = after([grad_v[:8]], [to[0]])
-    total_a = kept + sum(move(to[k], True, 4 - k) for k in (1, 2, 3))
+    blocks = [kept] + [move(to[k], True, 4 - k) for k in (1, 2, 3)]
+    side, total_a = sum(t[64:] for t in blocks), sum(t[:64] for t in blocks)
     inv_a = jnp.concatenate([inv_near, inv_late], axis=1)
-    row_loss, inner_a = total_a[64], total_a[65:66]
-    grad_a = scale * (total_a[0:64] * inv_a - audio_t * (inv_a * inv_a * inner_a))
+    row_loss, inner_a = side[0], side[1:2]
+    grad_a = scale * (total_a * inv_a - audio_t * (inv_a * inv_a * inner_a))
     return row_loss, grad_a.T, grad_v.T
 
 

time: 177 us -> 177 us (level)
    add x2 -> x3, other arithmetic: 3.85 us -> 4.26 us  [the longest x2 3.4 us: rows_of(): sum((c[low:high] for c in came))]
  transfers between devices with their start and end apart: 16 -> 16, of which waited for: 8 -> 9; matrix products, arithmetic and copies ran while one was open for 8% -> 8% of each run, Pallas kernels for 35% -> 36%
where the time goes in v6:
time: 177 us; the launch traced here: 175 us
  Pallas kernels  62.3 us (35%)
  waiting for transfers between devices  59.3 us (34%)
  starting transfers between devices  20.2 us (11%)
  between operations  15.3 us (9%)
  other arithmetic  12 us (7%)
  local copies, waits for them, and re-layouts  6.35 us (4%)
    pallas_call x2, Pallas kernels, pairs(): pl.pallas_call(body, grid_spec=pltpu.PrefetchScalarGridSpec(num_scalar_pr...  53.4 us
    ppermute x12, waiting for transfers between devices, move(): return lax.ppermute(block, PLANE, perm(inner, k))  37.4 us
    ppermute x12, starting transfers between devices, move(): return lax.ppermute(block, PLANE, perm(inner, k))  20 us
    all_gather x1, waiting for transfers between devices, local(): whole_video = lax.all_gather(video, ('z', 'core'), axis=1, tiled=True)  13.2 us
    pallas_call x1, Pallas kernels, prepare(): pl.pallas_call(prepare_kernel, in_specs=[pl.BlockSpec(memory_space=pltpu....  8.96 us
    reduce_scatter x1, waiting for transfers between devices, local(): lax.psum_scatter(state.reshape(1088, n), ('z', 'core'), scatter_dimension...  7.94 us
  transfers between devices with their start and end apart: 16, of which 9 were waited for; matrix products, arithmetic and copies ran while one was open for 8% of the time, Pallas kernels for 36%

profile of v6, /device:TPU:0, one launch (start us, length us, event | category | flops | bytes accessed | tf_op | source)
XLA Modules:
  0.0 175.4 jit_solution(13362949545709895202)
XLA Ops:
  7.9 1.6 collective-permute-start
  9.6 2.7 %collective-permute-start.1 = (f32[64,2048]{1,0:T(8,128)}, f32[64,2048]{1,0:T(8,128)S(1)}, u32[]{:S(2)}, u32[]{:S(2)}) collective-permute-start(f32[64,2048]{1,0:T(8,128)} %bitcast.27), channel_id=1, source_target_pairs={{0,2},{1,3},{2,0},{3,1},{4,6},{5,7},{6,4},{7,5},{8,10},{9,11},{10,... | collective-permute-start | bytes 1572872 | tf_op jit(solution)/shard_map/ppermute | solution.py:313
  12.3 1.4 collective-permute-start.2
  14.8 3.8 %collective-permute-done = f32[64,2048]{1,0:T(8,128)S(1)} collective-permute-done((f32[64,2048]{1,0:T(8,128)}, f32[64,2048]{1,0:T(8,128)S(1)}, u32[]{:S(2)}, u32[]{:S(2)}) %collective-permute-start) | collective-permute-done | bytes 524320 | tf_op jit(solution)/shard_map/ppermute | solution.py:313
  18.7 6.6 %collective-permute-done.1 = f32[64,2048]{1,0:T(8,128)S(1)} collective-permute-done((f32[64,2048]{1,0:T(8,128)}, f32[64,2048]{1,0:T(8,128)S(1)}, u32[]{:S(2)}, u32[]{:S(2)}) %collective-permute-start.1) | collective-permute-done | bytes 524320 | tf_op jit(solution)/shard_map/ppermute | solution.py:313
  25.4 1.1 pad_maximum_fusion
  26.7 1.6 collective-permute-start.3
  28.3 2.9 %collective-permute-start.4 = (f32[256,1024]{1,0:T(8,128)S(1)}, f32[256,1024]{1,0:T(8,128)S(1)}, u32[]{:S(2)}, u32[]{:S(2)}) collective-permute-start(f32[256,1024]{1,0:T(8,128)S(1)} %pad_maximum_fusion.1.refs_2_), channel_id=1, source_target_pairs={{0,8},{1,9},{2,10},{3,11},{4,12},{5,13},{6,14},{7,15},{8,0},{9,1},... | collective-permute-start | bytes 3145736 | tf_op jit(solution)/shard_map/ppermute | solution.py:313
  31.2 1.3 collective-permute-start.5
  35.2 13.2 %all-gather.5.cloned.1.call-done.video = f32[1024,1024]{1,0:T(8,128)} async-done(((f32[1024,128]{1,0:T(8,128)}), f32[1024,1024]{1,0:T(8,128)}) %all-gather.5.cloned.1.call-update) | async-done | bytes 4194320 | tf_op jit(solution)/shard_map/all_gather | solution.py:336
  48.5 9.0 %video_parts.1 = (f32[1,1024]{1,0:T(1,128)}, f32[1024,1024]{1,0:T(8,128)}, bf16[1024,1024]{1,0:T(8,128)(2,1)}, f8e4m3fn[1024,2048]{1,0:T(32,128)(4,1)}, bf16[102...) custom-call(s32[5]{0:T(128)} %stack.32.place.refs_0_, f32[1024,1024]{1,0:T(8,128)} %all-gather.5.cloned.1.call-done.video), custom_call_target="tpu_custom_call" | custom-call | bytes 16777216 | tf_op jit(solution)/shard_map/video_parts/pallas_call | solution.py:94
  58.8 27.7 %pairs_first.1 = (f32[4,264,1024]{2,1,0:T(8,128)}, f32[1,1024]{1,0:T(1,128)}, f32[1024,1024]{1,0:T(8,128)}) custom-call(s32[5]{0:T(128)} %stack.32.place.refs_0_, f32[2]{0:T(128)} %pad_maximum_fusion.3.refs_1_, f32[256,1024]{1,0:T(8,128)} %copy-done.4, f32[256,1024]{1,0:T(8,128)} %copy-done.8, f32[256,1024]{1,0:T(8,128)} %copy-done.9, ...), custom_call_target="tpu_custom_call" | custom-call | flops 12884901888 | bytes 25165824 | tf_op jit(solution)/shard_map/pairs_first/pallas_call | solution.py:283
  86.6 25.7 %pairs_last.1 = (f32[264,1024]{1,0:T(8,128)}, f32[264,1024]{1,0:T(8,128)}, f32[264,1024]{1,0:T(8,128)}, f32[264,1024]{1,0:T(8,128)}, f32[1,1024]{1,0:T(1,128)}, /*index=5*/f32[8,136,1024]{2,1,0:T(8,128)}) custom-call(s32[5]{0:T(128)} %stack.32.place.refs_0_, f32[2]{0:T(128)} %pad_maximum_fusion.3.refs_1_, ...), custom_call_target="tpu_custom_call" | custom-call | flops 12884901888 | bytes 25165824 | tf_op jit(solution)/shard_map/pairs_last/pallas_call | solution.py:283
  114.7 13.1 %collective-permute-done.6 = f32[264,1024]{1,0:T(8,128)S(1)} collective-permute-done((f32[264,1024]{1,0:T(8,128)}, f32[264,1024]{1,0:T(8,128)S(1)}, u32[]{:S(2)}, u32[]{:S(2)}) %collective-permute-start.6) | collective-permute-done | bytes 1081376 | tf_op jit(solution)/shard_map/ppermute | solution.py:313
  127.8 2.1 %collective-permute-done.7 = f32[264,1024]{1,0:T(8,128)} collective-permute-done((f32[264,1024]{1,0:T(8,128)}, f32[264,1024]{1,0:T(8,128)}, u32[]{:S(2)}, u32[]{:S(2)}) %collective-permute-start.7) | collective-permute-done | bytes 1081376 | tf_op jit(solution)/shard_map/ppermute | solution.py:313
  129.8 11.5 %collective-permute-done.8 = f32[264,1024]{1,0:T(8,128)} collective-permute-done((f32[264,1024]{1,0:T(8,128)}, f32[264,1024]{1,0:T(8,128)}, u32[]{:S(2)}, u32[]{:S(2)}) %collective-permute-start.8) | collective-permute-done | bytes 1081376 | tf_op jit(solution)/shard_map/ppermute | solution.py:313
  142.1 2.6 %slice_add_fusion.12 = (f32[64,1024]{1,0:T(8,128)S(1)}, f32[64,1024]{1,0:T(8,128)S(1)}, f32[64,1024]{1,0:T(8,128)S(1)}, f32[64,1024]{1,0:T(8,128)}) fusion(f32[264,1024]{1,0:T(8,128)} %collective-permute-done.8, f32[264,1024]{1,0:T(8,128)} %collective-permute-done.7, f32[264,1024]{1,0:T(8,128)S(1)} %collective-permute-done.6, f32[264,1024]{1,0:T(8,128)S(1)} %copy-done.2), kind=kLoop, calls=%fused_computation.26 | loop fusion | flops 786432 | bytes 5242880 | tf_op jit(solution)/shard_map/add | solution.py:352
  144.7 1.3 fusion.10
  146.1 1.3 fusion.3
  147.4 3.0 %collective-permute-start.10 = (f32[72,2048]{1,0:T(8,128)}, f32[72,2048]{1,0:T(8,128)S(1)}, u32[]{:S(2)}, u32[]{:S(2)}) collective-permute-start(f32[72,2048]{1,0:T(8,128)} %get-tuple-element.56), channel_id=1, source_target_pairs={{0,2},{1,3},{2,0},{3,1},{4,6},{5,7},{6,4},{7,5},{8,10},{9,11},{10,... | collective-permute-start | bytes 1769480 | tf_op jit(solution)/shard_map/ppermute | solution.py:313
  151.0 2.7 %collective-permute-start.9 = (f32[72,2048]{1,0:T(8,128)S(1)}, f32[72,2048]{1,0:T(8,128)S(1)}, u32[]{:S(2)}, u32[]{:S(2)}) collective-permute-start(f32[72,2048]{1,0:T(8,128)S(1)} %get-tuple-element.55), channel_id=1, source_target_pairs={{0,3},{1,0},{2,1},{3,2},{4,7},{5,4},{6,5},{7,6},{8,11},{9,8},{10,9... | collective-permute-start | bytes 1769480 | tf_op jit(solution)/shard_map/ppermute | solution.py:313
  153.7 7.9 %reduce-scatter.3.cloned.1.call-done = f32[136,1024]{1,0:T(8,128)} async-done(((f32[1088,1024]{1,0:T(8,128)}), f32[136,1024]{1,0:T(8,128)}) %reduce-scatter.3.cloned.1.call-update) | async-done | bytes 557072 | tf_op jit(solution)/shard_map/reduce_scatter | solution.py:358
  162.4 1.1 fusion.9
  166.9 2.0 %fusion.7 = f32[2048,64]{0,1:T(8,128)} fusion(f32[72,2048]{1,0:T(8,128)S(1)} %collective-permute-done.11, f32[72,2048]{1,0:T(8,128)S(1)} %collective-permute-done.10, f32[72,2048]{1,0:T(8,128)S(1)} %collective-permute-done.9, f32[72,2048]{1,0:T(8,128)} %after.1, f32[2048]{0:T(1024)S(1)} %bitcast.31, f32[2048]{0:T(1024)S(1)} %bitcast.30, f32[]{:T(128)} %copy.12, ...), kind=kLoop, calls=%fused_computation.11 | loop fusion | flops 917504 | bytes 3162116 | tf_op jit(solution)/shard_map/transpose | solution.py:366
  (60 shorter events, 12.7 us)
Async XLA Ops:
  7.2 41.3 %all-gather.5.cloned.1.call-start = ((), (), s32[]{:S(2)}) async-start(), calls=%async_computation.3 | async-start | bytes 4718592 | tf_op jit(solution)/shard_map/all_gather | solution.py:336
  7.9 78.7 %all-gather.3.cloned.1.call-start = ((), (), s32[]{:S(2)}) async-start(), calls=%async_computation.2 | async-start | bytes 5242880 | tf_op jit(solution)/shard_map/all_gather | solution.py:341
  7.9 10.7 %collective-permute-start = (f32[64,2048]{1,0:T(8,128)}, f32[64,2048]{1,0:T(8,128)S(1)}, u32[]{:S(2)}, u32[]{:S(2)}) collective-permute-start(f32[64,2048]{1,0:T(8,128)} %bitcast.26), channel_id=1, source_target_pairs={{0,1},{1,2},{2,3},{3,0},{4,5},{5,6},{6,7},{7,4},{8,9},{9,10},{10,1... | collective-permute-start | bytes 1572872 | tf_op jit(solution)/shard_map/ppermute | solution.py:313
  9.6 15.7 %collective-permute-start.1 = (f32[64,2048]{1,0:T(8,128)}, f32[64,2048]{1,0:T(8,128)S(1)}, u32[]{:S(2)}, u32[]{:S(2)}) collective-permute-start(f32[64,2048]{1,0:T(8,128)} %bitcast.27), channel_id=1, source_target_pairs={{0,2},{1,3},{2,0},{3,1},{4,6},{5,7},{6,4},{7,5},{8,10},{9,11},{10,... | collective-permute-start | bytes 1572872 | tf_op jit(solution)/shard_map/ppermute | solution.py:313
  12.3 13.0 %collective-permute-start.2 = (f32[64,2048]{1,0:T(8,128)}, f32[64,2048]{1,0:T(8,128)S(1)}, u32[]{:S(2)}, u32[]{:S(2)}) collective-permute-start(f32[64,2048]{1,0:T(8,128)} %bitcast.28), channel_id=1, source_target_pairs={{0,3},{1,0},{2,1},{3,2},{4,7},{5,4},{6,5},{7,6},{8,11},{9,8},{10,9... | collective-permute-start | bytes 1572872 | tf_op jit(solution)/shard_map/ppermute | solution.py:313
  26.5 118.2 %reduce-scatter.5.cloned.1.call-start = ((), (), s32[]{:S(2)}) async-start(), calls=%async_computation.5 | async-start | bytes 5406720 | tf_op jit(solution)/shard_map/reduce_scatter | solution.py:348
  26.7 30.7 %copy-start.4 = (f32[256,1024]{1,0:T(8,128)}, f32[256,1024]{1,0:T(8,128)S(1)}, u32[]{:S(2)}) copy-start(f32[256,1024]{1,0:T(8,128)S(1)} %pad_maximum_fusion.1.refs_2_) | copy-start | bytes 3145732
  26.7 30.7 %collective-permute-start.3 = (f32[256,1024]{1,0:T(8,128)S(1)}, f32[256,1024]{1,0:T(8,128)S(1)}, u32[]{:S(2)}, u32[]{:S(2)}) collective-permute-start(f32[256,1024]{1,0:T(8,128)S(1)} %pad_maximum_fusion.1.refs_2_), channel_id=1, source_target_pairs={{0,4},{1,5},{2,6},{3,7},{4,8},{5,9},{6,10},{7,11},{8,12},{9,13},{1... | collective-permute-start | bytes 3145736 | tf_op jit(solution)/shard_map/ppermute | solution.py:313
  28.3 29.1 %collective-permute-start.4 = (f32[256,1024]{1,0:T(8,128)S(1)}, f32[256,1024]{1,0:T(8,128)S(1)}, u32[]{:S(2)}, u32[]{:S(2)}) collective-permute-start(f32[256,1024]{1,0:T(8,128)S(1)} %pad_maximum_fusion.1.refs_2_), channel_id=1, source_target_pairs={{0,8},{1,9},{2,10},{3,11},{4,12},{5,13},{6,14},{7,15},{8,0},{9,1},... | collective-permute-start | bytes 3145736 | tf_op jit(solution)/shard_map/ppermute | solution.py:313
  31.2 26.2 %collective-permute-start.5 = (f32[256,1024]{1,0:T(8,128)S(1)}, f32[256,1024]{1,0:T(8,128)}, u32[]{:S(2)}, u32[]{:S(2)}) collective-permute-start(f32[256,1024]{1,0:T(8,128)S(1)} %pad_maximum_fusion.1.refs_2_), channel_id=1, source_target_pairs={{0,12},{1,13},{2,14},{3,15},{4,0},{5,1},{6,2},{7,3},{8,4},{9,5},{1... | collective-permute-start | bytes 3145736 | tf_op jit(solution)/shard_map/ppermute | solution.py:313
  86.5 75.1 %reduce-scatter.3.cloned.1.call-start = ((), (), s32[]{:S(2)}) async-start(), calls=%async_computation.4 | async-start | bytes 5013504 | tf_op jit(solution)/shard_map/reduce_scatter | solution.py:358
  112.3 2.2 %copy-start = (f32[1024,128]{1,0:T(8,128)S(1)}, f32[1024,128]{1,0:T(8,128)}, u32[]{:S(2)}) copy-start(f32[1024,128]{1,0:T(8,128)} %param.5) | copy-start | bytes 1572868
  112.3 2.4 %copy-start.7 = (f32[1,1024]{1,0:T(1,128)S(1)}, f32[1,1024]{1,0:T(1,128)}, u32[]{:S(2)}) copy-start(f32[1,1024]{1,0:T(1,128)} %get-tuple-element.31) | copy-start | bytes 12292
  112.3 29.0 %copy-start.2 = (f32[264,1024]{1,0:T(8,128)S(1)}, f32[264,1024]{1,0:T(8,128)}, u32[]{:S(2)}) copy-start(f32[264,1024]{1,0:T(8,128)} %get-tuple-element.27) | copy-start | bytes 3244036
  112.3 15.4 %collective-permute-start.6 = (f32[264,1024]{1,0:T(8,128)}, f32[264,1024]{1,0:T(8,128)S(1)}, u32[]{:S(2)}, u32[]{:S(2)}) collective-permute-start(f32[264,1024]{1,0:T(8,128)} %get-tuple-element.28), channel_id=1, source_target_pairs={{0,12},{1,13},{2,14},{3,15},{4,0},{5,1},{6,2},{7,3},{8,4},{9,5},{1... | collective-permute-start | bytes 3244040 | tf_op jit(solution)/shard_map/ppermute | solution.py:313
  112.7 17.1 %collective-permute-start.7 = (f32[264,1024]{1,0:T(8,128)}, f32[264,1024]{1,0:T(8,128)}, u32[]{:S(2)}, u32[]{:S(2)}) collective-permute-start(f32[264,1024]{1,0:T(8,128)} %get-tuple-element.29), channel_id=1, source_target_pairs={{0,8},{1,9},{2,10},{3,11},{4,12},{5,13},{6,14},{7,15},{8,0},{9,1},... | collective-permute-start | bytes 3244040 | tf_op jit(solution)/shard_map/ppermute | solution.py:313
  113.6 27.8 %collective-permute-start.8 = (f32[264,1024]{1,0:T(8,128)}, f32[264,1024]{1,0:T(8,128)}, u32[]{:S(2)}, u32[]{:S(2)}) collective-permute-start(f32[264,1024]{1,0:T(8,128)} %get-tuple-element.30), channel_id=1, source_target_pairs={{0,4},{1,5},{2,6},{3,7},{4,8},{5,9},{6,10},{7,11},{8,12},{9,13},{1... | collective-permute-start | bytes 3244040 | tf_op jit(solution)/shard_map/ppermute | solution.py:313
  144.7 1.4 slice-start
  146.1 7.6 %copy-start.6 = (f32[1,1024]{1,0:T(1,128)S(1)}, f32[1,1024]{1,0:T(1,128)}, u32[]{:S(2)}) copy-start(f32[1,1024]{1,0:T(1,128)} %get-tuple-element.32) | copy-start | bytes 12292
  146.1 15.5 %copy-start.5 = (f32[1,1024]{1,0:T(1,128)S(1)}, f32[1,1024]{1,0:T(1,128)}, u32[]{:S(2)}) copy-start(f32[1,1024]{1,0:T(1,128)} %get-tuple-element.25) | copy-start | bytes 12292
  147.4 17.7 %collective-permute-start.10 = (f32[72,2048]{1,0:T(8,128)}, f32[72,2048]{1,0:T(8,128)S(1)}, u32[]{:S(2)}, u32[]{:S(2)}) collective-permute-start(f32[72,2048]{1,0:T(8,128)} %get-tuple-element.56), channel_id=1, source_target_pairs={{0,2},{1,3},{2,0},{3,1},{4,6},{5,7},{6,4},{7,5},{8,10},{9,11},{10,... | collective-permute-start | bytes 1769480 | tf_op jit(solution)/shard_map/ppermute | solution.py:313
  150.4 14.9 %collective-permute-start.11 = (f32[72,2048]{1,0:T(8,128)}, f32[72,2048]{1,0:T(8,128)S(1)}, u32[]{:S(2)}, u32[]{:S(2)}) collective-permute-start(f32[72,2048]{1,0:T(8,128)} %get-tuple-element.57), channel_id=1, source_target_pairs={{0,1},{1,2},{2,3},{3,0},{4,5},{5,6},{6,7},{7,4},{8,9},{9,10},{10,1... | collective-permute-start | bytes 1769480 | tf_op jit(solution)/shard_map/ppermute | solution.py:313
  151.0 14.4 %collective-permute-start.9 = (f32[72,2048]{1,0:T(8,128)S(1)}, f32[72,2048]{1,0:T(8,128)S(1)}, u32[]{:S(2)}, u32[]{:S(2)}) collective-permute-start(f32[72,2048]{1,0:T(8,128)S(1)} %get-tuple-element.55), channel_id=1, source_target_pairs={{0,3},{1,0},{2,1},{3,2},{4,7},{5,4},{6,5},{7,6},{8,11},{9,8},{10,9... | collective-permute-start | bytes 1769480 | tf_op jit(solution)/shard_map/ppermute | solution.py:313
  164.1 2.8 %copy-start.1 = (f32[2048,64]{0,1:T(8,128)S(1)}, f32[2048,64]{0,1:T(8,128)}, u32[]{:S(2)}) copy-start(f32[2048,64]{0,1:T(8,128)} %param.4) | copy-start | bytes 1572868
  (3 other events, 3.7 us)
Sparse Core Ops, SparseCore 0:
  9.7 38.7 all-gather.4
  50.1 32.6 all-gather.2
  86.6 31.6 reduce-scatter.4
  120.6 40.9 reduce-scatter.2

commit v7 on v6

--- a/solution.py
+++ b/solution.py
@@ -346,7 +346,7 @@
     *grads, inv_late, state = pairs(late, parts, place, scalars, state, True)
     whole = whole.reshape(1056, part)
     early = lax.psum_scatter(whole, PLANE, scatter_dimension=0, tiled=True, axis_index_groups=OUTER)
-    came = [grads[0]] + [move(grads[k], False, 4 - k) for k in (1, 2, 3)]
+    came = [grads[0]] + [move(grads[k], False, 4 - k) for k in (2, 1, 3)]
 
     def rows_of(low, high):
         return jnp.concatenate([early[low:high], sum(c[low:high] for c in came)], axis=1)

time: 177 us -> 184 us (1.040)
  waiting for transfers between devices: 59.3 us -> 67.7 us
    reduce_scatter x1, waiting for transfers between devices: 7.94 us -> 17.6 us  [local(): lax.psum_scatter(state.reshape(1088, n), ('z', 'core'), scatter_dimension...]
  transfers between devices with their start and end apart: 16 -> 16, of which waited for: 9 -> 7; matrix products, arithmetic and copies ran while one was open for 8% -> 7% of each run, Pallas kernels for 36% -> 34%
where the time goes in v7:
time: 184 us
  waiting for transfers between devices  67.7 us (37%)
  Pallas kernels  62.3 us (34%)
  starting transfers between devices  20.3 us (11%)
  between operations  15.3 us (8%)
  other arithmetic  12 us (7%)
  local copies, waits for them, and re-layouts  6.34 us (3%)
    pallas_call x2, Pallas kernels, pairs(): pl.pallas_call(body, grid_spec=pltpu.PrefetchScalarGridSpec(num_scalar_pr...  53.4 us
    ppermute x12, waiting for transfers between devices, move(): return lax.ppermute(block, PLANE, perm(inner, k))  36.1 us
    ppermute x12, starting transfers between devices, move(): return lax.ppermute(block, PLANE, perm(inner, k))  20.1 us
    reduce_scatter x1, waiting for transfers between devices, local(): lax.psum_scatter(state.reshape(1088, n), ('z', 'core'), scatter_dimension...  17.6 us
    all_gather x1, waiting for transfers between devices, local(): whole_video = lax.all_gather(video, ('z', 'core'), axis=1, tiled=True)  13.2 us
    pallas_call x1, Pallas kernels, prepare(): pl.pallas_call(prepare_kernel, in_specs=[pl.BlockSpec(memory_space=pltpu....  8.96 us
  transfers between devices with their start and end apart: 16, of which 7 were waited for; matrix products, arithmetic and copies ran while one was open for 7% of the time, Pallas kernels for 34%

profile of v7, /device:TPU:0, one launch (start us, length us, event | category | flops | bytes accessed | tf_op | source)
XLA Modules:
  0.0 183.9 jit_solution(15760429489192082138)
XLA Ops:
  7.9 1.6 collective-permute-start
  9.6 2.7 %collective-permute-start.1 = (f32[64,2048]{1,0:T(8,128)}, f32[64,2048]{1,0:T(8,128)S(1)}, u32[]{:S(2)}, u32[]{:S(2)}) collective-permute-start(f32[64,2048]{1,0:T(8,128)} %bitcast.27), channel_id=1, source_target_pairs={{0,2},{1,3},{2,0},{3,1},{4,6},{5,7},{6,4},{7,5},{8,10},{9,11},{10,... | collective-permute-start | bytes 1572872 | tf_op jit(solution)/shard_map/ppermute | solution.py:313
  12.3 1.4 collective-permute-start.2
  14.8 3.8 %collective-permute-done = f32[64,2048]{1,0:T(8,128)S(1)} collective-permute-done((f32[64,2048]{1,0:T(8,128)}, f32[64,2048]{1,0:T(8,128)S(1)}, u32[]{:S(2)}, u32[]{:S(2)}) %collective-permute-start) | collective-permute-done | bytes 524320 | tf_op jit(solution)/shard_map/ppermute | solution.py:313
  18.7 6.6 %collective-permute-done.1 = f32[64,2048]{1,0:T(8,128)S(1)} collective-permute-done((f32[64,2048]{1,0:T(8,128)}, f32[64,2048]{1,0:T(8,128)S(1)}, u32[]{:S(2)}, u32[]{:S(2)}) %collective-permute-start.1) | collective-permute-done | bytes 524320 | tf_op jit(solution)/shard_map/ppermute | solution.py:313
  26.7 1.6 collective-permute-start.3
  28.3 2.9 %collective-permute-start.4 = (f32[256,1024]{1,0:T(8,128)S(1)}, f32[256,1024]{1,0:T(8,128)S(1)}, u32[]{:S(2)}, u32[]{:S(2)}) collective-permute-start(f32[256,1024]{1,0:T(8,128)S(1)} %pad_maximum_fusion.1.refs_2_), channel_id=1, source_target_pairs={{0,8},{1,9},{2,10},{3,11},{4,12},{5,13},{6,14},{7,15},{8,0},{9,1},... | collective-permute-start | bytes 3145736 | tf_op jit(solution)/shard_map/ppermute | solution.py:313
  31.2 1.3 collective-permute-start.5
  35.2 13.2 %all-gather.5.cloned.1.call-done.video = f32[1024,1024]{1,0:T(8,128)} async-done(((f32[1024,128]{1,0:T(8,128)}), f32[1024,1024]{1,0:T(8,128)}) %all-gather.5.cloned.1.call-update) | async-done | bytes 4194320 | tf_op jit(solution)/shard_map/all_gather | solution.py:336
  48.5 9.0 %video_parts.1 = (f32[1,1024]{1,0:T(1,128)}, f32[1024,1024]{1,0:T(8,128)}, bf16[1024,1024]{1,0:T(8,128)(2,1)}, f8e4m3fn[1024,2048]{1,0:T(32,128)(4,1)}, bf16[102...) custom-call(s32[5]{0:T(128)} %stack.32.place.refs_0_, f32[1024,1024]{1,0:T(8,128)} %all-gather.5.cloned.1.call-done.video), custom_call_target="tpu_custom_call" | custom-call | bytes 16777216 | tf_op jit(solution)/shard_map/video_parts/pallas_call | solution.py:94
  58.8 27.7 %pairs_first.1 = (f32[4,264,1024]{2,1,0:T(8,128)}, f32[1,1024]{1,0:T(1,128)}, f32[1024,1024]{1,0:T(8,128)}) custom-call(s32[5]{0:T(128)} %stack.32.place.refs_0_, f32[2]{0:T(128)} %pad_maximum_fusion.3.refs_1_, f32[256,1024]{1,0:T(8,128)} %copy-done.4, f32[256,1024]{1,0:T(8,128)} %copy-done.8, f32[256,1024]{1,0:T(8,128)} %copy-done.9, ...), custom_call_target="tpu_custom_call" | custom-call | flops 12884901888 | bytes 25165824 | tf_op jit(solution)/shard_map/pairs_first/pallas_call | solution.py:283
  86.6 25.7 %pairs_last.1 = (f32[264,1024]{1,0:T(8,128)}, f32[264,1024]{1,0:T(8,128)}, f32[264,1024]{1,0:T(8,128)}, f32[264,1024]{1,0:T(8,128)}, f32[1,1024]{1,0:T(1,128)}, /*index=5*/f32[8,136,1024]{2,1,0:T(8,128)}) custom-call(s32[5]{0:T(128)} %stack.32.place.refs_0_, f32[2]{0:T(128)} %pad_maximum_fusion.3.refs_1_, ...), custom_call_target="tpu_custom_call" | custom-call | flops 12884901888 | bytes 25165824 | tf_op jit(solution)/shard_map/pairs_last/pallas_call | solution.py:283
  113.0 1.1 collective-permute-start.7
  115.3 14.1 %collective-permute-done.6 = f32[264,1024]{1,0:T(8,128)S(1)} collective-permute-done((f32[264,1024]{1,0:T(8,128)}, f32[264,1024]{1,0:T(8,128)S(1)}, u32[]{:S(2)}, u32[]{:S(2)}) %collective-permute-start.6) | collective-permute-done | bytes 1081376 | tf_op jit(solution)/shard_map/ppermute | solution.py:313
  129.4 9.6 %collective-permute-done.7 = f32[264,1024]{1,0:T(8,128)} collective-permute-done((f32[264,1024]{1,0:T(8,128)}, f32[264,1024]{1,0:T(8,128)}, u32[]{:S(2)}, u32[]{:S(2)}) %collective-permute-start.7) | collective-permute-done | bytes 1081376 | tf_op jit(solution)/shard_map/ppermute | solution.py:313
  139.0 2.0 %collective-permute-done.8 = f32[264,1024]{1,0:T(8,128)} collective-permute-done((f32[264,1024]{1,0:T(8,128)}, f32[264,1024]{1,0:T(8,128)}, u32[]{:S(2)}, u32[]{:S(2)}) %collective-permute-start.8) | collective-permute-done | bytes 1081376 | tf_op jit(solution)/shard_map/ppermute | solution.py:313
  141.8 2.6 %slice_add_fusion.12 = (f32[64,1024]{1,0:T(8,128)S(1)}, f32[64,1024]{1,0:T(8,128)S(1)}, f32[64,1024]{1,0:T(8,128)S(1)}, f32[64,1024]{1,0:T(8,128)}) fusion(f32[264,1024]{1,0:T(8,128)} %collective-permute-done.8, f32[264,1024]{1,0:T(8,128)} %collective-permute-done.7, f32[264,1024]{1,0:T(8,128)S(1)} %collective-permute-done.6, f32[264,1024]{1,0:T(8,128)S(1)} %copy-done.2), kind=kLoop, calls=%fused_computation.26 | loop fusion | flops 786432 | bytes 5242880 | tf_op jit(solution)/shard_map/add | solution.py:352
  144.4 1.3 fusion.10
  145.8 1.3 fusion.3
  147.1 2.4 %collective-permute-start.10 = (f32[72,2048]{1,0:T(8,128)}, f32[72,2048]{1,0:T(8,128)S(1)}, u32[]{:S(2)}, u32[]{:S(2)}) collective-permute-start(f32[72,2048]{1,0:T(8,128)} %get-tuple-element.56), channel_id=1, source_target_pairs={{0,2},{1,3},{2,0},{3,1},{4,6},{5,7},{6,4},{7,5},{8,10},{9,11},{10,... | collective-permute-start | bytes 1769480 | tf_op jit(solution)/shard_map/ppermute | solution.py:313
  150.1 2.7 %collective-permute-start.9 = (f32[72,2048]{1,0:T(8,128)S(1)}, f32[72,2048]{1,0:T(8,128)S(1)}, u32[]{:S(2)}, u32[]{:S(2)}) collective-permute-start(f32[72,2048]{1,0:T(8,128)S(1)} %get-tuple-element.55), channel_id=1, source_target_pairs={{0,3},{1,0},{2,1},{3,2},{4,7},{5,4},{6,5},{7,6},{8,11},{9,8},{10,9... | collective-permute-start | bytes 1769480 | tf_op jit(solution)/shard_map/ppermute | solution.py:313
  152.8 17.6 %reduce-scatter.3.cloned.1.call-done = f32[136,1024]{1,0:T(8,128)} async-done(((f32[1088,1024]{1,0:T(8,128)}), f32[136,1024]{1,0:T(8,128)}) %reduce-scatter.3.cloned.1.call-update) | async-done | bytes 557072 | tf_op jit(solution)/shard_map/reduce_scatter | solution.py:358
  171.2 1.1 fusion.9
  175.4 2.0 %fusion.7 = f32[2048,64]{0,1:T(8,128)} fusion(f32[72,2048]{1,0:T(8,128)S(1)} %collective-permute-done.11, f32[72,2048]{1,0:T(8,128)S(1)} %collective-permute-done.10, f32[72,2048]{1,0:T(8,128)S(1)} %collective-permute-done.9, f32[72,2048]{1,0:T(8,128)} %after.1, f32[2048]{0:T(1024)S(1)} %bitcast.31, f32[2048]{0:T(1024)S(1)} %bitcast.30, f32[]{:T(128)} %copy.12, ...), kind=kLoop, calls=%fused_computation.11 | loop fusion | flops 917504 | bytes 3162116 | tf_op jit(solution)/shard_map/transpose | solution.py:366
  (60 shorter events, 13.0 us)
Async XLA Ops:
  7.2 41.3 %all-gather.5.cloned.1.call-start = ((), (), s32[]{:S(2)}) async-start(), calls=%async_computation.3 | async-start | bytes 4718592 | tf_op jit(solution)/shard_map/all_gather | solution.py:336
  7.9 78.7 %all-gather.3.cloned.1.call-start = ((), (), s32[]{:S(2)}) async-start(), calls=%async_computation.2 | async-start | bytes 5242880 | tf_op jit(solution)/shard_map/all_gather | solution.py:341
  7.9 10.7 %collective-permute-start = (f32[64,2048]{1,0:T(8,128)}, f32[64,2048]{1,0:T(8,128)S(1)}, u32[]{:S(2)}, u32[]{:S(2)}) collective-permute-start(f32[64,2048]{1,0:T(8,128)} %bitcast.26), channel_id=1, source_target_pairs={{0,1},{1,2},{2,3},{3,0},{4,5},{5,6},{6,7},{7,4},{8,9},{9,10},{10,1... | collective-permute-start | bytes 1572872 | tf_op jit(solution)/shard_map/ppermute | solution.py:313
  9.6 15.7 %collective-permute-start.1 = (f32[64,2048]{1,0:T(8,128)}, f32[64,2048]{1,0:T(8,128)S(1)}, u32[]{:S(2)}, u32[]{:S(2)}) collective-permute-start(f32[64,2048]{1,0:T(8,128)} %bitcast.27), channel_id=1, source_target_pairs={{0,2},{1,3},{2,0},{3,1},{4,6},{5,7},{6,4},{7,5},{8,10},{9,11},{10,... | collective-permute-start | bytes 1572872 | tf_op jit(solution)/shard_map/ppermute | solution.py:313
  12.3 13.0 %collective-permute-start.2 = (f32[64,2048]{1,0:T(8,128)}, f32[64,2048]{1,0:T(8,128)S(1)}, u32[]{:S(2)}, u32[]{:S(2)}) collective-permute-start(f32[64,2048]{1,0:T(8,128)} %bitcast.28), channel_id=1, source_target_pairs={{0,3},{1,0},{2,1},{3,2},{4,7},{5,4},{6,5},{7,6},{8,11},{9,8},{10,9... | collective-permute-start | bytes 1572872 | tf_op jit(solution)/shard_map/ppermute | solution.py:313
  26.5 117.8 %reduce-scatter.5.cloned.1.call-start = ((), (), s32[]{:S(2)}) async-start(), calls=%async_computation.5 | async-start | bytes 5406720 | tf_op jit(solution)/shard_map/reduce_scatter | solution.py:348
  26.7 30.7 %copy-start.4 = (f32[256,1024]{1,0:T(8,128)}, f32[256,1024]{1,0:T(8,128)S(1)}, u32[]{:S(2)}) copy-start(f32[256,1024]{1,0:T(8,128)S(1)} %pad_maximum_fusion.1.refs_2_) | copy-start | bytes 3145732
  26.7 30.7 %collective-permute-start.3 = (f32[256,1024]{1,0:T(8,128)S(1)}, f32[256,1024]{1,0:T(8,128)S(1)}, u32[]{:S(2)}, u32[]{:S(2)}) collective-permute-start(f32[256,1024]{1,0:T(8,128)S(1)} %pad_maximum_fusion.1.refs_2_), channel_id=1, source_target_pairs={{0,4},{1,5},{2,6},{3,7},{4,8},{5,9},{6,10},{7,11},{8,12},{9,13},{1... | collective-permute-start | bytes 3145736 | tf_op jit(solution)/shard_map/ppermute | solution.py:313
  28.3 29.1 %collective-permute-start.4 = (f32[256,1024]{1,0:T(8,128)S(1)}, f32[256,1024]{1,0:T(8,128)S(1)}, u32[]{:S(2)}, u32[]{:S(2)}) collective-permute-start(f32[256,1024]{1,0:T(8,128)S(1)} %pad_maximum_fusion.1.refs_2_), channel_id=1, source_target_pairs={{0,8},{1,9},{2,10},{3,11},{4,12},{5,13},{6,14},{7,15},{8,0},{9,1},... | collective-permute-start | bytes 3145736 | tf_op jit(solution)/shard_map/ppermute | solution.py:313
  31.2 26.2 %collective-permute-start.5 = (f32[256,1024]{1,0:T(8,128)S(1)}, f32[256,1024]{1,0:T(8,128)}, u32[]{:S(2)}, u32[]{:S(2)}) collective-permute-start(f32[256,1024]{1,0:T(8,128)S(1)} %pad_maximum_fusion.1.refs_2_), channel_id=1, source_target_pairs={{0,12},{1,13},{2,14},{3,15},{4,0},{5,1},{6,2},{7,3},{8,4},{9,5},{1... | collective-permute-start | bytes 3145736 | tf_op jit(solution)/shard_map/ppermute | solution.py:313
  86.5 83.9 %reduce-scatter.3.cloned.1.call-start = ((), (), s32[]{:S(2)}) async-start(), calls=%async_computation.4 | async-start | bytes 5013504 | tf_op jit(solution)/shard_map/reduce_scatter | solution.py:358
  112.3 2.8 %copy-start = (f32[1024,128]{1,0:T(8,128)S(1)}, f32[1024,128]{1,0:T(8,128)}, u32[]{:S(2)}) copy-start(f32[1024,128]{1,0:T(8,128)} %param.5) | copy-start | bytes 1572868
  112.3 3.0 %copy-start.7 = (f32[1,1024]{1,0:T(1,128)S(1)}, f32[1,1024]{1,0:T(1,128)}, u32[]{:S(2)}) copy-start(f32[1,1024]{1,0:T(1,128)} %get-tuple-element.31) | copy-start | bytes 12292
  112.3 28.7 %copy-start.2 = (f32[264,1024]{1,0:T(8,128)S(1)}, f32[264,1024]{1,0:T(8,128)}, u32[]{:S(2)}) copy-start(f32[264,1024]{1,0:T(8,128)} %get-tuple-element.27) | copy-start | bytes 3244036
  112.3 17.0 %collective-permute-start.6 = (f32[264,1024]{1,0:T(8,128)}, f32[264,1024]{1,0:T(8,128)S(1)}, u32[]{:S(2)}, u32[]{:S(2)}) collective-permute-start(f32[264,1024]{1,0:T(8,128)} %get-tuple-element.28), channel_id=1, source_target_pairs={{0,8},{1,9},{2,10},{3,11},{4,12},{5,13},{6,14},{7,15},{8,0},{9,1},... | collective-permute-start | bytes 3244040 | tf_op jit(solution)/shard_map/ppermute | solution.py:313
  113.0 25.9 %collective-permute-start.7 = (f32[264,1024]{1,0:T(8,128)}, f32[264,1024]{1,0:T(8,128)}, u32[]{:S(2)}, u32[]{:S(2)}) collective-permute-start(f32[264,1024]{1,0:T(8,128)} %get-tuple-element.29), channel_id=1, source_target_pairs={{0,12},{1,13},{2,14},{3,15},{4,0},{5,1},{6,2},{7,3},{8,4},{9,5},{1... | collective-permute-start | bytes 3244040 | tf_op jit(solution)/shard_map/ppermute | solution.py:313
  114.2 26.8 %collective-permute-start.8 = (f32[264,1024]{1,0:T(8,128)}, f32[264,1024]{1,0:T(8,128)}, u32[]{:S(2)}, u32[]{:S(2)}) collective-permute-start(f32[264,1024]{1,0:T(8,128)} %get-tuple-element.30), channel_id=1, source_target_pairs={{0,4},{1,5},{2,6},{3,7},{4,8},{5,9},{6,10},{7,11},{8,12},{9,13},{1... | collective-permute-start | bytes 3244040 | tf_op jit(solution)/shard_map/ppermute | solution.py:313
  144.4 1.3 slice-start
  145.7 7.0 %copy-start.6 = (f32[1,1024]{1,0:T(1,128)S(1)}, f32[1,1024]{1,0:T(1,128)}, u32[]{:S(2)}) copy-start(f32[1,1024]{1,0:T(1,128)} %get-tuple-element.32) | copy-start | bytes 12292
  145.7 24.7 %copy-start.5 = (f32[1,1024]{1,0:T(1,128)S(1)}, f32[1,1024]{1,0:T(1,128)}, u32[]{:S(2)}) copy-start(f32[1,1024]{1,0:T(1,128)} %get-tuple-element.25) | copy-start | bytes 12292
  147.1 26.8 %collective-permute-start.10 = (f32[72,2048]{1,0:T(8,128)}, f32[72,2048]{1,0:T(8,128)S(1)}, u32[]{:S(2)}, u32[]{:S(2)}) collective-permute-start(f32[72,2048]{1,0:T(8,128)} %get-tuple-element.56), channel_id=1, source_target_pairs={{0,2},{1,3},{2,0},{3,1},{4,6},{5,7},{6,4},{7,5},{8,10},{9,11},{10,... | collective-permute-start | bytes 1769480 | tf_op jit(solution)/shard_map/ppermute | solution.py:313
  149.5 24.4 %collective-permute-start.11 = (f32[72,2048]{1,0:T(8,128)}, f32[72,2048]{1,0:T(8,128)S(1)}, u32[]{:S(2)}, u32[]{:S(2)}) collective-permute-start(f32[72,2048]{1,0:T(8,128)} %get-tuple-element.57), channel_id=1, source_target_pairs={{0,1},{1,2},{2,3},{3,0},{4,5},{5,6},{6,7},{7,4},{8,9},{9,10},{10,1... | collective-permute-start | bytes 1769480 | tf_op jit(solution)/shard_map/ppermute | solution.py:313
  150.1 23.8 %collective-permute-start.9 = (f32[72,2048]{1,0:T(8,128)S(1)}, f32[72,2048]{1,0:T(8,128)S(1)}, u32[]{:S(2)}, u32[]{:S(2)}) collective-permute-start(f32[72,2048]{1,0:T(8,128)S(1)} %get-tuple-element.55), channel_id=1, source_target_pairs={{0,3},{1,0},{2,1},{3,2},{4,7},{5,4},{6,5},{7,6},{8,11},{9,8},{10,9... | collective-permute-start | bytes 1769480 | tf_op jit(solution)/shard_map/ppermute | solution.py:313
  172.9 2.5 %copy-start.1 = (f32[2048,64]{0,1:T(8,128)S(1)}, f32[2048,64]{0,1:T(8,128)}, u32[]{:S(2)}) copy-start(f32[2048,64]{0,1:T(8,128)} %param.4) | copy-start | bytes 1572868
  (3 other events, 3.7 us)
Sparse Core Ops, SparseCore 0:
  9.7 38.7 all-gather.4
  50.1 32.6 all-gather.2
  86.6 31.6 reduce-scatter.4
  120.6 49.7 reduce-scatter.2
